TPU v7x, 512 devices: a whole 4x8x8 slice. The times are simulated.
512 devices in a mesh: mp: 64 (over z, y), replica: 8 (over x, core).
Axes of the slice: x: 4, y: 8, z: 8, core: 2. Of those that a mesh axis runs over, the one named last changes fastest.
Arguments:
- table: float32 [32768, 256], P('mp'), may hold values from -6 to 6
- accum: float32 [32768], P('mp'), may hold values from 2 to 400
- bag_blocks: int32 [8, 4096, 3], P('replica', 'mp'), may hold values from 0 to 3
- bag_entries: int32 [8, 524288, 4], P('replica', 'mp'), may hold values from 0 to 383, as said below
- bag_weights: float32 [8, 524288, 4], P('replica', 'mp'), may hold values from 0.5 to 1.5
- bag_target: int32 [8, 524288], P('replica', 'mp'), may hold values from 0 to 511
- other_feats: bfloat16 [8, 32768, 256], P('replica', 'mp'), may hold values from -6 to 6
- cross_w: bfloat16 [2, 512, 512], replicated, may hold values from -0.25 to 0.25
- cross_b: float32 [2, 512], replicated, may hold values from -3 to 3
- evict_grads: bfloat16 [8, 2560, 128, 256], P('replica', 'mp'), may hold values from -6 to 6
- evict_owner: int32 [8, 2560, 1], P('replica', 'mp'), may hold values from 0 to 63; in each aligned block of 40 rows (0 to 39, 40 to 79, ..., all dimensions but the last counted through in order) at most 2 rows name the same one
- evict_block: int32 [8, 2560], P('replica', 'mp'), may hold values from 0 to 3
Outputs:
- cross_out: bfloat16 [8, 32768, 512], P('replica', 'mp')
- new_table: float32 [32768, 256], P('mp')
- new_accum: float32 [32768], P('mp')
Inputs may be any that keep to these rules, and one draw needn't show every extreme that they name: `bag_entries`: within one row the 4 entries are distinct: entry l lies in [l * 3 * 32, (l + 1) * 3 * 32). `evict_owner`: the 40 evicted blocks of one device name one owner at most 2 times.
All inputs are finite; a program needn't handle non-finite values.
Results may differ from a plain program's by a relative error of at most 0.011.
Values may be sent and summed in bfloat16 or wider, within the bound.
No kernel may reach another device: no remote copies, remote signals or barrier semaphores. Data moves between devices by JAX's collectives and lax.ppermute only.
A program may use at most 128 MiB of HBM per device.

v0:
```python
import jax
import jax.numpy as jnp
from jax import lax
from jax.sharding import PartitionSpec as P

CAP = 2


learn_rate = 0.3


def adagrad(gradient, old_accum, old_table):
    fresh_accum = old_accum + jnp.mean(gradient * gradient, axis=1)
    fresh_table = old_table - learn_rate * gradient / jnp.sqrt(fresh_accum)[:, None]
    return (fresh_table, fresh_accum)


def local(
    table,
    accum,
    bag_blocks,
    bag_entries,
    bag_weights,
    bag_target,
    other_feats,
    cross_w,
    cross_b,
    evict_grads,
    evict_owner,
    evict_block,
):
    owner_count = lax.axis_size("mp")
    block_rows = evict_grads.shape[2]
    embed_width = evict_grads.shape[3]
    owners = evict_owner[0, :, 0]
    block_ids = evict_block[0]
    evicted = owners.shape[0]
    positions = jnp.arange(evicted)
    earlier = (owners[:, None] == owners[None, :]) & (positions[None, :] < positions[:, None])
    earlier_count = jnp.sum(earlier.astype(jnp.int32), axis=1)
    wanted_slot = owners * CAP + earlier_count
    slot_ids = jnp.arange(owner_count * CAP)
    matches = slot_ids[:, None] == wanted_slot[None, :]
    filled = jnp.any(matches, axis=1)
    source = jnp.argmax(matches.astype(jnp.int32), axis=1)
    picked = jnp.take(evict_grads[0], source, axis=0)
    send_blocks = jnp.where(filled[:, None, None], picked, jnp.zeros_like(picked)).reshape(
        owner_count, CAP, block_rows, embed_width
    )
    send_ids = jnp.where(filled, jnp.take(block_ids, source), -1).reshape(owner_count, CAP)
    slab_rows = table.shape[0]
    block_count = slab_rows // block_rows
    slab_blocks = table.astype(jnp.bfloat16).reshape(block_count, block_rows, embed_width)
    tile_blocks = bag_blocks[0]
    tile_count = tile_blocks.shape[0]
    tile_width = tile_blocks.shape[1] * block_rows
    gathered = jnp.take(slab_blocks, tile_blocks.reshape(-1), axis=0).reshape(
        tile_count, tile_width, embed_width
    )
    entries = bag_entries[0].reshape(tile_count, block_rows, -1)
    weights_bf = bag_weights[0].astype(jnp.bfloat16).reshape(tile_count, block_rows, -1)
    columns = jnp.arange(tile_width)
    incidence = jnp.zeros((tile_count, block_rows, tile_width), jnp.bfloat16)
    for entry_no in range(entries.shape[2]):
        incidence = incidence + jnp.where(
            entries[:, :, entry_no, None] == columns,
            weights_bf[:, :, entry_no, None],
            jnp.zeros((), jnp.bfloat16),
        )
    partial_sums = jnp.einsum(
        "tij,tje->tie", incidence, gathered, preferred_element_type=jnp.float32
    )
    partial_value = partial_sums.astype(jnp.bfloat16)
    send_targets = bag_target[0].reshape(owner_count, -1)
    recv_blocks, recv_ids, recv_rows, recv_targets = (
        lax.all_to_all(send_blocks, "mp", split_axis=0, concat_axis=0, tiled=True),
        lax.all_to_all(send_ids, "mp", split_axis=0, concat_axis=0, tiled=True),
        lax.all_to_all(partial_value, "mp", split_axis=0, concat_axis=0, tiled=True),
        lax.all_to_all(send_targets, "mp", split_axis=0, concat_axis=0, tiled=True),
    )
    flat_rows = recv_rows.reshape(-1, embed_width)
    flat_targets = recv_targets.reshape(-1)
    sample_count = other_feats.shape[1]
    selector = (flat_targets[None, :] == jnp.arange(sample_count)[:, None]).astype(jnp.bfloat16)
    pooled = jnp.dot(selector, flat_rows, preferred_element_type=jnp.float32)
    first_input = jnp.concatenate([pooled, other_feats[0].astype(jnp.float32)], axis=1)
    crossed = first_input
    for layer_index in range(cross_w.shape[0]):
        mixing = (
            jnp.dot(
                crossed.astype(jnp.bfloat16),
                cross_w[layer_index],
                preferred_element_type=jnp.float32,
            )
            + cross_b[layer_index]
        )
        crossed = first_input * mixing + crossed
    cross_out = crossed.astype(jnp.bfloat16)[None]
    flat_ids = recv_ids.reshape(-1)
    onehot = (jnp.arange(block_count)[:, None] == flat_ids[None, :]).astype(jnp.bfloat16)
    local_grad = jnp.dot(
        onehot, recv_blocks.reshape(flat_ids.shape[0], -1), preferred_element_type=jnp.float32
    ).reshape(slab_rows, embed_width)
    table_grad = lax.psum(local_grad.astype(jnp.bfloat16), "replica").astype(jnp.float32)
    new_table, new_accum = adagrad(table_grad, accum, table)
    return (cross_out, new_table, new_accum)


def solution(mesh):
    in_specs = (
        P("mp", None),
        P("mp"),
        P("replica", "mp", None),
        P("replica", "mp", None),
        P("replica", "mp", None),
        P("replica", "mp"),
        P("replica", "mp", None),
        P(),
        P(),
        P("replica", "mp", None, None),
        P("replica", "mp", None),
        P("replica", "mp"),
    )
    out_specs = (P("replica", "mp", None), P("mp", None), P("mp"))
    return jax.shard_map(local, mesh=mesh, in_specs=in_specs, out_specs=out_specs, check_vma=False)
```

profile of v0, /device:TPU:39, one launch (start us, length us, event | category | flops | bytes accessed | tf_op | source)
XLA Modules:
  0.0 652.6 jit_solution(7754442421919832160)
XLA Ops:
  7.2 1.0 convert_reduce_fusion
  8.2 0.7 multiply_add_fusion.2
  8.8 0.6 iota_reduce_fusion
  9.6 1.6 gather_fusion.1
  11.2 0.8 select_n.94
  11.9 15.7 %all-to-all-start.2 = ((s32[64,1,2]{2,1,0:T(1,128)}), s32[64,1,2]{2,1,0:T(1,128)S(1)}, u32[]{:S(2)}, u32[]{:S(2)}) async-start(s32[64,1,2]{2,1,0:T(1,128)} %bitcast.22), calls=%async_computation.2 | async-start | bytes 65536 | tf_op jit(solution)/shard_map/all_to_all | solution.py:77
  27.6 0.1 broadcast_in_dim.121
  27.8 0.2 broadcast_in_dim.123
  27.9 6.4 gather_fusion.2
  34.3 7.4 %select_select_fusion = bf16[64,2,128,256]{3,2,1,0:T(8,128)(2,1)} fusion(bf16[64,2,128,256]{3,2,1,0:T(8,128)(2,1)} %bitcast.77, pred[64,2]{1,0:T(8,128)(4,1)S(1)} %broadcast_in_dim.123, pred[64,2]{1,0:T(8,128)(4,1)S(1)} %broadcast_in_dim.121), kind=kLoop, calls=%fused_computation.15 | loop fusion | flops 8388608 | bytes 16777472 | tf_op jit(solution)/shard_map/jit(_where)/select_n | solution.py:47
  41.7 12.5 %all-to-all-start.3 = ((bf16[64,2,128,256]{3,2,1,0:T(8,128)(2,1)}), bf16[64,2,128,256]{3,2,1,0:T(8,128)(2,1)}, u32[]{:S(2)}, u32[]{:S(2)}) async-start(bf16[64,2,128,256]{3,2,1,0:T(8,128)(2,1)} %select_select_fusion), calls=%async_computation.3 | async-start | bytes 16777216 | tf_op jit(solution)/shard_map/all_to_all | solution.py:76
  54.6 0.5 broadcast.77
  55.1 0.7 reduce.22
  56.0 246.0 %all-to-all-done.3 = bf16[64,2,128,256]{3,2,1,0:T(8,128)(2,1)} async-done(((bf16[64,2,128,256]{3,2,1,0:T(8,128)(2,1)}), bf16[64,2,128,256]{3,2,1,0:T(8,128)(2,1)}, u32[]{:S(2)}, u32[]{:S(2)}) %all-to-all-start.3) | async-done | bytes 8388640 | tf_op jit(solution)/shard_map/all_to_all | solution.py:76
  302.0 33.1 %all-to-all-start = ((s32[64,1,128]{2,1,0:T(1,128)}), s32[64,1,128]{2,1,0:T(1,128)S(1)}, u32[]{:S(2)}, u32[]{:S(2)}) async-start(s32[64,1,128]{2,1,0:T(1,128)} %bitcast), calls=%async_computation | async-start | bytes 65536 | tf_op jit(solution)/shard_map/all_to_all | solution.py:79
  335.1 0.2 all-reduce.2.cloned.1.call-start
  335.3 12.3 %copy.46 = bf16[16,8,128,256]{3,1,2,0:T(8,128)(2,1)} copy(bf16[16,8,128,256]{3,2,1,0:T(8,128)(2,1)} %bitcast.40) | data formatting | bytes 16777216
  347.7 4.6 convolution_convert_fusion
  352.3 0.9 convert_element_type.57
  353.5 98.5 %all-reduce.2.cloned.1.call-done = bf16[512,256]{1,0:T(8,128)(2,1)} async-done(((bf16[512,256]{1,0:T(8,128)(2,1)}), bf16[512,256]{1,0:T(8,128)(2,1)}) %all-reduce.2.cloned.1.call-update) | async-done | bytes 262160 | tf_op jit(solution)/shard_map/psum | solution.py:104
  452.0 1.1 fusion.34
  453.1 0.6 fusion.45
  453.7 1.9 fusion.33
  455.5 8.0 %gather_fusion = bf16[192,128,256]{2,1,0:T(8,128)(2,1)} fusion(bf16[4,128,256]{2,1,0:T(8,128)(2,1)S(1)} %bitcast.74, s32[1024]{0:T(1024)S(1)} %pad_clamp_fusion.1), kind=kCustom, calls=%fused_computation | custom fusion | bytes 25166592 | tf_op jit(solution)/shard_map/jit(_take)/gather | solution.py:57
  463.6 7.6 %bitcast_select_fusion = bf16[64,384,256]{2,1,0:T(8,128)(2,1)S(1)} fusion(pred[64,384]{1,0:T(8,128)(4,1)S(1)} %bitcast.83, bf16[64,384,256]{2,1,0:T(8,128)(2,1)} %bitcast.76), kind=kLoop, calls=%fused_computation.6 | loop fusion | flops 6291456 | bytes 25190400 | tf_op jit(solution)/shard_map/jit(_take)/select_n | solution.py:57
  471.1 17.7 %fusion.23 = bf16[64,128,256]{2,1,0:T(8,128)(2,1)} fusion(bf16[64,384,256]{2,1,0:T(8,128)(2,1)S(1)} %bitcast_select_fusion, s32[64,128]{1,0:T(8,128)S(1)} %get-tuple-element.24, s32[64,128]{1,0:T(8,128)S(1)} %get-tuple-element.25, s32[64,128]{1,0:T(8,128)S(1)} %get-tuple-element.26, s32[64,128]{1,0:T(8,128)S(1)} %get-tuple-element.23, ...), kind=kOutput, calls=%fused_computation.30 | convolution fusion | flops 1663041536 | bytes 16973824 | tf_op jit(solution)/shard_map/tij,tje->tie/dot_general | solution.py:70
  488.8 13.1 %all-to-all-start.1 = ((bf16[64,128,256]{2,1,0:T(8,128)(2,1)}), bf16[64,128,256]{2,1,0:T(8,128)(2,1)}, u32[]{:S(2)}, u32[]{:S(2)}) async-start(bf16[64,128,256]{2,1,0:T(8,128)(2,1)} %fusion.23), calls=%async_computation.1 | async-start | bytes 8388608 | tf_op jit(solution)/shard_map/all_to_all | solution.py:78
  502.2 132.8 %all-to-all-done.1 = bf16[64,128,256]{2,1,0:T(8,128)(2,1)} async-done(((bf16[64,128,256]{2,1,0:T(8,128)(2,1)}), bf16[64,128,256]{2,1,0:T(8,128)(2,1)}, u32[]{:S(2)}, u32[]{:S(2)}) %all-to-all-start.1) | async-done | bytes 4194336 | tf_op jit(solution)/shard_map/all_to_all | solution.py:78
  635.0 5.9 fusion
  640.9 1.5 multiply_add_fusion
  642.4 1.3 fusion.29
  643.7 2.0 copy.39
  (44 shorter events, 1.1 us)
Async XLA Ops:
  7.2 20.8 %copy-start = (bf16[1,40,128,256]{3,2,1,0:T(8,128)(2,1)S(1)}, bf16[1,40,128,256]{3,2,1,0:T(8,128)(2,1)}, u32[]{:S(2)}) copy-start(bf16[1,40,128,256]{3,2,1,0:T(8,128)(2,1)} %param.21) | copy-start | bytes 7864324
  11.9 29.8 %all-to-all-start.2 = ((s32[64,1,2]{2,1,0:T(1,128)}), s32[64,1,2]{2,1,0:T(1,128)S(1)}, u32[]{:S(2)}, u32[]{:S(2)}) async-start(s32[64,1,2]{2,1,0:T(1,128)} %bitcast.22), calls=%async_computation.2 | async-start | bytes 65536 | tf_op jit(solution)/shard_map/all_to_all | solution.py:77
  41.7 12.5 %copy-start.7 = (s32[1,64,3]{1,0,2:T(1,128)S(1)}, s32[1,64,3]{1,0,2:T(1,128)}, u32[]{:S(2)}) copy-start(s32[1,64,3]{1,0,2:T(1,128)} %param.14) | copy-start | bytes 2308
  41.7 12.7 %copy-start.6 = (s32[1,8192,4]{1,2,0:T(4,128)S(1)}, s32[1,8192,4]{1,2,0:T(4,128)}, u32[]{:S(2)}) copy-start(s32[1,8192,4]{1,2,0:T(4,128)} %param.15) | copy-start | bytes 393220
  41.7 12.8 %copy-start.5 = (f32[1,8192,4]{1,2,0:T(4,128)S(1)}, f32[1,8192,4]{1,2,0:T(4,128)}, u32[]{:S(2)}) copy-start(f32[1,8192,4]{1,2,0:T(4,128)} %param.16) | copy-start | bytes 393220
  41.7 260.3 %all-to-all-start.3 = ((bf16[64,2,128,256]{3,2,1,0:T(8,128)(2,1)}), bf16[64,2,128,256]{3,2,1,0:T(8,128)(2,1)}, u32[]{:S(2)}, u32[]{:S(2)}) async-start(bf16[64,2,128,256]{3,2,1,0:T(8,128)(2,1)} %select_select_fusion), calls=%async_computation.3 | async-start | bytes 16777216 | tf_op jit(solution)/shard_map/all_to_all | solution.py:76
  302.0 186.8 %all-to-all-start = ((s32[64,1,128]{2,1,0:T(1,128)}), s32[64,1,128]{2,1,0:T(1,128)S(1)}, u32[]{:S(2)}, u32[]{:S(2)}) async-start(s32[64,1,128]{2,1,0:T(1,128)} %bitcast), calls=%async_computation | async-start | bytes 65536 | tf_op jit(solution)/shard_map/all_to_all | solution.py:79
  335.1 116.9 %all-reduce.2.cloned.1.call-start = ((), (), s32[]{:S(2)}) async-start(), calls=%async_computation.4 | async-start | bytes 524288 | tf_op jit(solution)/shard_map/psum | solution.py:104
  347.7 105.4 %copy-start.9 = (f32[512]{0:T(512)S(1)}, f32[512]{0:T(512)}, u32[]{:S(2)}) copy-start(f32[512]{0:T(512)} %param.13) | copy-start | bytes 6148
  347.7 106.0 %copy-start.3 = (f32[512,256]{1,0:T(8,128)S(1)}, f32[512,256]{1,0:T(8,128)}, u32[]{:S(2)}) copy-start(f32[512,256]{1,0:T(8,128)} %param.12) | copy-start | bytes 1572868
  488.8 13.2 %copy-start.4 = (bf16[1,512,256]{2,1,0:T(8,128)(2,1)S(1)}, bf16[1,512,256]{2,1,0:T(8,128)(2,1)}, u32[]{:S(2)}) copy-start(bf16[1,512,256]{2,1,0:T(8,128)(2,1)} %param.18) | copy-start | bytes 786436
  488.8 13.3 %copy-start.8 = (f32[2,512]{1,0:T(2,128)S(1)}, f32[2,512]{1,0:T(2,128)}, u32[]{:S(2)}) copy-start(f32[2,512]{1,0:T(2,128)} %param.20) | copy-start | bytes 12292
  488.8 146.2 %all-to-all-start.1 = ((bf16[64,128,256]{2,1,0:T(8,128)(2,1)}), bf16[64,128,256]{2,1,0:T(8,128)(2,1)}, u32[]{:S(2)}, u32[]{:S(2)}) async-start(bf16[64,128,256]{2,1,0:T(8,128)(2,1)} %fusion.23), calls=%async_computation.1 | async-start | bytes 8388608 | tf_op jit(solution)/shard_map/all_to_all | solution.py:78
  635.0 10.8 %copy-start.1 = (bf16[1,40,128,256]{3,2,1,0:T(8,128)(2,1)S(1)}, bf16[1,40,128,256]{3,2,1,0:T(8,128)(2,1)}, u32[]{:S(2)}) copy-start(bf16[1,40,128,256]{3,2,1,0:T(8,128)(2,1)} %param.21) | copy-start | bytes 7864324
  635.0 7.4 %copy-start.2 = (bf16[2,512,512]{2,1,0:T(8,128)(2,1)S(1)}, bf16[2,512,512]{2,1,0:T(8,128)(2,1)}, u32[]{:S(2)}) copy-start(bf16[2,512,512]{2,1,0:T(8,128)(2,1)} %param.19) | copy-start | bytes 3145732
Sparse Core Ops, SparseCore 0:
  353.3 98.5 all-reduce.1
where the time goes:
time: 653 us
  waiting for transfers between devices  477 us (73%)
  starting transfers between devices  74.6 us (11%)
  local copies, waits for them, and re-layouts  33.7 us (5%)
  matrix products  31 us (5%)
  other arithmetic  21.7 us (3%)
  between operations  14.3 us (2%)
    all_to_all x1, waiting for transfers between devices, local(): lax.all_to_all(send_blocks, 'mp', split_axis=0, concat_axis=0, tiled=True)  246 us
    all_to_all x1, waiting for transfers between devices, local(): lax.all_to_all(partial_value, 'mp', split_axis=0, concat_axis=0, tiled=True)  133 us
    psum x1, waiting for transfers between devices, local(): lax.psum(local_grad.astype(jnp.bfloat16), 'replica').astype(jnp.float32)  98.5 us
    all_to_all x1, starting transfers between devices, local(): lax.all_to_all(send_targets, 'mp', split_axis=0, concat_axis=0, tiled=True)  33.1 us
    dot_general x1, matrix products, local(): jnp.einsum('tij,tje->tie', incidence, gathered, preferred_element_type=jn...  17.7 us
    all_to_all x1, starting transfers between devices, local(): lax.all_to_all(send_ids, 'mp', split_axis=0, concat_axis=0, tiled=True)  15.7 us
    unnamed x27, local copies, waits for them, and re-layouts  14.7 us
    all_to_all x1, starting transfers between devices, local(): lax.all_to_all(partial_value, 'mp', split_axis=0, concat_axis=0, tiled=True)  13.1 us
  transfers between devices with their start and end apart: 5, of which 3 were waited for; matrix products, arithmetic and copies ran while one was open for 11% of the time, Pallas kernels for 0%

commit v1 on v0

v1 whole, which is shorter than its diff:
```python
import jax
import jax.numpy as jnp
from jax import lax
from jax.experimental import pallas as pl
from jax.experimental.pallas import tpu as pltpu
from jax.sharding import PartitionSpec as P

VMEM_LIMIT = 48 * 1024 * 1024
learn_rate = 0.3
BAG_ROWS = 16
STEP = 4


def adagrad(gradient, old_accum, old_table):
    fresh_accum = old_accum + jnp.mean(gradient * gradient, axis=1)
    fresh_table = old_table - learn_rate * gradient / jnp.sqrt(fresh_accum)[:, None]
    return (fresh_table, fresh_accum)


def pack_blocks(grads, slots, parts):
    count, rows, width = grads.shape
    part = rows // parts

    def kernel(grads_ref, slots_ref, out_ref, sems):
        copies = []
        for j in range(parts):
            copies.append(
                pltpu.make_async_copy(
                    grads_ref.at[:, pl.ds(j * part, part), :],
                    out_ref.at[j, pl.ds(0, count)],
                    sems.at[2 * j],
                )
            )
            copies.append(
                pltpu.make_async_copy(slots_ref, out_ref.at[j, pl.ds(count, 1)], sems.at[2 * j + 1])
            )
        for copy in copies:
            copy.start()
        for copy in copies:
            copy.wait()

    return pl.pallas_call(
        kernel,
        out_shape=jax.ShapeDtypeStruct((parts, count + 1, part, width), grads.dtype),
        in_specs=[pl.BlockSpec(memory_space=pl.ANY)] * 2,
        out_specs=pl.BlockSpec(memory_space=pl.ANY),
        scratch_shapes=[pltpu.SemaphoreType.DMA((2 * parts,))],
        cost_estimate=pl.CostEstimate(flops=0, bytes_accessed=2 * grads.size * 2, transcendentals=0),
        name="pack_blocks",
    )(grads, slots)


def owners_payload(recv, slots, entries, weights, targets, blocks, owner_count, block_count):
    parts, extra, part, width = recv.shape
    count = extra - 1
    rows = block_count * part
    span = 96
    lanes = 128

    def kernel(slots_ref, recv_ref, entries_ref, weights_ref, targets_ref, blocks_ref, out_ref, acc_ref):
        acc_ref[...] = jnp.zeros_like(acc_ref)

        def add(n, carry):
            for j in range(parts):
                slot = slots_ref[j * count + n]
                acc_ref[slot] = acc_ref[slot] + recv_ref[j, n].astype(jnp.float32)
            return carry

        lax.fori_loop(0, count, add, 0)
        shift = lax.broadcasted_iota(jnp.int32, (entries_ref.shape[0], lanes), 0) * span

        def place(o, carry):
            for b in range(block_count):
                out_ref[o, pl.ds(b * part, part), :] = acc_ref[o * block_count + b].astype(out_ref.dtype)
            columns = pl.ds(pl.multiple_of(o * lanes, lanes), lanes)
            bag = jnp.concatenate(
                [
                    (entries_ref[:, columns] - shift).astype(jnp.float32),
                    weights_ref[:, columns],
                    (targets_ref[:, columns] - 256).astype(jnp.float32),
                    blocks_ref[o],
                    jnp.zeros((BAG_ROWS - 10, lanes), jnp.float32),
                ],
                axis=0,
            )
            out_ref[o, pl.ds(rows, BAG_ROWS), pl.ds(0, lanes)] = bag.astype(out_ref.dtype)
            out_ref[o, pl.ds(rows, BAG_ROWS), pl.ds(lanes, width - lanes)] = jnp.zeros(
                (BAG_ROWS, width - lanes), out_ref.dtype
            )
            return carry

        lax.fori_loop(0, owner_count, place, 0)

    whole = pl.BlockSpec(memory_space=pltpu.VMEM)
    return pl.pallas_call(
        kernel,
        out_shape=jax.ShapeDtypeStruct((owner_count, rows + BAG_ROWS, width), jnp.bfloat16),
        in_specs=[pl.BlockSpec(memory_space=pltpu.SMEM)] + [whole] * 5,
        out_specs=whole,
        scratch_shapes=[pltpu.VMEM((owner_count * block_count, part, width), jnp.float32)],
        compiler_params=pltpu.CompilerParams(vmem_limit_bytes=VMEM_LIMIT),
        cost_estimate=pl.CostEstimate(flops=0, bytes_accessed=10 * 1024 * 1024, transcendentals=0),
        name="owners_payload",
    )(slots, recv, entries, weights, targets, blocks)


def pool_and_cross(tile_blocks, core, own, other, received, other_feats, cross_w, cross_b, rows):
    owner_count, block_count, half, block_rows = own.shape
    samples, other_width = other_feats.shape
    width = cross_w.shape[1]
    layers = cross_w.shape[0]
    per_tile = tile_blocks.shape[0] // owner_count
    entry_count = 4
    span = per_tile * block_rows // entry_count
    lanes = block_rows

    def kernel(blocks_ref, core_ref, own_ref, other_ref, bag_ref, feats_ref, w_ref, b_ref, out_ref, acc_ref, x_ref, y_ref):
        step = pl.program_id(0)

        @pl.when(step == 0)
        def _():
            acc_ref[...] = jnp.zeros_like(acc_ref)

        position = lax.broadcasted_iota(jnp.int32, (span, lanes), 0)
        sample = lax.broadcasted_iota(jnp.int32, (samples, STEP * lanes), 0)
        partials, targets = [], []
        for t in range(STEP):
            bag = bag_ref[t].astype(jnp.float32)
            entries = bag[0:entry_count].astype(jnp.int32)
            weights = bag[entry_count : 2 * entry_count]
            targets.append(bag[2 * entry_count : 2 * entry_count + 1].astype(jnp.int32) + 256)
            incidence = jnp.concatenate(
                [
                    jnp.where(position == entries[l : l + 1], weights[l : l + 1], 0.0)
                    for l in range(entry_count)
                ],
                axis=0,
            ).astype(jnp.bfloat16)
            chosen = [blocks_ref[(step * STEP + t) * per_tile + j] for j in range(per_tile)]
            slab = jnp.concatenate(
                [
                    jnp.concatenate([own_ref[t, b] for b in chosen], axis=1),
                    jnp.concatenate([other_ref[t, b] for b in chosen], axis=1),
                ],
                axis=0,
            )
            partials.append(
                jnp.dot(slab, incidence, preferred_element_type=jnp.float32).astype(jnp.bfloat16)
            )
        selector = jnp.where(sample == jnp.concatenate(targets, axis=1), 1.0, 0.0).astype(jnp.bfloat16)
        acc_ref[...] += lax.dot_general(
            selector,
            jnp.concatenate(partials, axis=1),
            (((1,), (1,)), ((), ())),
            preferred_element_type=jnp.float32,
        )

        @pl.when(step == pl.num_programs(0) - 1)
        def _():
            low = core_ref[0] == 0
            x_ref[:, 0:half] = jnp.where(low, acc_ref[:, 0:half], acc_ref[:, half : 2 * half])
            x_ref[:, half : 2 * half] = jnp.where(low, acc_ref[:, half : 2 * half], acc_ref[:, 0:half])
            x_ref[:, 2 * half :] = feats_ref[...].astype(jnp.float32)
            y_ref[...] = x_ref[...]
            for layer in range(layers):
                mixing = (
                    jnp.dot(y_ref[...].astype(jnp.bfloat16), w_ref[layer], preferred_element_type=jnp.float32)
                    + b_ref[layer : layer + 1, :]
                )
                if layer < layers - 1:
                    y_ref[...] = x_ref[...] * mixing + y_ref[...]
                else:
                    out_ref[...] = (x_ref[...] * mixing + y_ref[...]).astype(out_ref.dtype)

    bag_block = rows // BAG_ROWS
    return pl.pallas_call(
        kernel,
        out_shape=jax.ShapeDtypeStruct((samples, width), jnp.bfloat16),
        grid_spec=pltpu.PrefetchScalarGridSpec(
            num_scalar_prefetch=2,
            grid=(owner_count // STEP,),
            in_specs=[
                pl.BlockSpec((STEP, block_count, half, block_rows), lambda i, *_: (i, 0, 0, 0)),
                pl.BlockSpec((STEP, block_count, half, block_rows), lambda i, *_: (i, 0, 0, 0)),
                pl.BlockSpec((STEP, BAG_ROWS, lanes), lambda i, *_: (i, bag_block, 0)),
                pl.BlockSpec((samples, other_width), lambda i, *_: (0, 0)),
                pl.BlockSpec((layers, width, width), lambda i, *_: (0, 0, 0)),
                pl.BlockSpec((layers, width), lambda i, *_: (0, 0)),
            ],
            out_specs=pl.BlockSpec((samples, width), lambda i, *_: (0, 0)),
            scratch_shapes=[
                pltpu.VMEM((samples, 2 * half), jnp.float32),
                pltpu.VMEM((samples, width), jnp.float32),
                pltpu.VMEM((samples, width), jnp.float32),
            ],
        ),
        compiler_params=pltpu.CompilerParams(
            dimension_semantics=("arbitrary",), vmem_limit_bytes=VMEM_LIMIT
        ),
        cost_estimate=pl.CostEstimate(
            flops=8_000_000_000, bytes_accessed=20 * 1024 * 1024, transcendentals=0
        ),
        name="pool_and_cross",
    )(tile_blocks, core, own, other, received, other_feats, cross_w, cross_b)


def local(
    table,
    accum,
    bag_blocks,
    bag_entries,
    bag_weights,
    bag_target,
    other_feats,
    cross_w,
    cross_b,
    evict_grads,
    evict_owner,
    evict_block,
):
    owner_count = lax.axis_size("mp")
    parts = lax.axis_size("replica")
    count, block_rows, width = evict_grads.shape[1:]
    slab_rows = table.shape[0]
    block_count = slab_rows // block_rows
    part = block_rows // parts
    half = width // 2
    core = lax.axis_index("replica") % 2

    with jax.named_scope("table_gather"):
        own_half = lax.dynamic_slice(table, (0, core * half), (slab_rows, half)).astype(jnp.bfloat16)
        own_half = own_half.reshape(block_count, block_rows, half).transpose(0, 2, 1)
        own = lax.all_gather(own_half, "mp", axis=0)
        other = lax.ppermute(own, "replica", [(i, i ^ 1) for i in range(parts)])

    with jax.named_scope("evicted_over_replica"):
        slots = (evict_owner[0, :, 0] * block_count + evict_block[0]).astype(jnp.bfloat16)
        slots_block = jnp.pad(slots[None, None, :], ((0, 0), (0, part - 1), (0, width - count)))
        sent = pack_blocks(evict_grads[0], slots_block, parts)
        arrived = lax.all_to_all(sent, "replica", split_axis=0, concat_axis=0, tiled=True)
        arrived_slots = arrived[:, count, 0, :count].astype(jnp.int32).reshape(-1)

    with jax.named_scope("parts_over_mp"):
        blocks_row = jnp.pad(
            bag_blocks[0].astype(jnp.float32), ((0, 0), (0, 128 - bag_blocks.shape[2]))
        )[:, None, :]
        payload = owners_payload(
            arrived,
            arrived_slots,
            bag_entries[0].T,
            bag_weights[0].T,
            bag_target,
            blocks_row,
            owner_count,
            block_count,
        )
        received = lax.all_to_all(payload, "mp", split_axis=0, concat_axis=0, tiled=True)

    rows = block_count * part
    with jax.named_scope("table_update"):
        grad_part = jnp.sum(received[:, :rows, :].astype(jnp.float32), axis=0).astype(jnp.bfloat16)
        grads = lax.all_gather(grad_part, "replica", axis=0)
        table_grad = (
            grads.reshape(parts, block_count, part, width)
            .transpose(1, 0, 2, 3)
            .reshape(slab_rows, width)
            .astype(jnp.float32)
        )
        new_table, new_accum = adagrad(table_grad, accum, table)

    with jax.named_scope("pooling"):
        tile_blocks = received[:, rows + 9, : bag_blocks.shape[2]].astype(jnp.int32).reshape(-1)
        cross_out = pool_and_cross(
            tile_blocks,
            core.reshape(1),
            own,
            other,
            received,
            other_feats[0],
            cross_w,
            cross_b,
            rows,
        )
    return (cross_out[None], new_table, new_accum)


def solution(mesh):
    in_specs = (
        P("mp", None),
        P("mp"),
        P("replica", "mp", None),
        P("replica", "mp", None),
        P("replica", "mp", None),
        P("replica", "mp"),
        P("replica", "mp", None),
        P(),
        P(),
        P("replica", "mp", None, None),
        P("replica", "mp", None),
        P("replica", "mp"),
    )
    out_specs = (P("replica", "mp", None), P("mp", None), P("mp"))
    return jax.shard_map(local, mesh=mesh, in_specs=in_specs, out_specs=out_specs, check_vma=False)
```

time: 653 us -> 259 us (0.40)
  the two profiles are of different devices: /device:TPU:39 before, /device:TPU:1 now
where the time goes in v1:
time: 259 us; the launch traced here: 258 us
  Pallas kernels  103 us (40%)
  blocking collectives  89.8 us (35%)
  waiting for transfers between devices  30 us (12%)
  between operations  14.2 us (5%)
  starting transfers between devices  13.2 us (5%)
  local copies, waits for them, and re-layouts  4.14 us (2%)
  other arithmetic  3.85 us (1%)
    pallas_call x1, Pallas kernels, pack_blocks(): pl.pallas_call(kernel, out_shape=jax.ShapeDtypeStruct((parts, count + 1,...  82.6 us
    all_to_all x1, blocking collectives, local(): lax.all_to_all(payload, 'mp', split_axis=0, concat_axis=0, tiled=True)  73.7 us
    pallas_call x1, Pallas kernels, pool_and_cross(): pl.pallas_call(kernel, out_shape=jax.ShapeDtypeStruct((samples, width), j...  18.1 us
    all_to_all x1, waiting for transfers between devices, local(): lax.all_to_all(sent, 'replica', split_axis=0, concat_axis=0, tiled=True)  17 us
    all_gather x1, blocking collectives, local(): grads = lax.all_gather(grad_part, 'replica', axis=0)  16 us
    all_gather x1, waiting for transfers between devices, local(): own = lax.all_gather(own_half, 'mp', axis=0)  13 us
    all_to_all x1, starting transfers between devices, local(): lax.all_to_all(sent, 'replica', split_axis=0, concat_axis=0, tiled=True)  10.6 us
  transfers between devices with their start and end apart: 3, of which 2 were waited for; matrix products, arithmetic and copies ran while one was open for 2% of the time, Pallas kernels for 33%

profile of v1, /device:TPU:1, one launch (start us, length us, event | category | flops | bytes accessed | tf_op | source)
XLA Modules:
  0.0 258.5 jit_solution(8380045055027317676)
XLA Ops:
  7.2 0.0 all-gather.4.cloned.1.call-start
  7.2 1.0 dynamic-slice_convert_fusion
  8.2 0.8 copy.27
  9.0 0.0 all-gather.4.cloned.1.call-update
  9.0 0.7 fusion.4
  9.7 0.6 pad.8.slots_ref
  10.3 82.6 %pack_blocks.1 = bf16[8,41,16,256]{3,2,1,0:T(8,128)(2,1)} custom-call(bf16[40,128,256]{2,1,0:T(8,128)(2,1)} %bitcast.35, bf16[1,16,256]{2,1,0:T(8,128)(2,1)} %pad.8.slots_ref), custom_call_target="tpu_custom_call" | custom-call | bytes 5242880 | tf_op jit(solution)/shard_map/evicted_over_replica/pack_blocks/pallas_call | solution.py:42
  92.9 0.0 copy-start.7
  92.9 0.0 copy-start
  93.0 0.0 copy-start.1
  93.0 0.0 copy-start.2
  93.0 10.6 %all-to-all-start = ((bf16[8,41,16,256]{3,2,1,0:T(8,128)(2,1)}), bf16[8,41,16,256]{3,2,1,0:T(8,128)(2,1)S(1)}, u32[]{:S(2)}, u32[]{:S(2)}) async-start(bf16[8,41,16,256]{3,2,1,0:T(8,128)(2,1)} %pack_blocks.1), calls=%async_computation | async-start | bytes 5373952 | tf_op jit(solution)/shard_map/evicted_over_replica/all_to_all | solution.py:240
  103.5 13.0 %all-gather.4.cloned.1.call-done = bf16[256,128,128]{2,1,0:T(8,128)(2,1)} async-done(((bf16[4,128,128]{2,1,0:T(8,128)(2,1)}), bf16[256,128,128]{2,1,0:T(8,128)(2,1)}) %all-gather.4.cloned.1.call-update) | async-done | bytes 8388624 | tf_op jit(solution)/shard_map/table_gather/all_gather | solution.py:233
  116.5 2.6 %collective-permute-start = (bf16[64,4,128,128]{3,2,1,0:T(8,128)(2,1)}, bf16[64,4,128,128]{3,2,1,0:T(8,128)(2,1)}, u32[]{:S(2)}, u32[]{:S(2)}) collective-permute-start(bf16[64,4,128,128]{3,2,1,0:T(8,128)(2,1)} %bitcast.39), channel_id=1, source_target_pairs={{0,1},{1,0},{2,3},{3,2},{4,5},{5,4},{6,7},{7,6},{8,9},{9,8},{10,11... | collective-permute-start | bytes 25165832 | tf_op jit(solution)/shard_map/table_gather/ppermute | solution.py:234
  119.1 0.1 copy.26
  119.2 17.0 %all-to-all-done.recv_ref = bf16[8,41,16,256]{3,2,1,0:T(8,128)(2,1)S(1)} async-done(((bf16[8,41,16,256]{3,2,1,0:T(8,128)(2,1)}), bf16[8,41,16,256]{3,2,1,0:T(8,128)(2,1)S(1)}, u32[]{:S(2)}, u32[]{:S(2)}) %all-to-all-start) | async-done | bytes 2687008 | tf_op jit(solution)/shard_map/evicted_over_replica/all_to_all | solution.py:240
  136.2 0.1 reshape.63.slots_ref
  136.3 2.6 %owners_payload.1 = bf16[64,80,256]{2,1,0:T(8,128)(2,1)S(1)} custom-call(s32[320]{0:T(512)S(1)} %reshape.63.slots_ref, bf16[8,41,16,256]{3,2,1,0:T(8,128)(2,1)S(1)} %all-to-all-done.recv_ref, s32[4,8192]{1,0:T(4,128)S(1)} %bitcast.32, f32[4,8192]{1,0:T(4,128)S(1)} %bitcast.33, s32[1,8192]{1,0:T(1,128)S(1)} %copy-done.2, f32[64,1,128]{2,1,0:T(1,128)S(1)} %bitcast.31), custom_call_target="tpu_custom_call" | custom-call | bytes 10485760 | tf_op jit(solution)/shard_map/parts_over_mp/owners_payload/pallas_call | solution.py:95
  139.0 73.7 %all_to_all.10.bag_ref = bf16[64,80,256]{2,1,0:T(8,128)(2,1)S(1)} all-to-all(bf16[64,80,256]{2,1,0:T(8,128)(2,1)S(1)} %owners_payload.1), channel_id=1, replica_groups=mesh['mp'=64,'replica'=8] {'mp'}, dimensions={0} | all-to-all | bytes 5242880 | tf_op jit(solution)/shard_map/parts_over_mp/all_to_all | solution.py:257
  212.7 0.1 fusion.2
  212.9 0.1 reshape.64.blocks_ref
  213.0 0.0 copy-start.4
  213.0 0.0 copy-start.5
  213.0 0.3 slice_reduce_fusion
  213.3 16.0 %all-gather.1 = bf16[512,256]{1,0:T(8,128)(2,1)S(1)} all-gather(bf16[64,256]{1,0:T(8,128)(2,1)S(1)} %slice_reduce_fusion), channel_id=3, replica_groups=mesh['mp'=64,'replica'=8] {'replica'}, dimensions={0}, use_global_device_ids=true | all-gather | bytes 294912 | tf_op jit(solution)/shard_map/table_update/all_gather | solution.py:262
  229.4 0.1 fusion
  229.6 0.1 reshape.66
  229.7 0.1 div.21
  229.7 0.6 fusion.5
  230.3 2.0 fusion.1
  232.3 1.2 copy-done.3
  233.5 18.1 %pool_and_cross.1 = bf16[512,512]{1,0:T(8,128)(2,1)} custom-call(s32[192]{0:T(256)S(1)} %reshape.64.blocks_ref, s32[1]{0:T(128)} %bitcast.9.core_ref, bf16[64,4,128,128]{3,2,1,0:T(8,128)(2,1)} %bitcast.40, bf16[64,4,128,128]{3,2,1,0:T(8,128)(2,1)} %collective-permute-done.other_ref, bf16[64,80,256]{2,1,0:T(8,128)(2,1)S(1)} %all_to_all.10.bag_ref, ...), custom_call_target="tpu_custom_call" | custom-call | flops 8000000000 | bytes 20971520 | tf_op jit(solution)/shard_map/pooling/pool_and_cross/pallas_call | solution.py:176
  (16 shorter events, 0.1 us)
Async XLA Ops:
  7.2 109.3 %all-gather.4.cloned.1.call-start = ((), (), s32[]{:S(2)}) async-start(), calls=%async_computation.2 | async-start | bytes 8519680 | tf_op jit(solution)/shard_map/table_gather/all_gather | solution.py:233
  92.9 26.2 %copy-start.7 = (s32[1,64,3]{1,0,2:T(1,128)S(1)}, s32[1,64,3]{1,0,2:T(1,128)}, u32[]{:S(2)}) copy-start(s32[1,64,3]{1,0,2:T(1,128)} %param.14) | copy-start | bytes 2308
  92.9 43.4 %copy-start = (s32[1,8192,4]{1,2,0:T(4,128)S(1)}, s32[1,8192,4]{1,2,0:T(4,128)}, u32[]{:S(2)}) copy-start(s32[1,8192,4]{1,2,0:T(4,128)} %param.15) | copy-start | bytes 393220
  93.0 43.4 %copy-start.1 = (f32[1,8192,4]{1,2,0:T(4,128)S(1)}, f32[1,8192,4]{1,2,0:T(4,128)}, u32[]{:S(2)}) copy-start(f32[1,8192,4]{1,2,0:T(4,128)} %param.16) | copy-start | bytes 393220
  93.0 43.4 %copy-start.2 = (s32[1,8192]{1,0:T(1,128)S(1)}, s32[1,8192]{1,0:T(1,128)}, u32[]{:S(2)}) copy-start(s32[1,8192]{1,0:T(1,128)} %targets_ref.1) | copy-start | bytes 98308
  93.0 43.2 %all-to-all-start = ((bf16[8,41,16,256]{3,2,1,0:T(8,128)(2,1)}), bf16[8,41,16,256]{3,2,1,0:T(8,128)(2,1)S(1)}, u32[]{:S(2)}, u32[]{:S(2)}) async-start(bf16[8,41,16,256]{3,2,1,0:T(8,128)(2,1)} %pack_blocks.1), calls=%async_computation | async-start | bytes 5373952 | tf_op jit(solution)/shard_map/evicted_over_replica/all_to_all | solution.py:240
  116.5 115.8 %collective-permute-start = (bf16[64,4,128,128]{3,2,1,0:T(8,128)(2,1)}, bf16[64,4,128,128]{3,2,1,0:T(8,128)(2,1)}, u32[]{:S(2)}, u32[]{:S(2)}) collective-permute-start(bf16[64,4,128,128]{3,2,1,0:T(8,128)(2,1)} %bitcast.39), channel_id=1, source_target_pairs={{0,1},{1,0},{2,3},{3,2},{4,5},{5,4},{6,7},{7,6},{8,9},{9,8},{10,11... | collective-permute-start | bytes 25165832 | tf_op jit(solution)/shard_map/table_gather/ppermute | solution.py:234
  212.7 17.0 %copy-start.6 = (f32[512]{0:T(512)S(1)}, f32[512]{0:T(512)}, u32[]{:S(2)}) copy-start(f32[512]{0:T(512)} %param.13) | copy-start | bytes 6148
  213.0 19.3 %copy-start.4 = (bf16[1,512,256]{2,1,0:T(8,128)(2,1)S(1)}, bf16[1,512,256]{2,1,0:T(8,128)(2,1)}, u32[]{:S(2)}) copy-start(bf16[1,512,256]{2,1,0:T(8,128)(2,1)} %param.18) | copy-start | bytes 786436
  213.0 19.3 %copy-start.5 = (f32[2,512]{1,0:T(2,128)S(1)}, f32[2,512]{1,0:T(2,128)}, u32[]{:S(2)}) copy-start(f32[2,512]{1,0:T(2,128)} %b_ref.1) | copy-start | bytes 12292
  232.3 1.2 copy-start.3
Sparse Core Ops, SparseCore 0:
  11.6 104.8 all-gather.3

commit v2 on v1

--- a/solution.py
+++ b/solution.py
@@ -21,57 +21,36 @@
     count, rows, width = grads.shape
     part = rows // parts
 
-    def kernel(grads_ref, slots_ref, out_ref, sems):
-        copies = []
+    def kernel(grads_ref, slots_ref, out_ref):
+        def place(n, carry):
+            for j in range(parts):
+                out_ref[j, n] = grads_ref[n, pl.ds(j * part, part), :]
+            return carry
+
+        lax.fori_loop(0, count, place, 0)
         for j in range(parts):
-            copies.append(
-                pltpu.make_async_copy(
-                    grads_ref.at[:, pl.ds(j * part, part), :],
-                    out_ref.at[j, pl.ds(0, count)],
-                    sems.at[2 * j],
-                )
-            )
-            copies.append(
-                pltpu.make_async_copy(slots_ref, out_ref.at[j, pl.ds(count, 1)], sems.at[2 * j + 1])
-            )
-        for copy in copies:
-            copy.start()
-        for copy in copies:
-            copy.wait()
-
+            out_ref[j, count] = slots_ref[...]
+
+    whole = pl.BlockSpec(memory_space=pltpu.VMEM)
     return pl.pallas_call(
         kernel,
         out_shape=jax.ShapeDtypeStruct((parts, count + 1, part, width), grads.dtype),
-        in_specs=[pl.BlockSpec(memory_space=pl.ANY)] * 2,
-        out_specs=pl.BlockSpec(memory_space=pl.ANY),
-        scratch_shapes=[pltpu.SemaphoreType.DMA((2 * parts,))],
+        in_specs=[whole] * 2,
+        out_specs=whole,
+        compiler_params=pltpu.CompilerParams(vmem_limit_bytes=VMEM_LIMIT),
         cost_estimate=pl.CostEstimate(flops=0, bytes_accessed=2 * grads.size * 2, transcendentals=0),
         name="pack_blocks",
     )(grads, slots)
 
 
-def owners_payload(recv, slots, entries, weights, targets, blocks, owner_count, block_count):
-    parts, extra, part, width = recv.shape
-    count = extra - 1
-    rows = block_count * part
+def pack_bags(entries, weights, targets, blocks):
+    owner_count, _, lanes = blocks.shape
     span = 96
-    lanes = 128
-
-    def kernel(slots_ref, recv_ref, entries_ref, weights_ref, targets_ref, blocks_ref, out_ref, acc_ref):
-        acc_ref[...] = jnp.zeros_like(acc_ref)
-
-        def add(n, carry):
-            for j in range(parts):
-                slot = slots_ref[j * count + n]
-                acc_ref[slot] = acc_ref[slot] + recv_ref[j, n].astype(jnp.float32)
-            return carry
-
-        lax.fori_loop(0, count, add, 0)
+
+    def kernel(entries_ref, weights_ref, targets_ref, blocks_ref, out_ref):
         shift = lax.broadcasted_iota(jnp.int32, (entries_ref.shape[0], lanes), 0) * span
 
         def place(o, carry):
-            for b in range(block_count):
-                out_ref[o, pl.ds(b * part, part), :] = acc_ref[o * block_count + b].astype(out_ref.dtype)
             columns = pl.ds(pl.multiple_of(o * lanes, lanes), lanes)
             bag = jnp.concatenate(
                 [
@@ -83,10 +62,7 @@
                 ],
                 axis=0,
             )
-            out_ref[o, pl.ds(rows, BAG_ROWS), pl.ds(0, lanes)] = bag.astype(out_ref.dtype)
-            out_ref[o, pl.ds(rows, BAG_ROWS), pl.ds(lanes, width - lanes)] = jnp.zeros(
-                (BAG_ROWS, width - lanes), out_ref.dtype
-            )
+            out_ref[o] = bag.astype(out_ref.dtype)
             return carry
 
         lax.fori_loop(0, owner_count, place, 0)
@@ -94,17 +70,51 @@
     whole = pl.BlockSpec(memory_space=pltpu.VMEM)
     return pl.pallas_call(
         kernel,
-        out_shape=jax.ShapeDtypeStruct((owner_count, rows + BAG_ROWS, width), jnp.bfloat16),
-        in_specs=[pl.BlockSpec(memory_space=pltpu.SMEM)] + [whole] * 5,
+        out_shape=jax.ShapeDtypeStruct((owner_count, BAG_ROWS, lanes), jnp.bfloat16),
+        in_specs=[whole] * 4,
+        out_specs=whole,
+        compiler_params=pltpu.CompilerParams(vmem_limit_bytes=VMEM_LIMIT),
+        cost_estimate=pl.CostEstimate(flops=0, bytes_accessed=1024 * 1024, transcendentals=0),
+        name="pack_bags",
+    )(entries, weights, targets, blocks)
+
+
+def add_blocks(recv, slots, owner_count, block_count):
+    parts, extra, part, width = recv.shape
+    count = extra - 1
+
+    def kernel(slots_ref, recv_ref, out_ref, acc_ref):
+        acc_ref[...] = jnp.zeros_like(acc_ref)
+
+        def add(n, carry):
+            for j in range(parts):
+                slot = slots_ref[j * count + n]
+                acc_ref[slot] = acc_ref[slot] + recv_ref[j, n].astype(jnp.float32)
+            return carry
+
+        lax.fori_loop(0, count, add, 0)
+
+        def place(o, carry):
+            for b in range(block_count):
+                out_ref[o, pl.ds(b * part, part), :] = acc_ref[o * block_count + b].astype(out_ref.dtype)
+            return carry
+
+        lax.fori_loop(0, owner_count, place, 0)
+
+    whole = pl.BlockSpec(memory_space=pltpu.VMEM)
+    return pl.pallas_call(
+        kernel,
+        out_shape=jax.ShapeDtypeStruct((owner_count, block_count * part, width), jnp.bfloat16),
+        in_specs=[pl.BlockSpec(memory_space=pltpu.SMEM), whole],
         out_specs=whole,
         scratch_shapes=[pltpu.VMEM((owner_count * block_count, part, width), jnp.float32)],
         compiler_params=pltpu.CompilerParams(vmem_limit_bytes=VMEM_LIMIT),
         cost_estimate=pl.CostEstimate(flops=0, bytes_accessed=10 * 1024 * 1024, transcendentals=0),
-        name="owners_payload",
-    )(slots, recv, entries, weights, targets, blocks)
-
-
-def pool_and_cross(tile_blocks, core, own, other, received, other_feats, cross_w, cross_b, rows):
+        name="add_blocks",
+    )(slots, recv)
+
+
+def pool_and_cross(tile_blocks, core, own, other, bags, other_feats, cross_w, cross_b):
     owner_count, block_count, half, block_rows = own.shape
     samples, other_width = other_feats.shape
     width = cross_w.shape[1]
@@ -172,7 +182,6 @@
                 else:
                     out_ref[...] = (x_ref[...] * mixing + y_ref[...]).astype(out_ref.dtype)
 
-    bag_block = rows // BAG_ROWS
     return pl.pallas_call(
         kernel,
         out_shape=jax.ShapeDtypeStruct((samples, width), jnp.bfloat16),
@@ -182,7 +191,7 @@
             in_specs=[
                 pl.BlockSpec((STEP, block_count, half, block_rows), lambda i, *_: (i, 0, 0, 0)),
                 pl.BlockSpec((STEP, block_count, half, block_rows), lambda i, *_: (i, 0, 0, 0)),
-                pl.BlockSpec((STEP, BAG_ROWS, lanes), lambda i, *_: (i, bag_block, 0)),
+                pl.BlockSpec((STEP, BAG_ROWS, lanes), lambda i, *_: (i, 0, 0)),
                 pl.BlockSpec((samples, other_width), lambda i, *_: (0, 0)),
                 pl.BlockSpec((layers, width, width), lambda i, *_: (0, 0, 0)),
                 pl.BlockSpec((layers, width), lambda i, *_: (0, 0)),
@@ -201,7 +210,7 @@
             flops=8_000_000_000, bytes_accessed=20 * 1024 * 1024, transcendentals=0
         ),
         name="pool_and_cross",
-    )(tile_blocks, core, own, other, received, other_feats, cross_w, cross_b)
+    )(tile_blocks, core, own, other, bags, other_feats, cross_w, cross_b)
 
 
 def local(
@@ -231,34 +240,36 @@
         own_half = lax.dynamic_slice(table, (0, core * half), (slab_rows, half)).astype(jnp.bfloat16)
         own_half = own_half.reshape(block_count, block_rows, half).transpose(0, 2, 1)
         own = lax.all_gather(own_half, "mp", axis=0)
-        other = lax.ppermute(own, "replica", [(i, i ^ 1) for i in range(parts)])
+
+    with jax.named_scope("packing"):
+        slots = (evict_owner[0, :, 0] * block_count + evict_block[0]).astype(jnp.bfloat16)
+        slots_block = jnp.pad(slots[None, :], ((0, part - 1), (0, width - count)))
+        sent = pack_blocks(evict_grads[0], slots_block, parts)
+        blocks_row = jnp.pad(
+            bag_blocks[0].astype(jnp.float32), ((0, 0), (0, block_rows - bag_blocks.shape[2]))
+        )[:, None, :]
+        bags_sent = pack_bags(bag_entries[0].T, bag_weights[0].T, bag_target, blocks_row)
+        sent, bags_sent = lax.optimization_barrier((sent, bags_sent))
 
     with jax.named_scope("evicted_over_replica"):
-        slots = (evict_owner[0, :, 0] * block_count + evict_block[0]).astype(jnp.bfloat16)
-        slots_block = jnp.pad(slots[None, None, :], ((0, 0), (0, part - 1), (0, width - count)))
-        sent = pack_blocks(evict_grads[0], slots_block, parts)
         arrived = lax.all_to_all(sent, "replica", split_axis=0, concat_axis=0, tiled=True)
         arrived_slots = arrived[:, count, 0, :count].astype(jnp.int32).reshape(-1)
 
+    with jax.named_scope("bags_over_mp"):
+        bags = lax.all_to_all(bags_sent, "mp", split_axis=0, concat_axis=0, tiled=True)
+        tile_blocks = bags[:, 9, : bag_blocks.shape[2]].astype(jnp.int32).reshape(-1)
+
     with jax.named_scope("parts_over_mp"):
-        blocks_row = jnp.pad(
-            bag_blocks[0].astype(jnp.float32), ((0, 0), (0, 128 - bag_blocks.shape[2]))
-        )[:, None, :]
-        payload = owners_payload(
-            arrived,
-            arrived_slots,
-            bag_entries[0].T,
-            bag_weights[0].T,
-            bag_target,
-            blocks_row,
-            owner_count,
-            block_count,
-        )
+        payload = add_blocks(arrived, arrived_slots, owner_count, block_count)
+        payload, bags = lax.optimization_barrier((payload, bags))
         received = lax.all_to_all(payload, "mp", split_axis=0, concat_axis=0, tiled=True)
-
-    rows = block_count * part
+        received, own = lax.optimization_barrier((received, own))
+
+    with jax.named_scope("table_exchange"):
+        other = lax.ppermute(own, "replica", [(i, i ^ 1) for i in range(parts)])
+
     with jax.named_scope("table_update"):
-        grad_part = jnp.sum(received[:, :rows, :].astype(jnp.float32), axis=0).astype(jnp.bfloat16)
+        grad_part = jnp.sum(received.astype(jnp.float32), axis=0).astype(jnp.bfloat16)
         grads = lax.all_gather(grad_part, "replica", axis=0)
         table_grad = (
             grads.reshape(parts, block_count, part, width)
@@ -269,17 +280,8 @@
         new_table, new_accum = adagrad(table_grad, accum, table)
 
     with jax.named_scope("pooling"):
-        tile_blocks = received[:, rows + 9, : bag_blocks.shape[2]].astype(jnp.int32).reshape(-1)
         cross_out = pool_and_cross(
-            tile_blocks,
-            core.reshape(1),
-            own,
-            other,
-            received,
-            other_feats[0],
-            cross_w,
-            cross_b,
-            rows,
+            tile_blocks, core.reshape(1), own, other, bags, other_feats[0], cross_w, cross_b
         )
     return (cross_out[None], new_table, new_accum)
 

time: 259 us -> 216 us (0.83)
  Pallas kernels: 103 us -> 22 us
  blocking collectives: 89.8 us -> 135 us
  waiting for transfers between devices: 30 us -> 18.1 us
  local copies, waits for them, and re-layouts: 4.14 us -> 6.74 us
    pallas_call x1, Pallas kernels: 82.6 us -> 0.25 us  [pack_blocks(): pl.pallas_call(kernel, out_shape=jax.ShapeDtypeStruct((parts, count + 1,...]
    all_to_all x0 -> x1, blocking collectives: none -> 42.5 us  [local(): lax.all_to_all(sent, 'replica', split_axis=0, concat_axis=0, tiled=True)]
    all_to_all x1, waiting for transfers between devices: 17 us -> 8.78 us  [local(): lax.all_to_all(bags_sent, 'mp', split_axis=0, concat_axis=0, tiled=True)]
    all_gather x1, waiting for transfers between devices: 13 us -> 9.32 us  [local(): own = lax.all_gather(own_half, 'mp', axis=0)]
    unnamed x17 -> x21, local copies, waits for them, and re-layouts: 1.36 us -> 4.56 us
  transfers between devices with their start and end apart: 3 -> 3, of which waited for: 2 -> 2; matrix products, arithmetic and copies ran while one was open for 2% -> 3% of each run, Pallas kernels for 33% -> 2%
where the time goes in v2:
time: 216 us; the launch traced here: 215 us
  blocking collectives  135 us (62%)
  Pallas kernels  22 us (10%)
  waiting for transfers between devices  18.1 us (8%)
  starting transfers between devices  15 us (7%)
  between operations  14.2 us (7%)
  local copies, waits for them, and re-layouts  6.74 us (3%)
  other arithmetic  4.52 us (2%)
    all_to_all x1, blocking collectives, local(): lax.all_to_all(payload, 'mp', split_axis=0, concat_axis=0, tiled=True)  74.2 us
    all_to_all x1, blocking collectives, local(): lax.all_to_all(sent, 'replica', split_axis=0, concat_axis=0, tiled=True)  42.5 us
    pallas_call x1, Pallas kernels, pool_and_cross(): pl.pallas_call(kernel, out_shape=jax.ShapeDtypeStruct((samples, width), j...  18.1 us
    all_gather x1, blocking collectives, local(): grads = lax.all_gather(grad_part, 'replica', axis=0)  18 us
    all_to_all x1, starting transfers between devices, local(): lax.all_to_all(bags_sent, 'mp', split_axis=0, concat_axis=0, tiled=True)  12.6 us
    all_gather x1, waiting for transfers between devices, local(): own = lax.all_gather(own_half, 'mp', axis=0)  9.32 us
    all_to_all x1, waiting for transfers between devices, local(): lax.all_to_all(bags_sent, 'mp', split_axis=0, concat_axis=0, tiled=True)  8.78 us
    unnamed x21, local copies, waits for them, and re-layouts  4.56 us
  transfers between devices with their start and end apart: 3, of which 2 were waited for; matrix products, arithmetic and copies ran while one was open for 3% of the time, Pallas kernels for 2%

profile of v2, /device:TPU:1, one launch (start us, length us, event | category | flops | bytes accessed | tf_op | source)
XLA Modules:
  0.0 215.3 jit_solution(11381685922226200631)
XLA Ops:
  7.2 0.0 all-gather.4.cloned.1.call-start
  7.2 1.0 dynamic-slice_convert_fusion
  8.2 0.8 copy.27
  9.0 0.0 all-gather.4.cloned.1.call-update
  9.0 0.8 copy.26
  9.8 0.7 fusion.4
  10.5 0.0 copy-start.1
  10.5 1.8 copy-done.1
  12.3 0.3 pack_blocks.1
  12.5 0.6 copy-done.3
  13.2 1.2 pack_bags.1
  14.4 42.5 %all_to_all.15.recv_ref = bf16[8,41,16,256]{3,2,1,0:T(8,128)(2,1)S(1)} all-to-all(bf16[8,41,16,256]{3,2,1,0:T(8,128)(2,1)S(1)} %pack_blocks.1), channel_id=1, replica_groups=mesh['mp'=64,'replica'=8] {'replica'}, dimensions={0} | all-to-all | bytes 5373952 | tf_op jit(solution)/shard_map/evicted_over_replica/all_to_all | solution.py:255
  56.8 12.6 %all-to-all-start = ((bf16[64,16,128]{2,1,0:T(8,128)(2,1)}), bf16[64,16,128]{2,1,0:T(8,128)(2,1)S(1)}, u32[]{:S(2)}, u32[]{:S(2)}) async-start(bf16[64,16,128]{2,1,0:T(8,128)(2,1)} %pack_bags.1), calls=%async_computation | async-start | bytes 524288 | tf_op jit(solution)/shard_map/bags_over_mp/all_to_all | solution.py:259
  69.5 0.1 reshape.51.slots_ref
  69.6 2.4 %add_blocks.1 = bf16[64,64,256]{2,1,0:T(8,128)(2,1)S(1)} custom-call(s32[320]{0:T(512)S(1)} %reshape.51.slots_ref, bf16[8,41,16,256]{3,2,1,0:T(8,128)(2,1)S(1)} %all_to_all.15.recv_ref), custom_call_target="tpu_custom_call" | custom-call | bytes 10485760 | tf_op jit(solution)/shard_map/parts_over_mp/add_blocks/pallas_call | solution.py:105
  72.0 1.3 copy-done
  73.4 8.8 %all-to-all-done.bag_ref = bf16[64,16,128]{2,1,0:T(8,128)(2,1)S(1)} async-done(((bf16[64,16,128]{2,1,0:T(8,128)(2,1)}), bf16[64,16,128]{2,1,0:T(8,128)(2,1)S(1)}, u32[]{:S(2)}, u32[]{:S(2)}) %all-to-all-start) | async-done | bytes 262176 | tf_op jit(solution)/shard_map/bags_over_mp/all_to_all | solution.py:259
  82.2 74.2 %all_to_all.16 = bf16[64,64,256]{2,1,0:T(8,128)(2,1)} all-to-all(bf16[64,64,256]{2,1,0:T(8,128)(2,1)} %copy-done), channel_id=1, replica_groups=mesh['mp'=64,'replica'=8] {'mp'}, dimensions={0} | all-to-all | bytes 4194304 | tf_op jit(solution)/shard_map/parts_over_mp/all_to_all | solution.py:265
  156.4 9.3 %all-gather.4.cloned.1.call-done = bf16[256,128,128]{2,1,0:T(8,128)(2,1)} async-done(((bf16[4,128,128]{2,1,0:T(8,128)(2,1)}), bf16[256,128,128]{2,1,0:T(8,128)(2,1)}) %all-gather.4.cloned.1.call-update) | async-done | bytes 8388624 | tf_op jit(solution)/shard_map/table_gather/all_gather | solution.py:242
  165.7 2.4 %collective-permute-start = (bf16[64,4,128,128]{3,2,1,0:T(8,128)(2,1)}, bf16[64,4,128,128]{3,2,1,0:T(8,128)(2,1)}, u32[]{:S(2)}, u32[]{:S(2)}) collective-permute-start(bf16[64,4,128,128]{3,2,1,0:T(8,128)(2,1)} %bitcast.37), channel_id=1, source_target_pairs={{0,1},{1,0},{2,3},{3,2},{4,5},{5,4},{6,7},{7,6},{8,9},{9,8},{10,11... | collective-permute-start | bytes 25165832 | tf_op jit(solution)/shard_map/table_exchange/ppermute | solution.py:269
  168.1 0.1 fusion.2
  168.2 0.1 reshape.50.blocks_ref
  168.3 0.0 copy-start.5
  168.4 0.0 copy-start.7
  168.4 2.0 reduce_sum.23
  170.4 18.0 %all-gather.1 = bf16[512,256]{1,0:T(8,128)(2,1)S(1)} all-gather(bf16[64,256]{1,0:T(8,128)(2,1)S(1)} %reduce_sum.23), channel_id=3, replica_groups=mesh['mp'=64,'replica'=8] {'replica'}, dimensions={0}, use_global_device_ids=true | all-gather | bytes 294912 | tf_op jit(solution)/shard_map/table_update/all_gather | solution.py:273
  188.4 0.1 fusion
  188.6 0.1 reshape.53
  188.7 0.1 div.21
  188.8 0.6 fusion.5
  189.4 1.0 fusion.1
  190.4 18.1 %pool_and_cross.1 = bf16[512,512]{1,0:T(8,128)(2,1)} custom-call(s32[192]{0:T(256)S(1)} %reshape.50.blocks_ref, s32[1]{0:T(128)} %bitcast.8.core_ref, bf16[64,4,128,128]{3,2,1,0:T(8,128)(2,1)} %bitcast.38, bf16[64,4,128,128]{3,2,1,0:T(8,128)(2,1)} %collective-permute-done.other_ref, bf16[64,16,128]{2,1,0:T(8,128)(2,1)S(1)} %all-to-all-done.bag_ref, ...), custom_call_target="tpu_custom_call" | custom-call | flops 8000000000 | bytes 20971520 | tf_op jit(solution)/shard_map/pooling/pool_and_cross/pallas_call | solution.py:185
  (22 shorter events, 0.1 us)
Async XLA Ops:
  7.2 158.5 %all-gather.4.cloned.1.call-start = ((), (), s32[]{:S(2)}) async-start(), calls=%async_computation.3 | async-start | bytes 8519680 | tf_op jit(solution)/shard_map/table_gather/all_gather | solution.py:242
  10.5 2.1 copy-start.2
  10.5 1.8 copy-start.1
  12.3 0.9 copy-start.3
  12.3 0.9 copy-start.4
  56.8 25.3 %all-to-all-start = ((bf16[64,16,128]{2,1,0:T(8,128)(2,1)}), bf16[64,16,128]{2,1,0:T(8,128)(2,1)S(1)}, u32[]{:S(2)}, u32[]{:S(2)}) async-start(bf16[64,16,128]{2,1,0:T(8,128)(2,1)} %pack_bags.1), calls=%async_computation | async-start | bytes 524288 | tf_op jit(solution)/shard_map/bags_over_mp/all_to_all | solution.py:259
  72.0 1.4 copy-start
  156.3 32.4 %copy-start.9 = (f32[512]{0:T(512)S(1)}, f32[512]{0:T(512)}, u32[]{:S(2)}) copy-start(f32[512]{0:T(512)} %param.13) | copy-start | bytes 6148
  156.3 33.0 %copy-start.8 = (f32[512,256]{1,0:T(8,128)S(1)}, f32[512,256]{1,0:T(8,128)}, u32[]{:S(2)}) copy-start(f32[512,256]{1,0:T(8,128)} %param.12) | copy-start | bytes 1572868
  165.7 24.7 %collective-permute-start = (bf16[64,4,128,128]{3,2,1,0:T(8,128)(2,1)}, bf16[64,4,128,128]{3,2,1,0:T(8,128)(2,1)}, u32[]{:S(2)}, u32[]{:S(2)}) collective-permute-start(bf16[64,4,128,128]{3,2,1,0:T(8,128)(2,1)} %bitcast.37), channel_id=1, source_target_pairs={{0,1},{1,0},{2,3},{3,2},{4,5},{5,4},{6,7},{7,6},{8,9},{9,8},{10,11... | collective-permute-start | bytes 25165832 | tf_op jit(solution)/shard_map/table_exchange/ppermute | solution.py:269
  168.3 22.0 %copy-start.5 = (bf16[2,512,512]{2,1,0:T(8,128)(2,1)S(1)}, bf16[2,512,512]{2,1,0:T(8,128)(2,1)}, u32[]{:S(2)}) copy-start(bf16[2,512,512]{2,1,0:T(8,128)(2,1)} %w_ref.1) | copy-start | bytes 3145732
  168.3 22.0 %copy-start.6 = (bf16[1,512,256]{2,1,0:T(8,128)(2,1)S(1)}, bf16[1,512,256]{2,1,0:T(8,128)(2,1)}, u32[]{:S(2)}) copy-start(bf16[1,512,256]{2,1,0:T(8,128)(2,1)} %param.18) | copy-start | bytes 786436
  168.4 22.0 %copy-start.7 = (f32[2,512]{1,0:T(2,128)S(1)}, f32[2,512]{1,0:T(2,128)}, u32[]{:S(2)}) copy-start(f32[2,512]{1,0:T(2,128)} %b_ref.1) | copy-start | bytes 12292
Sparse Core Ops, SparseCore 0:
  11.6 153.9 all-gather.3

commit v3 on v2

v3 whole, which is shorter than its diff:
```python
import jax
import jax.numpy as jnp
from jax import lax
from jax.experimental import pallas as pl
from jax.experimental.pallas import tpu as pltpu
from jax.sharding import PartitionSpec as P

VMEM_LIMIT = 48 * 1024 * 1024
learn_rate = 0.3
BAG_ROWS = 16
SAMPLES = 512


def adagrad(gradient, old_accum, old_table):
    fresh_accum = old_accum + jnp.mean(gradient * gradient, axis=1)
    fresh_table = old_table - learn_rate * gradient / jnp.sqrt(fresh_accum)[:, None]
    return (fresh_table, fresh_accum)


def pack_blocks(me, grads, slots, parts):
    count, rows, width = grads.shape
    part = rows // parts

    def kernel(me_ref, grads_ref, slots_ref, *out_refs):
        starts = [pl.multiple_of((me_ref[0] ^ k) * part, part) for k in range(parts)]

        def place(n, carry):
            for k in range(parts):
                out_refs[k][n] = grads_ref[n, pl.ds(starts[k], part), :]
            return carry

        lax.fori_loop(0, count, place, 0)
        for k in range(parts):
            out_refs[k][count] = slots_ref[...]

    whole = pl.BlockSpec(memory_space=pltpu.VMEM)
    return pl.pallas_call(
        kernel,
        out_shape=[jax.ShapeDtypeStruct((count + 1, part, width), grads.dtype)] * parts,
        in_specs=[pl.BlockSpec(memory_space=pltpu.SMEM)] + [whole] * 2,
        out_specs=[whole] * parts,
        compiler_params=pltpu.CompilerParams(vmem_limit_bytes=VMEM_LIMIT),
        cost_estimate=pl.CostEstimate(flops=0, bytes_accessed=2 * grads.size * 2, transcendentals=0),
        name="pack_blocks",
    )(me, grads, slots)


def pack_bags(entries, weights, targets, blocks):
    owner_count, _, lanes = blocks.shape
    span = 96

    def kernel(entries_ref, weights_ref, targets_ref, blocks_ref, out_ref):
        shift = lax.broadcasted_iota(jnp.int32, (entries_ref.shape[0], lanes), 0) * span

        def place(o, carry):
            columns = pl.ds(pl.multiple_of(o * lanes, lanes), lanes)
            bag = jnp.concatenate(
                [
                    (entries_ref[:, columns] - shift).astype(jnp.float32),
                    weights_ref[:, columns],
                    (targets_ref[:, columns] - 256).astype(jnp.float32),
                    blocks_ref[o],
                    jnp.zeros((BAG_ROWS - 10, lanes), jnp.float32),
                ],
                axis=0,
            )
            out_ref[o] = bag.astype(out_ref.dtype)
            return carry

        lax.fori_loop(0, owner_count, place, 0)

    whole = pl.BlockSpec(memory_space=pltpu.VMEM)
    return pl.pallas_call(
        kernel,
        out_shape=jax.ShapeDtypeStruct((owner_count, BAG_ROWS, lanes), jnp.bfloat16),
        in_specs=[whole] * 4,
        out_specs=whole,
        compiler_params=pltpu.CompilerParams(vmem_limit_bytes=VMEM_LIMIT),
        cost_estimate=pl.CostEstimate(flops=0, bytes_accessed=1024 * 1024, transcendentals=0),
        name="pack_bags",
    )(entries, weights, targets, blocks)


def add_blocks(arrived, owner_count, block_count):
    parts = len(arrived)
    extra, part, width = arrived[0].shape
    count = extra - 1
    lanes = 128

    def kernel(*refs):
        recv_refs = refs[:parts]
        out_ref, acc_ref, numbers_ref, slots_ref, sem = refs[parts:]
        for k in range(parts):
            numbers_ref[pl.ds(k, 1), :] = (
                recv_refs[k][count, :, pl.ds(0, lanes)].astype(jnp.float32)[0:1].astype(jnp.int32)
            )
        copy = pltpu.make_async_copy(numbers_ref, slots_ref, sem)
        copy.start()
        acc_ref[...] = jnp.zeros_like(acc_ref)
        copy.wait()

        def add(n, carry):
            for k in range(parts):
                slot = slots_ref[k, n]
                acc_ref[slot] = acc_ref[slot] + recv_refs[k][n].astype(jnp.float32)
            return carry

        lax.fori_loop(0, count, add, 0)

        def place(o, carry):
            for b in range(block_count):
                out_ref[o, pl.ds(b * part, part), :] = acc_ref[o * block_count + b].astype(out_ref.dtype)
            return carry

        lax.fori_loop(0, owner_count, place, 0)

    whole = pl.BlockSpec(memory_space=pltpu.VMEM)
    return pl.pallas_call(
        kernel,
        out_shape=jax.ShapeDtypeStruct((owner_count, block_count * part, width), jnp.bfloat16),
        in_specs=[whole] * parts,
        out_specs=whole,
        scratch_shapes=[
            pltpu.VMEM((owner_count * block_count, part, width), jnp.float32),
            pltpu.VMEM((parts, lanes), jnp.int32),
            pltpu.SMEM((parts, lanes), jnp.int32),
            pltpu.SemaphoreType.DMA(()),
        ],
        compiler_params=pltpu.CompilerParams(vmem_limit_bytes=VMEM_LIMIT),
        cost_estimate=pl.CostEstimate(flops=0, bytes_accessed=10 * 1024 * 1024, transcendentals=0),
        name="add_blocks",
    )(*arrived)


def pool_parts(first, many, tile_blocks, me, table, bags):
    owner_count, block_count, width, lanes = table.shape
    parts = bags.shape[0]
    per_tile = tile_blocks.shape[0] // (parts * owner_count)
    entry_count = 4
    span = per_tile * lanes // entry_count
    samples = SAMPLES

    def kernel(blocks_ref, me_ref, table_ref, bag_ref, *out_refs):
        step = pl.program_id(0)
        replica = me_ref[0] ^ (step + first)
        position = lax.broadcasted_iota(jnp.int32, (span, lanes), 0)
        sample = lax.broadcasted_iota(jnp.int32, (samples, owner_count * lanes), 0)
        partials, targets = [], []
        for t in range(owner_count):
            bag = bag_ref[0, t].astype(jnp.float32)
            entries = bag[0:entry_count].astype(jnp.int32)
            weights = bag[entry_count : 2 * entry_count]
            targets.append(bag[2 * entry_count : 2 * entry_count + 1].astype(jnp.int32) + 256)
            incidence = jnp.concatenate(
                [
                    jnp.where(position == entries[l : l + 1], weights[l : l + 1], 0.0)
                    for l in range(entry_count)
                ],
                axis=0,
            ).astype(jnp.bfloat16)
            chosen = [blocks_ref[(replica * owner_count + t) * per_tile + j] for j in range(per_tile)]
            slab = jnp.concatenate([table_ref[t, b] for b in chosen], axis=1)
            partials.append(
                jnp.dot(slab, incidence, preferred_element_type=jnp.float32).astype(jnp.bfloat16)
            )
        selector = jnp.where(sample == jnp.concatenate(targets, axis=1), 1.0, 0.0).astype(jnp.bfloat16)
        pooled = lax.dot_general(
            selector,
            jnp.concatenate(partials, axis=1),
            (((1,), (1,)), ((), ())),
            preferred_element_type=jnp.float32,
        ).astype(jnp.bfloat16)
        for i in range(many):

            @pl.when(step == i)
            def _(i=i):
                out_refs[i][...] = pooled

    return pl.pallas_call(
        kernel,
        out_shape=[jax.ShapeDtypeStruct((samples, width), jnp.bfloat16)] * many,
        grid_spec=pltpu.PrefetchScalarGridSpec(
            num_scalar_prefetch=2,
            grid=(many,),
            in_specs=[
                pl.BlockSpec((owner_count, block_count, width, lanes), lambda i, *_: (0, 0, 0, 0)),
                pl.BlockSpec(
                    (1, owner_count, BAG_ROWS, lanes),
                    lambda i, blocks_ref, me_ref: (me_ref[0] ^ (i + first), 0, 0, 0),
                ),
            ],
            out_specs=[pl.BlockSpec((samples, width), lambda i, *_: (0, 0))] * many,
        ),
        compiler_params=pltpu.CompilerParams(
            dimension_semantics=("arbitrary",), vmem_limit_bytes=VMEM_LIMIT
        ),
        cost_estimate=pl.CostEstimate(
            flops=many * 1_000_000_000, bytes_accessed=5 * 1024 * 1024, transcendentals=0
        ),
        name="pool_parts",
    )(tile_blocks, me, table, bags)


def cross_layers(pooled_parts, other_feats, cross_w, cross_b):
    parts = len(pooled_parts)
    samples, width = pooled_parts[0].shape
    layers, full, _ = cross_w.shape
    tile = 128

    def kernel(*refs):
        feats_ref, w_ref, b_ref, out_ref = refs[parts:]
        pooled = refs[0][...].astype(jnp.float32)
        for j in range(1, parts):
            pooled = pooled + refs[j][...].astype(jnp.float32)
        first = jnp.concatenate([pooled, feats_ref[...].astype(jnp.float32)], axis=1)
        crossed = first
        for layer in range(layers):
            mixing = (
                jnp.dot(crossed.astype(jnp.bfloat16), w_ref[layer], preferred_element_type=jnp.float32)
                + b_ref[layer : layer + 1, :]
            )
            crossed = first * mixing + crossed
        out_ref[...] = crossed.astype(out_ref.dtype)

    return pl.pallas_call(
        kernel,
        out_shape=jax.ShapeDtypeStruct((samples, full), jnp.bfloat16),
        grid=(samples // tile,),
        in_specs=[
            *[pl.BlockSpec((tile, width), lambda i: (i, 0))] * parts,
            pl.BlockSpec((tile, full - width), lambda i: (i, 0)),
            pl.BlockSpec((layers, full, full), lambda i: (0, 0, 0)),
            pl.BlockSpec((layers, full), lambda i: (0, 0)),
        ],
        out_specs=pl.BlockSpec((tile, full), lambda i: (i, 0)),
        compiler_params=pltpu.CompilerParams(
            dimension_semantics=("arbitrary",), vmem_limit_bytes=VMEM_LIMIT
        ),
        cost_estimate=pl.CostEstimate(
            flops=2 * layers * samples * full * full, bytes_accessed=5 * 1024 * 1024, transcendentals=0
        ),
        name="cross_layers",
    )(*pooled_parts, other_feats, cross_w, cross_b)


def local(
    table,
    accum,
    bag_blocks,
    bag_entries,
    bag_weights,
    bag_target,
    other_feats,
    cross_w,
    cross_b,
    evict_grads,
    evict_owner,
    evict_block,
):
    owner_count = lax.axis_size("mp")
    parts = lax.axis_size("replica")
    count, block_rows, width = evict_grads.shape[1:]
    slab_rows = table.shape[0]
    block_count = slab_rows // block_rows
    part = block_rows // parts
    columns = owner_count // parts
    me = lax.axis_index("replica").reshape(1)

    def to_replica(arrays, first):
        return [
            lax.ppermute(array, "replica", [(r, r ^ k) for r in range(parts)]) if k else array
            for k, array in enumerate(arrays, first)
        ]

    with jax.named_scope("packing"):
        slab = table.astype(jnp.bfloat16).reshape(block_count, block_rows, width).transpose(0, 2, 1)
        slots = (evict_owner[0, :, 0] * block_count + evict_block[0]).astype(jnp.bfloat16)
        slots_block = jnp.pad(slots[None, :], ((0, part - 1), (0, width - count)))
        sent = pack_blocks(me, evict_grads[0], slots_block, parts)
        blocks_row = jnp.pad(
            bag_blocks[0].astype(jnp.float32), ((0, 0), (0, block_rows - bag_blocks.shape[2]))
        )[:, None, :]
        bags_sent = pack_bags(bag_entries[0].T, bag_weights[0].T, bag_target, blocks_row)
        sent, bags_sent, slab = lax.optimization_barrier((sent, bags_sent, slab))

    with jax.named_scope("table_gather"):
        swap = [
            ((z * columns + y) * parts + r, (r * columns + y) * parts + z)
            for z in range(parts)
            for y in range(columns)
            for r in range(parts)
        ]
        moved = lax.ppermute(slab, ("mp", "replica"), swap)
        rows_of_z = [[z * columns + y for y in range(columns)] for z in range(parts)]
        slabs = lax.all_gather(moved, "mp", axis=0, axis_index_groups=rows_of_z)

    with jax.named_scope("evicted_over_replica"):
        arrived = to_replica(sent, 0)

    with jax.named_scope("bags_over_mp"):
        bags = lax.all_to_all(bags_sent, "mp", split_axis=0, concat_axis=0, tiled=True)
        bags = lax.all_to_all(
            bags.reshape(parts, columns, BAG_ROWS, block_rows), "replica", split_axis=0, concat_axis=0, tiled=True
        )
        tile_blocks = bags[:, :, 9, : bag_blocks.shape[2]].astype(jnp.int32).reshape(-1)

    with jax.named_scope("parts_over_mp"):
        payload = add_blocks(arrived, owner_count, block_count)
        payload, bags, tile_blocks = lax.optimization_barrier((payload, bags, tile_blocks))
        received = lax.all_to_all(payload, "mp", split_axis=0, concat_axis=0, tiled=True)

    with jax.named_scope("pooling"):
        pooled = []
        for first in range(0, parts, parts // 2):
            pooled += to_replica(pool_parts(first, parts // 2, tile_blocks, me, slabs, bags), first)

    with jax.named_scope("table_update"):
        grad_part = jnp.sum(received.astype(jnp.float32), axis=0).astype(jnp.bfloat16)
        grads = lax.all_gather(grad_part, "replica", axis=0)
        table_grad = (
            grads.reshape(parts, block_count, part, width)
            .transpose(1, 0, 2, 3)
            .reshape(slab_rows, width)
            .astype(jnp.float32)
        )
        new_table, new_accum = adagrad(table_grad, accum, table)

    with jax.named_scope("cross"):
        cross_out = cross_layers(pooled, other_feats[0], cross_w, cross_b)
    return (cross_out[None], new_table, new_accum)


def solution(mesh):
    in_specs = (
        P("mp", None),
        P("mp"),
        P("replica", "mp", None),
        P("replica", "mp", None),
        P("replica", "mp", None),
        P("replica", "mp"),
        P("replica", "mp", None),
        P(),
        P(),
        P("replica", "mp", None, None),
        P("replica", "mp", None),
        P("replica", "mp"),
    )
    out_specs = (P("replica", "mp", None), P("mp", None), P("mp"))
    return jax.shard_map(local, mesh=mesh, in_specs=in_specs, out_specs=out_specs, check_vma=False)
```

time: 216 us -> 194 us (0.90)
  blocking collectives: 135 us -> 16.6 us
  starting transfers between devices: 15 us -> 95.2 us
  waiting for transfers between devices: 18.1 us -> 37.9 us
  Pallas kernels: 22 us -> 18.1 us
    all_to_all x2 -> x0, blocking collectives: 117 us -> none  [the longest x1 74.2 us: local(): lax.all_to_all(payload, 'mp', split_axis=0, concat_axis=0, tiled=True)]
    ppermute x1 -> x15, starting transfers between devices: 2.38 us -> 64.3 us  [the longest x14 60.3 us: to_replica(): lax.ppermute(array, 'replica', [(r, r ^ k) for r in range(parts)])]
    ppermute x1 -> x15, waiting for transfers between devices: 0.01 us -> 32 us  [the longest x14 29.6 us: to_replica(): lax.ppermute(array, 'replica', [(r, r ^ k) for r in range(parts)])]
    all_to_all x0 -> x2, starting transfers between devices: none -> 13.4 us  [the longest x1 10 us: local(): lax.all_to_all(payload, 'mp', split_axis=0, concat_axis=0, tiled=True)]
    all_gather x1, waiting for transfers between devices: 9.32 us -> 0.02 us  [local(): slabs = lax.all_gather(moved, 'mp', axis=0, axis_index_groups=rows_of_z)]
    all_to_all x1, waiting for transfers between devices: 8.78 us -> 0.01 us  [local(): lax.all_to_all(bags_sent, 'mp', split_axis=0, concat_axis=0, tiled=True)]
    all_to_all x0 -> x2, waiting for transfers between devices: none -> 5.87 us  [the longest x1 5.87 us: local(): lax.all_to_all(payload, 'mp', split_axis=0, concat_axis=0, tiled=True)]
    pallas_call x2 -> x4, Pallas kernels: 18.3 us -> 12.9 us  [the longest x2 8.36 us: pool_parts(): pl.pallas_call(kernel, out_shape=[jax.ShapeDtypeStruct((samples, width),...]
  transfers between devices with their start and end apart: 3 -> 19, of which waited for: 2 -> 8; matrix products, arithmetic and copies ran while one was open for 3% -> 1% of each run, Pallas kernels for 2% -> 8%
where the time goes in v3:
time: 194 us; the launch traced here: 193 us
  starting transfers between devices  95.2 us (49%)
  waiting for transfers between devices  37.9 us (20%)
  Pallas kernels  18.1 us (9%)
  blocking collectives  16.6 us (9%)
  between operations  14.4 us (7%)
  other arithmetic  5.46 us (3%)
  local copies, waits for them, and re-layouts  5.38 us (3%)
    ppermute x14, starting transfers between devices, to_replica(): lax.ppermute(array, 'replica', [(r, r ^ k) for r in range(parts)])  60.3 us
    ppermute x14, waiting for transfers between devices, to_replica(): lax.ppermute(array, 'replica', [(r, r ^ k) for r in range(parts)])  29.6 us
    all_to_all x1, starting transfers between devices, local(): lax.all_to_all(bags_sent, 'mp', split_axis=0, concat_axis=0, tiled=True)  17.4 us
    all_gather x1, blocking collectives, local(): grads = lax.all_gather(grad_part, 'replica', axis=0)  16.6 us
    all_to_all x1, starting transfers between devices, local(): lax.all_to_all(payload, 'mp', split_axis=0, concat_axis=0, tiled=True)  10 us
    pallas_call x2, Pallas kernels, pool_parts(): pl.pallas_call(kernel, out_shape=[jax.ShapeDtypeStruct((samples, width),...  8.36 us
    all_to_all x1, waiting for transfers between devices, local(): lax.all_to_all(payload, 'mp', split_axis=0, concat_axis=0, tiled=True)  5.87 us
    unnamed x21, local copies, waits for them, and re-layouts  4.18 us
  transfers between devices with their start and end apart: 19, of which 8 were waited for; matrix products, arithmetic and copies ran while one was open for 1% of the time, Pallas kernels for 8%

profile of v3, /device:TPU:1, one launch (start us, length us, event | category | flops | bytes accessed | tf_op | source)
XLA Modules:
  0.0 193.0 jit_solution(7762231337595417097)
XLA Ops:
  11.5 1.8 pack_blocks.1
  14.6 17.4 %all-to-all-start = ((bf16[64,16,128]{2,1,0:T(8,128)(2,1)}), bf16[64,16,128]{2,1,0:T(8,128)(2,1)}, u32[]{:S(2)}, u32[]{:S(2)}) async-start(bf16[64,16,128]{2,1,0:T(8,128)(2,1)} %pack_bags.1), calls=%async_computation | async-start | bytes 524288 | tf_op jit(solution)/shard_map/bags_over_mp/all_to_all | solution.py:301
  32.0 4.0 %collective-permute-start.7 = (bf16[4,256,128]{1,2,0:T(8,128)(2,1)S(1)}, bf16[4,256,128]{1,2,0:T(8,128)(2,1)S(1)}, u32[]{:S(2)}, u32[]{:S(2)}) collective-permute-start(bf16[4,256,128]{1,2,0:T(8,128)(2,1)S(1)} %bitcast.39), channel_id=1, source_target_pairs={{0,0},{1,64},{2,128},{3,192},{4,256},{5,320},{6,384},{7,448},{8,8}... | collective-permute-start | bytes 786440 | tf_op jit(solution)/shard_map/table_gather/ppermute | solution.py:293
  36.0 1.9 collective-permute-start
  38.0 4.9 %collective-permute-start.1 = (bf16[41,16,256]{2,1,0:T(8,128)(2,1)S(1)}, bf16[41,16,256]{2,1,0:T(8,128)(2,1)S(1)}, u32[]{:S(2)}, u32[]{:S(2)}) collective-permute-start(bf16[41,16,256]{2,1,0:T(8,128)(2,1)S(1)} %get-tuple-element.42), channel_id=1, source_target_pairs={{0,2},{1,3},{2,0},{3,1},{4,6},{5,7},{6,4},{7,5},{8,10},{9,11},{10,... | collective-permute-start | bytes 1007624 | tf_op jit(solution)/shard_map/evicted_over_replica/ppermute | solution.py:271
  42.9 2.4 %collective-permute-done.7 = bf16[4,256,128]{1,2,0:T(8,128)(2,1)S(1)} collective-permute-done((bf16[4,256,128]{1,2,0:T(8,128)(2,1)S(1)}, bf16[4,256,128]{1,2,0:T(8,128)(2,1)S(1)}, u32[]{:S(2)}, u32[]{:S(2)}) %collective-permute-start.7) | collective-permute-done | bytes 262176 | tf_op jit(solution)/shard_map/table_gather/ppermute | solution.py:293
  46.1 17.7 %collective-permute-start.2 = (bf16[41,16,256]{2,1,0:T(8,128)(2,1)}, bf16[41,16,256]{2,1,0:T(8,128)(2,1)S(1)}, u32[]{:S(2)}, u32[]{:S(2)}) collective-permute-start(bf16[41,16,256]{2,1,0:T(8,128)(2,1)} %get-tuple-element.43), channel_id=1, source_target_pairs={{0,3},{1,2},{2,1},{3,0},{4,7},{5,6},{6,5},{7,4},{8,11},{9,10},{10,... | collective-permute-start | bytes 1007624 | tf_op jit(solution)/shard_map/evicted_over_replica/ppermute | solution.py:271
  63.9 1.9 collective-permute-start.3
  65.8 4.7 %collective-permute-start.4 = (bf16[41,16,256]{2,1,0:T(8,128)(2,1)}, bf16[41,16,256]{2,1,0:T(8,128)(2,1)S(1)}, u32[]{:S(2)}, u32[]{:S(2)}) collective-permute-start(bf16[41,16,256]{2,1,0:T(8,128)(2,1)} %get-tuple-element.45), channel_id=1, source_target_pairs={{0,5},{1,4},{2,7},{3,6},{4,1},{5,0},{6,3},{7,2},{8,13},{9,12},{10,... | collective-permute-start | bytes 1007624 | tf_op jit(solution)/shard_map/evicted_over_replica/ppermute | solution.py:271
  70.5 1.9 collective-permute-start.5
  72.4 5.3 %collective-permute-start.6 = (bf16[41,16,256]{2,1,0:T(8,128)(2,1)S(1)}, bf16[41,16,256]{2,1,0:T(8,128)(2,1)S(1)}, u32[]{:S(2)}, u32[]{:S(2)}) collective-permute-start(bf16[41,16,256]{2,1,0:T(8,128)(2,1)S(1)} %get-tuple-element.47), channel_id=1, source_target_pairs={{0,7},{1,6},{2,5},{3,4},{4,3},{5,2},{6,1},{7,0},{8,15},{9,14},{10,... | collective-permute-start | bytes 1007624 | tf_op jit(solution)/shard_map/evicted_over_replica/ppermute | solution.py:271
  77.8 3.4 %all-to-all-start.1 = ((bf16[8,8,16,128]{3,2,1,0:T(8,128)(2,1)}), bf16[8,8,16,128]{3,2,1,0:T(8,128)(2,1)S(1)}, u32[]{:S(2)}, u32[]{:S(2)}) async-start(bf16[8,8,16,128]{3,2,1,0:T(8,128)(2,1)} %bitcast.11), calls=%async_computation.1 | async-start | bytes 524288 | tf_op jit(solution)/shard_map/bags_over_mp/all_to_all | solution.py:302
  81.2 6.4 %collective-permute-done.4.refs_5_ = bf16[41,16,256]{2,1,0:T(8,128)(2,1)S(1)} collective-permute-done((bf16[41,16,256]{2,1,0:T(8,128)(2,1)}, bf16[41,16,256]{2,1,0:T(8,128)(2,1)S(1)}, u32[]{:S(2)}, u32[]{:S(2)}) %collective-permute-start.4) | collective-permute-done | bytes 335904 | tf_op jit(solution)/shard_map/evicted_over_replica/ppermute | solution.py:271
  87.5 7.5 %collective-permute-done.5.refs_6_ = bf16[41,16,256]{2,1,0:T(8,128)(2,1)S(1)} collective-permute-done((bf16[41,16,256]{2,1,0:T(8,128)(2,1)}, bf16[41,16,256]{2,1,0:T(8,128)(2,1)S(1)}, u32[]{:S(2)}, u32[]{:S(2)}) %collective-permute-start.5) | collective-permute-done | bytes 335904 | tf_op jit(solution)/shard_map/evicted_over_replica/ppermute | solution.py:271
  95.1 7.2 %collective-permute-done.6.refs_7_ = bf16[41,16,256]{2,1,0:T(8,128)(2,1)S(1)} collective-permute-done((bf16[41,16,256]{2,1,0:T(8,128)(2,1)S(1)}, bf16[41,16,256]{2,1,0:T(8,128)(2,1)S(1)}, u32[]{:S(2)}, u32[]{:S(2)}) %collective-permute-start.6) | collective-permute-done | bytes 335904 | tf_op jit(solution)/shard_map/evicted_over_replica/ppermute | solution.py:271
  102.3 4.0 %add_blocks.1 = bf16[64,64,256]{2,1,0:T(8,128)(2,1)} custom-call(bf16[41,16,256]{2,1,0:T(8,128)(2,1)S(1)} %get-tuple-element.40.refs_0_, bf16[41,16,256]{2,1,0:T(8,128)(2,1)S(1)} %collective-permute-done.refs_1_, bf16[41,16,256]{2,1,0:T(8,128)(2,1)S(1)} %collective-permute-done.1.refs_2_, bf16[41,16,256]{2,1,0:T(8,128)(2,1)S(1)} %collective-permute-done.2.refs_3_, ...), custom_call_target="tpu_custom_call" | custom-call | bytes 10485760 | tf_op jit(solution)/shard_map/parts_over_mp/add_blocks/pallas_call | solution.py:118
  106.6 10.0 %all-to-all-start.2 = ((bf16[64,64,256]{2,1,0:T(8,128)(2,1)}), bf16[64,64,256]{2,1,0:T(8,128)(2,1)}, u32[]{:S(2)}, u32[]{:S(2)}) async-start(bf16[64,64,256]{2,1,0:T(8,128)(2,1)} %add_blocks.1), calls=%async_computation.2 | async-start | bytes 4194304 | tf_op jit(solution)/shard_map/parts_over_mp/all_to_all | solution.py:310
  118.3 4.2 %pool_parts.3 = (bf16[512,256]{1,0:T(8,128)(2,1)S(1)}, bf16[512,256]{1,0:T(8,128)(2,1)S(1)}, bf16[512,256]{1,0:T(8,128)(2,1)S(1)}, bf16[512,256]{1,0:T(8,128)(2,1)S(1)}) custom-call(s32[192]{0:T(256)S(1)} %reshape.50.blocks_ref, s32[1]{0:T(128)} %bitcast.me_ref, bf16[8,4,256,128]{3,2,1,0:T(8,128)(2,1)S(1)} %bitcast.35, ...), custom_call_target="tpu_custom_call" | custom-call | flops 4000000000 | bytes 5242880 | tf_op jit(solution)/shard_map/pooling/pool_parts/pallas_call | solution.py:179
  122.4 2.9 %collective-permute-start.11 = (bf16[512,256]{1,0:T(8,128)(2,1)S(1)}, bf16[512,256]{1,0:T(8,128)(2,1)S(1)}, u32[]{:S(2)}, u32[]{:S(2)}) collective-permute-start(bf16[512,256]{1,0:T(8,128)(2,1)S(1)} %get-tuple-element.56), channel_id=1, source_target_pairs={{0,4},{1,5},{2,6},{3,7},{4,0},{5,1},{6,2},{7,3},{8,12},{9,13},{10,... | collective-permute-start | bytes 786440 | tf_op jit(solution)/shard_map/pooling/ppermute | solution.py:271
  125.4 4.9 %collective-permute-start.12 = (bf16[512,256]{1,0:T(8,128)(2,1)S(1)}, bf16[512,256]{1,0:T(8,128)(2,1)S(1)}, u32[]{:S(2)}, u32[]{:S(2)}) collective-permute-start(bf16[512,256]{1,0:T(8,128)(2,1)S(1)} %get-tuple-element.57), channel_id=1, source_target_pairs={{0,5},{1,4},{2,7},{3,6},{4,1},{5,0},{6,3},{7,2},{8,13},{9,12},{10,... | collective-permute-start | bytes 786440 | tf_op jit(solution)/shard_map/pooling/ppermute | solution.py:271
  130.3 2.4 %collective-permute-start.13 = (bf16[512,256]{1,0:T(8,128)(2,1)S(1)}, bf16[512,256]{1,0:T(8,128)(2,1)S(1)}, u32[]{:S(2)}, u32[]{:S(2)}) collective-permute-start(bf16[512,256]{1,0:T(8,128)(2,1)S(1)} %get-tuple-element.58), channel_id=1, source_target_pairs={{0,6},{1,7},{2,4},{3,5},{4,2},{5,3},{6,0},{7,1},{8,14},{9,15},{10,... | collective-permute-start | bytes 786440 | tf_op jit(solution)/shard_map/pooling/ppermute | solution.py:271
  132.7 3.8 %collective-permute-start.14 = (bf16[512,256]{1,0:T(8,128)(2,1)S(1)}, bf16[512,256]{1,0:T(8,128)(2,1)S(1)}, u32[]{:S(2)}, u32[]{:S(2)}) collective-permute-start(bf16[512,256]{1,0:T(8,128)(2,1)S(1)} %get-tuple-element.59), channel_id=1, source_target_pairs={{0,7},{1,6},{2,5},{3,4},{4,3},{5,2},{6,1},{7,0},{8,15},{9,14},{10,... | collective-permute-start | bytes 786440 | tf_op jit(solution)/shard_map/pooling/ppermute | solution.py:271
  136.5 4.2 %pool_parts.2 = (bf16[512,256]{1,0:T(8,128)(2,1)S(1)}, bf16[512,256]{1,0:T(8,128)(2,1)S(1)}, bf16[512,256]{1,0:T(8,128)(2,1)S(1)}, bf16[512,256]{1,0:T(8,128)(2,1)S(1)}) custom-call(s32[192]{0:T(256)S(1)} %reshape.50.blocks_ref, s32[1]{0:T(128)} %bitcast.me_ref, bf16[8,4,256,128]{3,2,1,0:T(8,128)(2,1)S(1)} %bitcast.36, ...), custom_call_target="tpu_custom_call" | custom-call | flops 4000000000 | bytes 5242880 | tf_op jit(solution)/shard_map/pooling/pool_parts/pallas_call | solution.py:179
  140.7 1.9 collective-permute-start.10
  142.6 2.8 %collective-permute-start.8 = (bf16[512,256]{1,0:T(8,128)(2,1)S(1)}, bf16[512,256]{1,0:T(8,128)(2,1)S(1)}, u32[]{:S(2)}, u32[]{:S(2)}) collective-permute-start(bf16[512,256]{1,0:T(8,128)(2,1)S(1)} %get-tuple-element.53), channel_id=1, source_target_pairs={{0,1},{1,0},{2,3},{3,2},{4,5},{5,4},{6,7},{7,6},{8,9},{9,8},{10,11... | collective-permute-start | bytes 786440 | tf_op jit(solution)/shard_map/pooling/ppermute | solution.py:271
  145.4 3.3 %collective-permute-start.9 = (bf16[512,256]{1,0:T(8,128)(2,1)S(1)}, bf16[512,256]{1,0:T(8,128)(2,1)S(1)}, u32[]{:S(2)}, u32[]{:S(2)}) collective-permute-start(bf16[512,256]{1,0:T(8,128)(2,1)S(1)} %get-tuple-element.54), channel_id=1, source_target_pairs={{0,2},{1,3},{2,0},{3,1},{4,6},{5,7},{6,4},{7,5},{8,10},{9,11},{10,... | collective-permute-start | bytes 786440 | tf_op jit(solution)/shard_map/pooling/ppermute | solution.py:271
  148.7 2.4 %collective-permute-done.14.refs_7_ = bf16[512,256]{1,0:T(8,128)(2,1)S(1)} collective-permute-done((bf16[512,256]{1,0:T(8,128)(2,1)S(1)}, bf16[512,256]{1,0:T(8,128)(2,1)S(1)}, u32[]{:S(2)}, u32[]{:S(2)}) %collective-permute-start.14) | collective-permute-done | bytes 262176 | tf_op jit(solution)/shard_map/pooling/ppermute | solution.py:271
  151.4 5.8 %collective-permute-done.9.refs_2_ = bf16[512,256]{1,0:T(8,128)(2,1)S(1)} collective-permute-done((bf16[512,256]{1,0:T(8,128)(2,1)S(1)}, bf16[512,256]{1,0:T(8,128)(2,1)S(1)}, u32[]{:S(2)}, u32[]{:S(2)}) %collective-permute-start.9) | collective-permute-done | bytes 262176 | tf_op jit(solution)/shard_map/pooling/ppermute | solution.py:271
  157.2 2.7 %cross_layers.1 = bf16[512,512]{1,0:T(8,128)(2,1)} custom-call(bf16[512,256]{1,0:T(8,128)(2,1)S(1)} %get-tuple-element.52.refs_0_, bf16[512,256]{1,0:T(8,128)(2,1)S(1)} %collective-permute-done.8.refs_1_, bf16[512,256]{1,0:T(8,128)(2,1)S(1)} %collective-permute-done.9.refs_2_, bf16[512,256]{1,0:T(8,128)(2,1)S(1)} %collective-permute-done.10.refs_3_, ...), custom_call_target="tpu_custom_call" | custom-call | flops 536870912 | bytes 5242880 | tf_op jit(solution)/shard_map/cross/cross_layers/pallas_call | solution.py:225
  159.9 5.9 %all-to-all-done.2 = bf16[64,64,256]{2,1,0:T(8,128)(2,1)} async-done(((bf16[64,64,256]{2,1,0:T(8,128)(2,1)}), bf16[64,64,256]{2,1,0:T(8,128)(2,1)}, u32[]{:S(2)}, u32[]{:S(2)}) %all-to-all-start.2) | async-done | bytes 2097184 | tf_op jit(solution)/shard_map/parts_over_mp/all_to_all | solution.py:310
  165.8 1.9 reduce_sum.23
  167.7 16.6 %all-gather.1 = bf16[512,256]{1,0:T(8,128)(2,1)S(1)} all-gather(bf16[64,256]{1,0:T(8,128)(2,1)S(1)} %reduce_sum.23), channel_id=3, replica_groups=mesh['mp'=64,'replica'=8] {'replica'}, dimensions={0}, use_global_device_ids=true | all-gather | bytes 294912 | tf_op jit(solution)/shard_map/table_update/all_gather | solution.py:319
  (52 shorter events, 10.5 us)
Async XLA Ops:
  7.2 6.2 %copy-start.3 = (s32[1,8192,4]{1,2,0:T(4,128)S(1)}, s32[1,8192,4]{1,2,0:T(4,128)}, u32[]{:S(2)}) copy-start(s32[1,8192,4]{1,2,0:T(4,128)} %param.15) | copy-start | bytes 393220
  7.2 6.2 %copy-start.4 = (f32[1,8192,4]{1,2,0:T(4,128)S(1)}, f32[1,8192,4]{1,2,0:T(4,128)}, u32[]{:S(2)}) copy-start(f32[1,8192,4]{1,2,0:T(4,128)} %param.16) | copy-start | bytes 393220
  7.2 6.2 %copy-start.5 = (s32[1,8192]{1,0:T(1,128)S(1)}, s32[1,8192]{1,0:T(1,128)}, u32[]{:S(2)}) copy-start(s32[1,8192]{1,0:T(1,128)} %targets_ref.1) | copy-start | bytes 98308
  9.8 1.7 copy-start
  14.6 63.2 %all-to-all-start = ((bf16[64,16,128]{2,1,0:T(8,128)(2,1)}), bf16[64,16,128]{2,1,0:T(8,128)(2,1)}, u32[]{:S(2)}, u32[]{:S(2)}) async-start(bf16[64,16,128]{2,1,0:T(8,128)(2,1)} %pack_bags.1), calls=%async_computation | async-start | bytes 524288 | tf_op jit(solution)/shard_map/bags_over_mp/all_to_all | solution.py:301
  32.0 84.7 %all-gather.4.cloned.1.call-start = ((), (), s32[]{:S(2)}) async-start(), calls=%async_computation.3 | async-start | bytes 2359296 | tf_op jit(solution)/shard_map/table_gather/all_gather | solution.py:295
  32.0 13.2 %collective-permute-start.7 = (bf16[4,256,128]{1,2,0:T(8,128)(2,1)S(1)}, bf16[4,256,128]{1,2,0:T(8,128)(2,1)S(1)}, u32[]{:S(2)}, u32[]{:S(2)}) collective-permute-start(bf16[4,256,128]{1,2,0:T(8,128)(2,1)S(1)} %bitcast.39), channel_id=1, source_target_pairs={{0,0},{1,64},{2,128},{3,192},{4,256},{5,320},{6,384},{7,448},{8,8}... | collective-permute-start | bytes 786440 | tf_op jit(solution)/shard_map/table_gather/ppermute | solution.py:293
  36.0 34.5 %collective-permute-start = (bf16[41,16,256]{2,1,0:T(8,128)(2,1)S(1)}, bf16[41,16,256]{2,1,0:T(8,128)(2,1)S(1)}, u32[]{:S(2)}, u32[]{:S(2)}) collective-permute-start(bf16[41,16,256]{2,1,0:T(8,128)(2,1)S(1)} %get-tuple-element.41), channel_id=1, source_target_pairs={{0,1},{1,0},{2,3},{3,2},{4,5},{5,4},{6,7},{7,6},{8,9},{9,8},{10,11... | collective-permute-start | bytes 1007624 | tf_op jit(solution)/shard_map/evicted_over_replica/ppermute | solution.py:271
  38.0 34.5 %collective-permute-start.1 = (bf16[41,16,256]{2,1,0:T(8,128)(2,1)S(1)}, bf16[41,16,256]{2,1,0:T(8,128)(2,1)S(1)}, u32[]{:S(2)}, u32[]{:S(2)}) collective-permute-start(bf16[41,16,256]{2,1,0:T(8,128)(2,1)S(1)} %get-tuple-element.42), channel_id=1, source_target_pairs={{0,2},{1,3},{2,0},{3,1},{4,6},{5,7},{6,4},{7,5},{8,10},{9,11},{10,... | collective-permute-start | bytes 1007624 | tf_op jit(solution)/shard_map/evicted_over_replica/ppermute | solution.py:271
  46.1 35.0 %collective-permute-start.2 = (bf16[41,16,256]{2,1,0:T(8,128)(2,1)}, bf16[41,16,256]{2,1,0:T(8,128)(2,1)S(1)}, u32[]{:S(2)}, u32[]{:S(2)}) collective-permute-start(bf16[41,16,256]{2,1,0:T(8,128)(2,1)} %get-tuple-element.43), channel_id=1, source_target_pairs={{0,3},{1,2},{2,1},{3,0},{4,7},{5,6},{6,5},{7,4},{8,11},{9,10},{10,... | collective-permute-start | bytes 1007624 | tf_op jit(solution)/shard_map/evicted_over_replica/ppermute | solution.py:271
  63.9 17.3 %collective-permute-start.3 = (bf16[41,16,256]{2,1,0:T(8,128)(2,1)}, bf16[41,16,256]{2,1,0:T(8,128)(2,1)S(1)}, u32[]{:S(2)}, u32[]{:S(2)}) collective-permute-start(bf16[41,16,256]{2,1,0:T(8,128)(2,1)} %get-tuple-element.44), channel_id=1, source_target_pairs={{0,4},{1,5},{2,6},{3,7},{4,0},{5,1},{6,2},{7,3},{8,12},{9,13},{10,... | collective-permute-start | bytes 1007624 | tf_op jit(solution)/shard_map/evicted_over_replica/ppermute | solution.py:271
  65.8 21.7 %collective-permute-start.4 = (bf16[41,16,256]{2,1,0:T(8,128)(2,1)}, bf16[41,16,256]{2,1,0:T(8,128)(2,1)S(1)}, u32[]{:S(2)}, u32[]{:S(2)}) collective-permute-start(bf16[41,16,256]{2,1,0:T(8,128)(2,1)} %get-tuple-element.45), channel_id=1, source_target_pairs={{0,5},{1,4},{2,7},{3,6},{4,1},{5,0},{6,3},{7,2},{8,13},{9,12},{10,... | collective-permute-start | bytes 1007624 | tf_op jit(solution)/shard_map/evicted_over_replica/ppermute | solution.py:271
  70.5 24.6 %collective-permute-start.5 = (bf16[41,16,256]{2,1,0:T(8,128)(2,1)}, bf16[41,16,256]{2,1,0:T(8,128)(2,1)S(1)}, u32[]{:S(2)}, u32[]{:S(2)}) collective-permute-start(bf16[41,16,256]{2,1,0:T(8,128)(2,1)} %get-tuple-element.46), channel_id=1, source_target_pairs={{0,6},{1,7},{2,4},{3,5},{4,2},{5,3},{6,0},{7,1},{8,14},{9,15},{10,... | collective-permute-start | bytes 1007624 | tf_op jit(solution)/shard_map/evicted_over_replica/ppermute | solution.py:271
  72.4 29.8 %collective-permute-start.6 = (bf16[41,16,256]{2,1,0:T(8,128)(2,1)S(1)}, bf16[41,16,256]{2,1,0:T(8,128)(2,1)S(1)}, u32[]{:S(2)}, u32[]{:S(2)}) collective-permute-start(bf16[41,16,256]{2,1,0:T(8,128)(2,1)S(1)} %get-tuple-element.47), channel_id=1, source_target_pairs={{0,7},{1,6},{2,5},{3,4},{4,3},{5,2},{6,1},{7,0},{8,15},{9,14},{10,... | collective-permute-start | bytes 1007624 | tf_op jit(solution)/shard_map/evicted_over_replica/ppermute | solution.py:271
  77.8 28.5 %all-to-all-start.1 = ((bf16[8,8,16,128]{3,2,1,0:T(8,128)(2,1)}), bf16[8,8,16,128]{3,2,1,0:T(8,128)(2,1)S(1)}, u32[]{:S(2)}, u32[]{:S(2)}) async-start(bf16[8,8,16,128]{3,2,1,0:T(8,128)(2,1)} %bitcast.11), calls=%async_computation.1 | async-start | bytes 524288 | tf_op jit(solution)/shard_map/bags_over_mp/all_to_all | solution.py:302
  106.6 59.2 %all-to-all-start.2 = ((bf16[64,64,256]{2,1,0:T(8,128)(2,1)}), bf16[64,64,256]{2,1,0:T(8,128)(2,1)}, u32[]{:S(2)}, u32[]{:S(2)}) async-start(bf16[64,64,256]{2,1,0:T(8,128)(2,1)} %add_blocks.1), calls=%async_computation.2 | async-start | bytes 4194304 | tf_op jit(solution)/shard_map/parts_over_mp/all_to_all | solution.py:310
  116.7 1.6 copy-start.7
  122.4 20.2 %collective-permute-start.11 = (bf16[512,256]{1,0:T(8,128)(2,1)S(1)}, bf16[512,256]{1,0:T(8,128)(2,1)S(1)}, u32[]{:S(2)}, u32[]{:S(2)}) collective-permute-start(bf16[512,256]{1,0:T(8,128)(2,1)S(1)} %get-tuple-element.56), channel_id=1, source_target_pairs={{0,4},{1,5},{2,6},{3,7},{4,0},{5,1},{6,2},{7,3},{8,12},{9,13},{10,... | collective-permute-start | bytes 786440 | tf_op jit(solution)/shard_map/pooling/ppermute | solution.py:271
  125.4 20.0 %collective-permute-start.12 = (bf16[512,256]{1,0:T(8,128)(2,1)S(1)}, bf16[512,256]{1,0:T(8,128)(2,1)S(1)}, u32[]{:S(2)}, u32[]{:S(2)}) collective-permute-start(bf16[512,256]{1,0:T(8,128)(2,1)S(1)} %get-tuple-element.57), channel_id=1, source_target_pairs={{0,5},{1,4},{2,7},{3,6},{4,1},{5,0},{6,3},{7,2},{8,13},{9,12},{10,... | collective-permute-start | bytes 786440 | tf_op jit(solution)/shard_map/pooling/ppermute | solution.py:271
  130.3 18.4 %collective-permute-start.13 = (bf16[512,256]{1,0:T(8,128)(2,1)S(1)}, bf16[512,256]{1,0:T(8,128)(2,1)S(1)}, u32[]{:S(2)}, u32[]{:S(2)}) collective-permute-start(bf16[512,256]{1,0:T(8,128)(2,1)S(1)} %get-tuple-element.58), channel_id=1, source_target_pairs={{0,6},{1,7},{2,4},{3,5},{4,2},{5,3},{6,0},{7,1},{8,14},{9,15},{10,... | collective-permute-start | bytes 786440 | tf_op jit(solution)/shard_map/pooling/ppermute | solution.py:271
  132.6 24.6 %copy-start.1 = (bf16[2,512,512]{2,1,0:T(8,128)(2,1)S(1)}, bf16[2,512,512]{2,1,0:T(8,128)(2,1)}, u32[]{:S(2)}) copy-start(bf16[2,512,512]{2,1,0:T(8,128)(2,1)} %refs_9_.1) | copy-start | bytes 3145732
  132.6 24.6 %copy-start.2 = (bf16[1,512,256]{2,1,0:T(8,128)(2,1)S(1)}, bf16[1,512,256]{2,1,0:T(8,128)(2,1)}, u32[]{:S(2)}) copy-start(bf16[1,512,256]{2,1,0:T(8,128)(2,1)} %param.18) | copy-start | bytes 786436
  132.7 24.6 %copy-start.6 = (f32[2,512]{1,0:T(2,128)S(1)}, f32[2,512]{1,0:T(2,128)}, u32[]{:S(2)}) copy-start(f32[2,512]{1,0:T(2,128)} %refs_10_.1) | copy-start | bytes 12292
  132.7 18.4 %collective-permute-start.14 = (bf16[512,256]{1,0:T(8,128)(2,1)S(1)}, bf16[512,256]{1,0:T(8,128)(2,1)S(1)}, u32[]{:S(2)}, u32[]{:S(2)}) collective-permute-start(bf16[512,256]{1,0:T(8,128)(2,1)S(1)} %get-tuple-element.59), channel_id=1, source_target_pairs={{0,7},{1,6},{2,5},{3,4},{4,3},{5,2},{6,1},{7,0},{8,15},{9,14},{10,... | collective-permute-start | bytes 786440 | tf_op jit(solution)/shard_map/pooling/ppermute | solution.py:271
  140.7 10.7 %collective-permute-start.10 = (bf16[512,256]{1,0:T(8,128)(2,1)S(1)}, bf16[512,256]{1,0:T(8,128)(2,1)S(1)}, u32[]{:S(2)}, u32[]{:S(2)}) collective-permute-start(bf16[512,256]{1,0:T(8,128)(2,1)S(1)} %get-tuple-element.55), channel_id=1, source_target_pairs={{0,3},{1,2},{2,1},{3,0},{4,7},{5,6},{6,5},{7,4},{8,11},{9,10},{10,... | collective-permute-start | bytes 786440 | tf_op jit(solution)/shard_map/pooling/ppermute | solution.py:271
  142.6 8.8 %collective-permute-start.8 = (bf16[512,256]{1,0:T(8,128)(2,1)S(1)}, bf16[512,256]{1,0:T(8,128)(2,1)S(1)}, u32[]{:S(2)}, u32[]{:S(2)}) collective-permute-start(bf16[512,256]{1,0:T(8,128)(2,1)S(1)} %get-tuple-element.53), channel_id=1, source_target_pairs={{0,1},{1,0},{2,3},{3,2},{4,5},{5,4},{6,7},{7,6},{8,9},{9,8},{10,11... | collective-permute-start | bytes 786440 | tf_op jit(solution)/shard_map/pooling/ppermute | solution.py:271
  145.4 11.8 %collective-permute-start.9 = (bf16[512,256]{1,0:T(8,128)(2,1)S(1)}, bf16[512,256]{1,0:T(8,128)(2,1)S(1)}, u32[]{:S(2)}, u32[]{:S(2)}) collective-permute-start(bf16[512,256]{1,0:T(8,128)(2,1)S(1)} %get-tuple-element.54), channel_id=1, source_target_pairs={{0,2},{1,3},{2,0},{3,1},{4,6},{5,7},{6,4},{7,5},{8,10},{9,11},{10,... | collective-permute-start | bytes 786440 | tf_op jit(solution)/shard_map/pooling/ppermute | solution.py:271
  159.9 24.7 %copy-start.9 = (f32[512]{0:T(512)S(1)}, f32[512]{0:T(512)}, u32[]{:S(2)}) copy-start(f32[512]{0:T(512)} %param.13) | copy-start | bytes 6148
  159.9 25.3 %copy-start.8 = (f32[512,256]{1,0:T(8,128)S(1)}, f32[512,256]{1,0:T(8,128)}, u32[]{:S(2)}) copy-start(f32[512,256]{1,0:T(8,128)} %param.12) | copy-start | bytes 1572868
Sparse Core Ops, SparseCore 0:
  46.3 50.6 all-gather.3

commit v4 on v3

v4 whole, which is shorter than its diff:
```python
import jax
import jax.numpy as jnp
from jax import lax
from jax.experimental import pallas as pl
from jax.experimental.pallas import tpu as pltpu
from jax.sharding import PartitionSpec as P

VMEM_LIMIT = 48 * 1024 * 1024
learn_rate = 0.3
BAG_ROWS = 16
SAMPLES = 512


def adagrad(gradient, old_accum, old_table):
    fresh_accum = old_accum + jnp.mean(gradient * gradient, axis=1)
    fresh_table = old_table - learn_rate * gradient / jnp.sqrt(fresh_accum)[:, None]
    return (fresh_table, fresh_accum)


def pack(place, blocks, grads, owners, numbers, entries, weights, targets, parts, columns, block_count):
    count, rows, width = grads.shape
    part = rows // parts
    span = 96
    per_tile, owner_count = blocks.shape
    lanes = entries.shape[1] // owner_count
    side = width // lanes

    def kernel(
        place_ref, blocks_ref, grads_ref, owners_ref, numbers_ref, entries_ref, weights_ref, targets_ref, out_ref, row_ref
    ):
        def cut(n, carry):
            for j in range(parts):
                out_ref[j, n] = grads_ref[n, pl.ds(j * part, part), :]
            return carry

        lax.fori_loop(0, count, cut, 0)
        row_ref[...] = jnp.zeros_like(row_ref)
        row_ref[0:1, 0:count] = (owners_ref[...] * block_count + numbers_ref[...]).astype(jnp.float32)
        slots = row_ref[...].astype(out_ref.dtype)
        shift = lax.broadcasted_iota(jnp.int32, (entries_ref.shape[0], lanes), 0) * span
        lane = lax.broadcasted_iota(jnp.int32, (1, lanes), 1)

        def bags(j, carry):
            out_ref[j, count] = slots
            z = lax.rem(j - place_ref[1] + parts, parts)
            for p in range(columns):
                d = z * columns + (place_ref[2] ^ p)
                at = pl.ds(pl.multiple_of(d * lanes, lanes), lanes)
                chosen = jnp.zeros((1, lanes), jnp.int32)
                for b in range(per_tile):
                    chosen = jnp.where(lane == b, blocks_ref[b, d], chosen)
                bag = jnp.concatenate(
                    [
                        (entries_ref[:, at] - shift).astype(jnp.float32),
                        weights_ref[:, at],
                        (targets_ref[:, at] - 256).astype(jnp.float32),
                        chosen.astype(jnp.float32),
                        jnp.zeros((BAG_ROWS - 10, lanes), jnp.float32),
                    ],
                    axis=0,
                )
                out_ref[j, count + 1 + p // side, :, pl.ds(p % side * lanes, lanes)] = bag.astype(out_ref.dtype)
            return carry

        lax.fori_loop(0, parts, bags, 0)

    whole = pl.BlockSpec(memory_space=pltpu.VMEM)
    scalars = pl.BlockSpec(memory_space=pltpu.SMEM)
    return pl.pallas_call(
        kernel,
        out_shape=jax.ShapeDtypeStruct((parts, count + 1 + columns // side, part, width), grads.dtype),
        in_specs=[scalars] * 2 + [whole] * 6,
        out_specs=whole,
        scratch_shapes=[pltpu.VMEM((part, width), jnp.float32)],
        compiler_params=pltpu.CompilerParams(vmem_limit_bytes=VMEM_LIMIT),
        cost_estimate=pl.CostEstimate(flops=0, bytes_accessed=2 * grads.size * 2, transcendentals=0),
        name="pack",
    )(place, blocks, grads, owners, numbers, entries, weights, targets)


def split_bags(bags, columns):
    parts, blocks, part, width = bags.shape
    side = columns // blocks
    lanes = width // side

    def kernel(bags_ref, *out_refs):
        for p in range(columns):
            out_refs[p][...] = bags_ref[:, p // side, :, pl.ds(p % side * lanes, lanes)]

    whole = pl.BlockSpec(memory_space=pltpu.VMEM)
    return pl.pallas_call(
        kernel,
        out_shape=[jax.ShapeDtypeStruct((parts, part, lanes), bags.dtype)] * columns,
        in_specs=[whole],
        out_specs=[whole] * columns,
        cost_estimate=pl.CostEstimate(flops=0, bytes_accessed=512 * 1024, transcendentals=0),
        name="split_bags",
    )(bags)


def add_blocks(arrived, count, owner_count, block_count):
    parts, _, part, width = arrived.shape
    lanes = 128

    def kernel(recv_ref, out_ref, acc_ref, numbers_ref, slots_ref, sem):
        for k in range(parts):
            numbers_ref[pl.ds(k, 1), :] = (
                recv_ref[k, count, :, pl.ds(0, lanes)].astype(jnp.float32)[0:1].astype(jnp.int32)
            )
        copy = pltpu.make_async_copy(numbers_ref, slots_ref, sem)
        copy.start()
        acc_ref[...] = jnp.zeros_like(acc_ref)
        copy.wait()

        def add(n, carry):
            for k in range(parts):
                slot = slots_ref[k, n]
                acc_ref[slot] = acc_ref[slot] + recv_ref[k, n].astype(jnp.float32)
            return carry

        lax.fori_loop(0, count, add, 0)

        def place(o, carry):
            for b in range(block_count):
                out_ref[o, pl.ds(b * part, part), :] = acc_ref[o * block_count + b].astype(out_ref.dtype)
            return carry

        lax.fori_loop(0, owner_count, place, 0)

    whole = pl.BlockSpec(memory_space=pltpu.VMEM)
    return pl.pallas_call(
        kernel,
        out_shape=jax.ShapeDtypeStruct((owner_count, block_count * part, width), jnp.bfloat16),
        in_specs=[whole],
        out_specs=whole,
        scratch_shapes=[
            pltpu.VMEM((owner_count * block_count, part, width), jnp.float32),
            pltpu.VMEM((parts, lanes), jnp.int32),
            pltpu.SMEM((parts, lanes), jnp.int32),
            pltpu.SemaphoreType.DMA(()),
        ],
        compiler_params=pltpu.CompilerParams(vmem_limit_bytes=VMEM_LIMIT),
        cost_estimate=pl.CostEstimate(flops=0, bytes_accessed=10 * 1024 * 1024, transcendentals=0),
        name="add_blocks",
    )(arrived)


def pool_parts(first, many, place, table, bags):
    owner_count, block_count, width, lanes = table.shape
    parts = bags[0].shape[0]
    per_tile = 3
    entry_count = 4
    span = per_tile * lanes // entry_count
    samples = SAMPLES

    def kernel(place_ref, table_ref, *refs):
        bag_refs, out_refs = refs[:owner_count], refs[owner_count : owner_count + many]
        numbers_ref, blocks_ref, sem = refs[owner_count + many :]
        step = pl.program_id(0)
        replica = place_ref[0] ^ (step + first)

        @pl.when(step == 0)
        def _():
            for p in range(owner_count):
                for r in range(parts):
                    numbers_ref[pl.ds(p * parts + r, 1), :] = (
                        bag_refs[p][r].astype(jnp.float32)[2 * entry_count + 1 : 2 * entry_count + 2].astype(jnp.int32)
                    )
            copy = pltpu.make_async_copy(numbers_ref, blocks_ref, sem)
            copy.start()
            copy.wait()

        position = lax.broadcasted_iota(jnp.int32, (span, lanes), 0)
        sample = lax.broadcasted_iota(jnp.int32, (samples, owner_count * lanes), 0)
        partials, targets = [], []
        for p in range(owner_count):
            bag = bag_refs[p][replica].astype(jnp.float32)
            entries = bag[0:entry_count].astype(jnp.int32)
            weights = bag[entry_count : 2 * entry_count]
            targets.append(bag[2 * entry_count : 2 * entry_count + 1].astype(jnp.int32) + 256)
            incidence = jnp.concatenate(
                [
                    jnp.where(position == entries[l : l + 1], weights[l : l + 1], 0.0)
                    for l in range(entry_count)
                ],
                axis=0,
            ).astype(jnp.bfloat16)
            owner = place_ref[2] ^ p
            chosen = [blocks_ref[p * parts + replica, j] for j in range(per_tile)]
            slab = jnp.concatenate([table_ref[owner, b] for b in chosen], axis=1)
            partials.append(
                jnp.dot(slab, incidence, preferred_element_type=jnp.float32).astype(jnp.bfloat16)
            )
        selector = jnp.where(sample == jnp.concatenate(targets, axis=1), 1.0, 0.0).astype(jnp.bfloat16)
        pooled = lax.dot_general(
            selector,
            jnp.concatenate(partials, axis=1),
            (((1,), (1,)), ((), ())),
            preferred_element_type=jnp.float32,
        ).astype(jnp.bfloat16)
        for i in range(many):

            @pl.when(step == i)
            def _(i=i):
                out_refs[i][...] = pooled

    whole = pl.BlockSpec(memory_space=pltpu.VMEM)
    return pl.pallas_call(
        kernel,
        out_shape=[jax.ShapeDtypeStruct((samples, width), jnp.bfloat16)] * many,
        grid=(many,),
        in_specs=[pl.BlockSpec(memory_space=pltpu.SMEM), whole] + [whole] * owner_count,
        out_specs=[whole] * many,
        scratch_shapes=[
            pltpu.VMEM((owner_count * parts, lanes), jnp.int32),
            pltpu.SMEM((owner_count * parts, lanes), jnp.int32),
            pltpu.SemaphoreType.DMA(()),
        ],
        compiler_params=pltpu.CompilerParams(
            dimension_semantics=("arbitrary",), vmem_limit_bytes=VMEM_LIMIT
        ),
        cost_estimate=pl.CostEstimate(
            flops=many * 1_000_000_000, bytes_accessed=5 * 1024 * 1024, transcendentals=0
        ),
        name="pool_parts",
    )(place, table, *bags)


def cross_layers(pooled_parts, other_feats, cross_w, cross_b):
    parts = len(pooled_parts)
    samples, width = pooled_parts[0].shape
    layers, full, _ = cross_w.shape
    tile = 128

    def kernel(*refs):
        feats_ref, w_ref, b_ref, out_ref = refs[parts:]
        pooled = refs[0][...].astype(jnp.float32)
        for j in range(1, parts):
            pooled = pooled + refs[j][...].astype(jnp.float32)
        first = jnp.concatenate([pooled, feats_ref[...].astype(jnp.float32)], axis=1)
        crossed = first
        for layer in range(layers):
            mixing = (
                jnp.dot(crossed.astype(jnp.bfloat16), w_ref[layer], preferred_element_type=jnp.float32)
                + b_ref[layer : layer + 1, :]
            )
            crossed = first * mixing + crossed
        out_ref[...] = crossed.astype(out_ref.dtype)

    return pl.pallas_call(
        kernel,
        out_shape=jax.ShapeDtypeStruct((samples, full), jnp.bfloat16),
        grid=(samples // tile,),
        in_specs=[
            *[pl.BlockSpec((tile, width), lambda i: (i, 0))] * parts,
            pl.BlockSpec((tile, full - width), lambda i: (i, 0)),
            pl.BlockSpec((layers, full, full), lambda i: (0, 0, 0)),
            pl.BlockSpec((layers, full), lambda i: (0, 0)),
        ],
        out_specs=pl.BlockSpec((tile, full), lambda i: (i, 0)),
        compiler_params=pltpu.CompilerParams(
            dimension_semantics=("arbitrary",), vmem_limit_bytes=VMEM_LIMIT
        ),
        cost_estimate=pl.CostEstimate(
            flops=2 * layers * samples * full * full, bytes_accessed=5 * 1024 * 1024, transcendentals=0
        ),
        name="cross_layers",
    )(*pooled_parts, other_feats, cross_w, cross_b)


def local(
    table,
    accum,
    bag_blocks,
    bag_entries,
    bag_weights,
    bag_target,
    other_feats,
    cross_w,
    cross_b,
    evict_grads,
    evict_owner,
    evict_block,
):
    owner_count = lax.axis_size("mp")
    parts = lax.axis_size("replica")
    count, block_rows, width = evict_grads.shape[1:]
    slab_rows = table.shape[0]
    block_count = slab_rows // block_rows
    part = block_rows // parts
    columns = owner_count // parts
    position = lax.axis_index("mp")
    place = jnp.stack([lax.axis_index("replica"), position // columns, position % columns]).astype(jnp.int32)
    along_z = [
        ((z * columns + y) * parts + r, ((r - z) % parts * columns + y) * parts + r)
        for z in range(parts)
        for y in range(columns)
        for r in range(parts)
    ]
    rows_of_z = [[z * columns + y for y in range(columns)] for z in range(parts)]

    def to_replica(arrays, first):
        return [
            lax.ppermute(array, "replica", [(r, r ^ k) for r in range(parts)]) if k else array
            for k, array in enumerate(arrays, first)
        ]

    def to_column(arrays):
        return [
            lax.ppermute(array, "mp", [(row[y], row[y ^ k]) for row in rows_of_z for y in range(columns)])
            if k
            else array
            for k, array in enumerate(arrays)
        ]

    with jax.named_scope("packing"):
        slab = table.astype(jnp.bfloat16).reshape(block_count, block_rows, width).transpose(0, 2, 1)
        sent = pack(
            place,
            bag_blocks[0].T,
            evict_grads[0],
            evict_owner[:, :, 0],
            evict_block,
            bag_entries[0].T,
            bag_weights[0].T,
            bag_target,
            parts,
            columns,
            block_count,
        )
        sent, slab = lax.optimization_barrier((sent, slab))

    with jax.named_scope("table_gather"):
        moved = lax.ppermute(slab, ("mp", "replica"), along_z)
        slabs = lax.all_gather(moved, "mp", axis=0, axis_index_groups=rows_of_z)

    with jax.named_scope("over_replica"):
        arrived = lax.all_to_all(sent, "replica", split_axis=0, concat_axis=0, tiled=True)

    with jax.named_scope("parts_over_mp"):
        payload = add_blocks(arrived, count, owner_count, block_count)
        received = lax.all_to_all(payload, "mp", split_axis=0, concat_axis=0, tiled=True)

    with jax.named_scope("bags_over_mp"):
        bags = lax.ppermute(arrived[:, count + 1 :], ("mp", "replica"), along_z)
        bags, _ = lax.optimization_barrier((bags, payload))
        bags = to_column(split_bags(bags, columns))

    with jax.named_scope("pooling"):
        pooled = []
        for first in range(0, parts, parts // 2):
            pooled += to_replica(pool_parts(first, parts // 2, place, slabs, bags), first)

    with jax.named_scope("table_update"):
        grad_part = jnp.sum(received.astype(jnp.float32), axis=0).astype(jnp.bfloat16)
        grads = lax.all_gather(grad_part, "replica", axis=0)
        table_grad = (
            grads.reshape(parts, block_count, part, width)
            .transpose(1, 0, 2, 3)
            .reshape(slab_rows, width)
            .astype(jnp.float32)
        )
        new_table, new_accum = adagrad(table_grad, accum, table)

    with jax.named_scope("cross"):
        cross_out = cross_layers(pooled, other_feats[0], cross_w, cross_b)
    return (cross_out[None], new_table, new_accum)


def solution(mesh):
    in_specs = (
        P("mp", None),
        P("mp"),
        P("replica", "mp", None),
        P("replica", "mp", None),
        P("replica", "mp", None),
        P("replica", "mp"),
        P("replica", "mp", None),
        P(),
        P(),
        P("replica", "mp", None, None),
        P("replica", "mp", None),
        P("replica", "mp"),
    )
    out_specs = (P("replica", "mp", None), P("mp", None), P("mp"))
    return jax.shard_map(local, mesh=mesh, in_specs=in_specs, out_specs=out_specs, check_vma=False)
```

time: 194 us -> 244 us (1.26)
  waiting for transfers between devices: 37.9 us -> 98.3 us
  starting transfers between devices: 95.2 us -> 80.7 us
  local copies, waits for them, and re-layouts: 5.38 us -> 13.3 us
  blocking collectives: 16.6 us -> 13.1 us
    ppermute x1 -> x9, waiting for transfers between devices: 2.38 us -> 60.7 us  [the longest x1 51.4 us: local(): bags = lax.ppermute(arrived[:, count + 1:], ('mp', 'replica'), along_z)]
    ppermute x14 -> x7, starting transfers between devices: 60.3 us -> 24.6 us  [to_replica(): lax.ppermute(array, 'replica', [(r, r ^ k) for r in range(parts)])]
    ppermute x1 -> x9, starting transfers between devices: 3.97 us -> 33.8 us  [the longest x7 29 us: to_column(): lax.ppermute(array, 'mp', [(row[y], row[y ^ k]) for row in rows_of_z for...]
    all_to_all x2 -> x1, waiting for transfers between devices: 0.01 us -> 27.2 us  [local(): lax.all_to_all(sent, 'replica', split_axis=0, concat_axis=0, tiled=True)]
    ppermute x14 -> x7, waiting for transfers between devices: 29.6 us -> 10.3 us  [to_replica(): lax.ppermute(array, 'replica', [(r, r ^ k) for r in range(parts)])]
    all_to_all x2 -> x1, starting transfers between devices: 20.8 us -> 10.4 us  [local(): lax.all_to_all(sent, 'replica', split_axis=0, concat_axis=0, tiled=True)]
    unnamed x21 -> x33, local copies, waits for them, and re-layouts: 4.18 us -> 12.3 us
    all_to_all x1, waiting for transfers between devices: 5.87 us -> 0.01 us  [local(): lax.all_to_all(payload, 'mp', split_axis=0, concat_axis=0, tiled=True)]
  transfers between devices with their start and end apart: 19 -> 19, of which waited for: 8 -> 7; matrix products, arithmetic and copies ran while one was open for 1% -> 0% of each run, Pallas kernels for 8% -> 7%
where the time goes in v4:
time: 244 us; the launch traced here: 243 us
  waiting for transfers between devices  98.3 us (40%)
  starting transfers between devices  80.7 us (33%)
  Pallas kernels  18.8 us (8%)
  between operations  14.4 us (6%)
  local copies, waits for them, and re-layouts  13.3 us (5%)
  blocking collectives  13.1 us (5%)
  other arithmetic  4.78 us (2%)
    ppermute x1, waiting for transfers between devices, local(): bags = lax.ppermute(arrived[:, count + 1:], ('mp', 'replica'), along_z)  51.4 us
    ppermute x7, starting transfers between devices, to_column(): lax.ppermute(array, 'mp', [(row[y], row[y ^ k]) for row in rows_of_z for...  29 us
    all_to_all x1, waiting for transfers between devices, local(): lax.all_to_all(sent, 'replica', split_axis=0, concat_axis=0, tiled=True)  27.2 us
    ppermute x7, starting transfers between devices, to_replica(): lax.ppermute(array, 'replica', [(r, r ^ k) for r in range(parts)])  24.6 us
    all_gather x1, blocking collectives, local(): grads = lax.all_gather(grad_part, 'replica', axis=0)  13.1 us
    unnamed x33, local copies, waits for them, and re-layouts  12.3 us
    all_to_all x1, starting transfers between devices, local(): lax.all_to_all(payload, 'mp', split_axis=0, concat_axis=0, tiled=True)  11.9 us
    pallas_call x2, Pallas kernels, pool_parts(): pl.pallas_call(kernel, out_shape=[jax.ShapeDtypeStruct((samples, width),...  10.7 us
  transfers between devices with their start and end apart: 19, of which 7 were waited for; matrix products, arithmetic and copies ran while one was open for 0% of the time, Pallas kernels for 7%

profile of v4, /device:TPU:1, one launch (start us, length us, event | category | flops | bytes accessed | tf_op | source)
XLA Modules:
  0.0 243.4 jit_solution(13150921698597094974)
XLA Ops:
  9.0 1.7 copy-done.2
  17.5 10.4 %all-to-all-start = ((bf16[8,45,16,256]{3,2,1,0:T(8,128)(2,1)}), bf16[8,45,16,256]{3,2,1,0:T(8,128)(2,1)S(1)}, u32[]{:S(2)}, u32[]{:S(2)}) async-start(bf16[8,45,16,256]{3,2,1,0:T(8,128)(2,1)} %copy-done), calls=%async_computation | async-start | bytes 5898240 | tf_op jit(solution)/shard_map/over_replica/all_to_all | solution.py:338
  27.9 1.9 collective-permute-start
  29.8 5.5 %collective-permute-done = bf16[4,256,128]{1,2,0:T(8,128)(2,1)S(1)} collective-permute-done((bf16[4,256,128]{1,2,0:T(8,128)(2,1)S(1)}, bf16[4,256,128]{1,2,0:T(8,128)(2,1)S(1)}, u32[]{:S(2)}, u32[]{:S(2)}) %collective-permute-start) | collective-permute-done | bytes 262176 | tf_op jit(solution)/shard_map/table_gather/ppermute | solution.py:334
  36.1 27.2 %all-to-all-done.recv_ref = bf16[8,45,16,256]{3,2,1,0:T(8,128)(2,1)S(1)} async-done(((bf16[8,45,16,256]{3,2,1,0:T(8,128)(2,1)}), bf16[8,45,16,256]{3,2,1,0:T(8,128)(2,1)S(1)}, u32[]{:S(2)}, u32[]{:S(2)}) %all-to-all-start) | async-done | bytes 2949152 | tf_op jit(solution)/shard_map/over_replica/all_to_all | solution.py:338
  63.4 2.5 %add_blocks.1 = bf16[64,64,256]{2,1,0:T(8,128)(2,1)S(1)} custom-call(bf16[8,45,16,256]{3,2,1,0:T(8,128)(2,1)S(1)} %all-to-all-done.recv_ref), custom_call_target="tpu_custom_call" | custom-call | bytes 10485760 | tf_op jit(solution)/shard_map/parts_over_mp/add_blocks/pallas_call | solution.py:131
  67.2 11.9 %all-to-all-start.1 = ((bf16[64,64,256]{2,1,0:T(8,128)(2,1)}), bf16[64,64,256]{2,1,0:T(8,128)(2,1)}, u32[]{:S(2)}, u32[]{:S(2)}) async-start(bf16[64,64,256]{2,1,0:T(8,128)(2,1)} %copy-done.1), calls=%async_computation.1 | async-start | bytes 4194304 | tf_op jit(solution)/shard_map/parts_over_mp/all_to_all | solution.py:342
  79.2 2.8 %collective-permute-start.1 = (bf16[8,4,16,256]{3,2,1,0:T(8,128)(2,1)S(1)}, bf16[8,4,16,256]{3,2,1,0:T(8,128)(2,1)S(1)}, u32[]{:S(2)}, u32[]{:S(2)}) collective-permute-start(bf16[8,4,16,256]{3,2,1,0:T(8,128)(2,1)S(1)} %slice.4), channel_id=1, source_target_pairs={{0,0},{1,65},{2,130},{3,195},{4,260},{5,325},{6,390},{7,455},{8,8}... | collective-permute-start | bytes 786440 | tf_op jit(solution)/shard_map/bags_over_mp/ppermute | solution.py:345
  82.0 51.4 %collective-permute-done.1.bags_ref = bf16[8,4,16,256]{3,2,1,0:T(8,128)(2,1)S(1)} collective-permute-done((bf16[8,4,16,256]{3,2,1,0:T(8,128)(2,1)S(1)}, bf16[8,4,16,256]{3,2,1,0:T(8,128)(2,1)S(1)}, u32[]{:S(2)}, u32[]{:S(2)}) %collective-permute-start.1) | collective-permute-done | bytes 262176 | tf_op jit(solution)/shard_map/bags_over_mp/ppermute | solution.py:345
  134.1 1.7 split_bags.1
  135.8 3.6 %collective-permute-start.2 = (bf16[8,16,128]{2,1,0:T(8,128)(2,1)}, bf16[8,16,128]{2,1,0:T(8,128)(2,1)S(1)}, u32[]{:S(2)}, u32[]{:S(2)}) collective-permute-start(bf16[8,16,128]{2,1,0:T(8,128)(2,1)} %get-tuple-element.26), channel_id=1, source_target_pairs={{0,8},{8,0},{16,24},{24,16},{32,40},{40,32},{48,56},{56,48},{64,72... | collective-permute-start | bytes 98312 | tf_op jit(solution)/shard_map/bags_over_mp/ppermute | solution.py:310
  139.4 4.3 %collective-permute-start.3 = (bf16[8,16,128]{2,1,0:T(8,128)(2,1)}, bf16[8,16,128]{2,1,0:T(8,128)(2,1)S(1)}, u32[]{:S(2)}, u32[]{:S(2)}) collective-permute-start(bf16[8,16,128]{2,1,0:T(8,128)(2,1)} %get-tuple-element.27), channel_id=1, source_target_pairs={{0,16},{8,24},{16,0},{24,8},{32,48},{40,56},{48,32},{56,40},{64,80... | collective-permute-start | bytes 98312 | tf_op jit(solution)/shard_map/bags_over_mp/ppermute | solution.py:310
  143.7 2.4 collective-permute-start.4
  146.1 10.3 %collective-permute-start.5 = (bf16[8,16,128]{2,1,0:T(8,128)(2,1)}, bf16[8,16,128]{2,1,0:T(8,128)(2,1)S(1)}, u32[]{:S(2)}, u32[]{:S(2)}) collective-permute-start(bf16[8,16,128]{2,1,0:T(8,128)(2,1)} %get-tuple-element.29), channel_id=1, source_target_pairs={{0,32},{8,40},{16,48},{24,56},{32,0},{40,8},{48,16},{56,24},{64,96... | collective-permute-start | bytes 98312 | tf_op jit(solution)/shard_map/bags_over_mp/ppermute | solution.py:310
  156.5 1.9 collective-permute-start.6
  158.4 4.3 %collective-permute-start.7 = (bf16[8,16,128]{2,1,0:T(8,128)(2,1)}, bf16[8,16,128]{2,1,0:T(8,128)(2,1)S(1)}, u32[]{:S(2)}, u32[]{:S(2)}) collective-permute-start(bf16[8,16,128]{2,1,0:T(8,128)(2,1)} %get-tuple-element.31), channel_id=1, source_target_pairs={{0,48},{8,56},{16,32},{24,40},{32,16},{40,24},{48,0},{56,8},{64,11... | collective-permute-start | bytes 98312 | tf_op jit(solution)/shard_map/bags_over_mp/ppermute | solution.py:310
  162.7 2.2 collective-permute-start.8
  165.4 3.4 %collective-permute-done.8.refs_7_ = bf16[8,16,128]{2,1,0:T(8,128)(2,1)S(1)} collective-permute-done((bf16[8,16,128]{2,1,0:T(8,128)(2,1)}, bf16[8,16,128]{2,1,0:T(8,128)(2,1)S(1)}, u32[]{:S(2)}, u32[]{:S(2)}) %collective-permute-start.8) | collective-permute-done | bytes 32800 | tf_op jit(solution)/shard_map/bags_over_mp/ppermute | solution.py:310
  171.2 5.3 %pool_parts.3 = (bf16[512,256]{1,0:T(8,128)(2,1)S(1)}, bf16[512,256]{1,0:T(8,128)(2,1)S(1)}, bf16[512,256]{1,0:T(8,128)(2,1)S(1)}, bf16[512,256]{1,0:T(8,128)(2,1)S(1)}) custom-call(s32[3]{0:T(128)S(1)} %pad_add_fusion.place_ref, bf16[8,4,256,128]{3,2,1,0:T(8,128)(2,1)S(1)} %bitcast.36, bf16[8,16,128]{2,1,0:T(8,128)(2,1)S(1)} %copy-done.12, ...), custom_call_target="tpu_custom_call" | custom-call | flops 4000000000 | bytes 5242880 | tf_op jit(solution)/shard_map/pooling/pool_parts/pallas_call | solution.py:208
  176.5 1.9 collective-permute-start.12
  178.4 1.9 collective-permute-start.13
  180.3 10.3 %collective-permute-start.14 = (bf16[512,256]{1,0:T(8,128)(2,1)S(1)}, bf16[512,256]{1,0:T(8,128)(2,1)S(1)}, u32[]{:S(2)}, u32[]{:S(2)}) collective-permute-start(bf16[512,256]{1,0:T(8,128)(2,1)S(1)} %get-tuple-element.39), channel_id=1, source_target_pairs={{0,6},{1,7},{2,4},{3,5},{4,2},{5,3},{6,0},{7,1},{8,14},{9,15},{10,... | collective-permute-start | bytes 786440 | tf_op jit(solution)/shard_map/pooling/ppermute | solution.py:304
  190.7 2.3 collective-permute-start.15
  193.0 5.3 %pool_parts.2 = (bf16[512,256]{1,0:T(8,128)(2,1)S(1)}, bf16[512,256]{1,0:T(8,128)(2,1)S(1)}, bf16[512,256]{1,0:T(8,128)(2,1)S(1)}, bf16[512,256]{1,0:T(8,128)(2,1)S(1)}) custom-call(s32[3]{0:T(128)S(1)} %pad_add_fusion.place_ref, bf16[8,4,256,128]{3,2,1,0:T(8,128)(2,1)S(1)} %bitcast.37, bf16[8,16,128]{2,1,0:T(8,128)(2,1)S(1)} %copy-done.12, ...), custom_call_target="tpu_custom_call" | custom-call | flops 4000000000 | bytes 5242880 | tf_op jit(solution)/shard_map/pooling/pool_parts/pallas_call | solution.py:208
  198.4 2.3 collective-permute-start.9
  200.7 3.9 %collective-permute-start.10 = (bf16[512,256]{1,0:T(8,128)(2,1)S(1)}, bf16[512,256]{1,0:T(8,128)(2,1)S(1)}, u32[]{:S(2)}, u32[]{:S(2)}) collective-permute-start(bf16[512,256]{1,0:T(8,128)(2,1)S(1)} %get-tuple-element.35), channel_id=1, source_target_pairs={{0,2},{1,3},{2,0},{3,1},{4,6},{5,7},{6,4},{7,5},{8,10},{9,11},{10,... | collective-permute-start | bytes 786440 | tf_op jit(solution)/shard_map/pooling/ppermute | solution.py:304
  204.6 1.9 collective-permute-start.11
  206.6 4.7 %collective-permute-done.10.refs_2_ = bf16[512,256]{1,0:T(8,128)(2,1)S(1)} collective-permute-done((bf16[512,256]{1,0:T(8,128)(2,1)S(1)}, bf16[512,256]{1,0:T(8,128)(2,1)S(1)}, u32[]{:S(2)}, u32[]{:S(2)}) %collective-permute-start.10) | collective-permute-done | bytes 262176 | tf_op jit(solution)/shard_map/pooling/ppermute | solution.py:304
  211.3 5.6 %collective-permute-done.11.refs_3_ = bf16[512,256]{1,0:T(8,128)(2,1)S(1)} collective-permute-done((bf16[512,256]{1,0:T(8,128)(2,1)S(1)}, bf16[512,256]{1,0:T(8,128)(2,1)S(1)}, u32[]{:S(2)}, u32[]{:S(2)}) %collective-permute-start.11) | collective-permute-done | bytes 262176 | tf_op jit(solution)/shard_map/pooling/ppermute | solution.py:304
  216.9 2.7 %cross_layers.1 = bf16[512,512]{1,0:T(8,128)(2,1)} custom-call(bf16[512,256]{1,0:T(8,128)(2,1)S(1)} %get-tuple-element.33.refs_0_, bf16[512,256]{1,0:T(8,128)(2,1)S(1)} %collective-permute-done.9.refs_1_, bf16[512,256]{1,0:T(8,128)(2,1)S(1)} %collective-permute-done.10.refs_2_, bf16[512,256]{1,0:T(8,128)(2,1)S(1)} %collective-permute-done.11.refs_3_, ...), custom_call_target="tpu_custom_call" | custom-call | flops 536870912 | bytes 5242880 | tf_op jit(solution)/shard_map/cross/cross_layers/pallas_call | solution.py:250
  219.6 2.0 reduce_sum.23
  221.6 13.1 %all-gather.1 = bf16[512,256]{1,0:T(8,128)(2,1)S(1)} all-gather(bf16[64,256]{1,0:T(8,128)(2,1)S(1)} %reduce_sum.23), channel_id=3, replica_groups=mesh['mp'=64,'replica'=8] {'replica'}, dimensions={0}, use_global_device_ids=true | all-gather | bytes 294912 | tf_op jit(solution)/shard_map/table_update/all_gather | solution.py:356
  (60 shorter events, 16.1 us)
Async XLA Ops:
  9.0 1.7 copy-start.2
  10.8 0.9 copy-start.5
  11.7 0.9 copy-start.6
  12.6 0.8 copy-start.7
  15.9 1.6 copy-start
  17.5 45.9 %all-to-all-start = ((bf16[8,45,16,256]{3,2,1,0:T(8,128)(2,1)}), bf16[8,45,16,256]{3,2,1,0:T(8,128)(2,1)S(1)}, u32[]{:S(2)}, u32[]{:S(2)}) async-start(bf16[8,45,16,256]{3,2,1,0:T(8,128)(2,1)} %copy-done), calls=%async_computation | async-start | bytes 5898240 | tf_op jit(solution)/shard_map/over_replica/all_to_all | solution.py:338
  27.9 140.9 %all-gather.4.cloned.1.call-start = ((), (), s32[]{:S(2)}) async-start(), calls=%async_computation.2 | async-start | bytes 2359296 | tf_op jit(solution)/shard_map/table_gather/all_gather | solution.py:335
  27.9 7.4 %collective-permute-start = (bf16[4,256,128]{1,2,0:T(8,128)(2,1)S(1)}, bf16[4,256,128]{1,2,0:T(8,128)(2,1)S(1)}, u32[]{:S(2)}, u32[]{:S(2)}) collective-permute-start(bf16[4,256,128]{1,2,0:T(8,128)(2,1)S(1)} %bitcast.40), channel_id=1, source_target_pairs={{0,0},{1,65},{2,130},{3,195},{4,260},{5,325},{6,390},{7,455},{8,8}... | collective-permute-start | bytes 786440 | tf_op jit(solution)/shard_map/table_gather/ppermute | solution.py:334
  65.9 1.3 copy-start.1
  67.2 152.4 %all-to-all-start.1 = ((bf16[64,64,256]{2,1,0:T(8,128)(2,1)}), bf16[64,64,256]{2,1,0:T(8,128)(2,1)}, u32[]{:S(2)}, u32[]{:S(2)}) async-start(bf16[64,64,256]{2,1,0:T(8,128)(2,1)} %copy-done.1), calls=%async_computation.1 | async-start | bytes 4194304 | tf_op jit(solution)/shard_map/parts_over_mp/all_to_all | solution.py:342
  79.2 54.3 %collective-permute-start.1 = (bf16[8,4,16,256]{3,2,1,0:T(8,128)(2,1)S(1)}, bf16[8,4,16,256]{3,2,1,0:T(8,128)(2,1)S(1)}, u32[]{:S(2)}, u32[]{:S(2)}) collective-permute-start(bf16[8,4,16,256]{3,2,1,0:T(8,128)(2,1)S(1)} %slice.4), channel_id=1, source_target_pairs={{0,0},{1,65},{2,130},{3,195},{4,260},{5,325},{6,390},{7,455},{8,8}... | collective-permute-start | bytes 786440 | tf_op jit(solution)/shard_map/bags_over_mp/ppermute | solution.py:345
  135.8 22.6 %collective-permute-start.2 = (bf16[8,16,128]{2,1,0:T(8,128)(2,1)}, bf16[8,16,128]{2,1,0:T(8,128)(2,1)S(1)}, u32[]{:S(2)}, u32[]{:S(2)}) collective-permute-start(bf16[8,16,128]{2,1,0:T(8,128)(2,1)} %get-tuple-element.26), channel_id=1, source_target_pairs={{0,8},{8,0},{16,24},{24,16},{32,40},{40,32},{48,56},{56,48},{64,72... | collective-permute-start | bytes 98312 | tf_op jit(solution)/shard_map/bags_over_mp/ppermute | solution.py:310
  139.4 23.3 %collective-permute-start.3 = (bf16[8,16,128]{2,1,0:T(8,128)(2,1)}, bf16[8,16,128]{2,1,0:T(8,128)(2,1)S(1)}, u32[]{:S(2)}, u32[]{:S(2)}) collective-permute-start(bf16[8,16,128]{2,1,0:T(8,128)(2,1)} %get-tuple-element.27), channel_id=1, source_target_pairs={{0,16},{8,24},{16,0},{24,8},{32,48},{40,56},{48,32},{56,40},{64,80... | collective-permute-start | bytes 98312 | tf_op jit(solution)/shard_map/bags_over_mp/ppermute | solution.py:310
  143.7 21.2 %collective-permute-start.4 = (bf16[8,16,128]{2,1,0:T(8,128)(2,1)}, bf16[8,16,128]{2,1,0:T(8,128)(2,1)S(1)}, u32[]{:S(2)}, u32[]{:S(2)}) collective-permute-start(bf16[8,16,128]{2,1,0:T(8,128)(2,1)} %get-tuple-element.28), channel_id=1, source_target_pairs={{0,24},{8,16},{16,8},{24,0},{32,56},{40,48},{48,40},{56,32},{64,88... | collective-permute-start | bytes 98312 | tf_op jit(solution)/shard_map/bags_over_mp/ppermute | solution.py:310
  146.1 18.8 %collective-permute-start.5 = (bf16[8,16,128]{2,1,0:T(8,128)(2,1)}, bf16[8,16,128]{2,1,0:T(8,128)(2,1)S(1)}, u32[]{:S(2)}, u32[]{:S(2)}) collective-permute-start(bf16[8,16,128]{2,1,0:T(8,128)(2,1)} %get-tuple-element.29), channel_id=1, source_target_pairs={{0,32},{8,40},{16,48},{24,56},{32,0},{40,8},{48,16},{56,24},{64,96... | collective-permute-start | bytes 98312 | tf_op jit(solution)/shard_map/bags_over_mp/ppermute | solution.py:310
  156.5 8.5 %collective-permute-start.6 = (bf16[8,16,128]{2,1,0:T(8,128)(2,1)}, bf16[8,16,128]{2,1,0:T(8,128)(2,1)S(1)}, u32[]{:S(2)}, u32[]{:S(2)}) collective-permute-start(bf16[8,16,128]{2,1,0:T(8,128)(2,1)} %get-tuple-element.30), channel_id=1, source_target_pairs={{0,40},{8,32},{16,56},{24,48},{32,8},{40,0},{48,24},{56,16},{64,10... | collective-permute-start | bytes 98312 | tf_op jit(solution)/shard_map/bags_over_mp/ppermute | solution.py:310
  158.4 7.0 %collective-permute-start.7 = (bf16[8,16,128]{2,1,0:T(8,128)(2,1)}, bf16[8,16,128]{2,1,0:T(8,128)(2,1)S(1)}, u32[]{:S(2)}, u32[]{:S(2)}) collective-permute-start(bf16[8,16,128]{2,1,0:T(8,128)(2,1)} %get-tuple-element.31), channel_id=1, source_target_pairs={{0,48},{8,56},{16,32},{24,40},{32,16},{40,24},{48,0},{56,8},{64,11... | collective-permute-start | bytes 98312 | tf_op jit(solution)/shard_map/bags_over_mp/ppermute | solution.py:310
  162.7 6.1 %collective-permute-start.8 = (bf16[8,16,128]{2,1,0:T(8,128)(2,1)}, bf16[8,16,128]{2,1,0:T(8,128)(2,1)S(1)}, u32[]{:S(2)}, u32[]{:S(2)}) collective-permute-start(bf16[8,16,128]{2,1,0:T(8,128)(2,1)} %get-tuple-element.32), channel_id=1, source_target_pairs={{0,56},{8,48},{16,40},{24,32},{32,24},{40,16},{48,8},{56,0},{64,12... | collective-permute-start | bytes 98312 | tf_op jit(solution)/shard_map/bags_over_mp/ppermute | solution.py:310
  168.8 1.6 copy-start.11
  170.4 0.8 copy-start.12
  176.5 24.2 %collective-permute-start.12 = (bf16[512,256]{1,0:T(8,128)(2,1)S(1)}, bf16[512,256]{1,0:T(8,128)(2,1)S(1)}, u32[]{:S(2)}, u32[]{:S(2)}) collective-permute-start(bf16[512,256]{1,0:T(8,128)(2,1)S(1)} %get-tuple-element.37), channel_id=1, source_target_pairs={{0,4},{1,5},{2,6},{3,7},{4,0},{5,1},{6,2},{7,3},{8,12},{9,13},{10,... | collective-permute-start | bytes 786440 | tf_op jit(solution)/shard_map/pooling/ppermute | solution.py:304
  178.4 26.2 %collective-permute-start.13 = (bf16[512,256]{1,0:T(8,128)(2,1)S(1)}, bf16[512,256]{1,0:T(8,128)(2,1)S(1)}, u32[]{:S(2)}, u32[]{:S(2)}) collective-permute-start(bf16[512,256]{1,0:T(8,128)(2,1)S(1)} %get-tuple-element.38), channel_id=1, source_target_pairs={{0,5},{1,4},{2,7},{3,6},{4,1},{5,0},{6,3},{7,2},{8,13},{9,12},{10,... | collective-permute-start | bytes 786440 | tf_op jit(solution)/shard_map/pooling/ppermute | solution.py:304
  180.3 26.2 %collective-permute-start.14 = (bf16[512,256]{1,0:T(8,128)(2,1)S(1)}, bf16[512,256]{1,0:T(8,128)(2,1)S(1)}, u32[]{:S(2)}, u32[]{:S(2)}) collective-permute-start(bf16[512,256]{1,0:T(8,128)(2,1)S(1)} %get-tuple-element.39), channel_id=1, source_target_pairs={{0,6},{1,7},{2,4},{3,5},{4,2},{5,3},{6,0},{7,1},{8,14},{9,15},{10,... | collective-permute-start | bytes 786440 | tf_op jit(solution)/shard_map/pooling/ppermute | solution.py:304
  190.6 26.3 %copy-start.3 = (bf16[2,512,512]{2,1,0:T(8,128)(2,1)S(1)}, bf16[2,512,512]{2,1,0:T(8,128)(2,1)}, u32[]{:S(2)}) copy-start(bf16[2,512,512]{2,1,0:T(8,128)(2,1)} %refs_9_.1) | copy-start | bytes 3145732
  190.6 26.2 %copy-start.4 = (bf16[1,512,256]{2,1,0:T(8,128)(2,1)S(1)}, bf16[1,512,256]{2,1,0:T(8,128)(2,1)}, u32[]{:S(2)}) copy-start(bf16[1,512,256]{2,1,0:T(8,128)(2,1)} %param.18) | copy-start | bytes 786436
  190.7 26.2 %copy-start.8 = (f32[2,512]{1,0:T(2,128)S(1)}, f32[2,512]{1,0:T(2,128)}, u32[]{:S(2)}) copy-start(f32[2,512]{1,0:T(2,128)} %refs_10_.1) | copy-start | bytes 12292
  190.7 15.9 %collective-permute-start.15 = (bf16[512,256]{1,0:T(8,128)(2,1)S(1)}, bf16[512,256]{1,0:T(8,128)(2,1)S(1)}, u32[]{:S(2)}, u32[]{:S(2)}) collective-permute-start(bf16[512,256]{1,0:T(8,128)(2,1)S(1)} %get-tuple-element.40), channel_id=1, source_target_pairs={{0,7},{1,6},{2,5},{3,4},{4,3},{5,2},{6,1},{7,0},{8,15},{9,14},{10,... | collective-permute-start | bytes 786440 | tf_op jit(solution)/shard_map/pooling/ppermute | solution.py:304
  198.4 8.2 %collective-permute-start.9 = (bf16[512,256]{1,0:T(8,128)(2,1)S(1)}, bf16[512,256]{1,0:T(8,128)(2,1)S(1)}, u32[]{:S(2)}, u32[]{:S(2)}) collective-permute-start(bf16[512,256]{1,0:T(8,128)(2,1)S(1)} %get-tuple-element.34), channel_id=1, source_target_pairs={{0,1},{1,0},{2,3},{3,2},{4,5},{5,4},{6,7},{7,6},{8,9},{9,8},{10,11... | collective-permute-start | bytes 786440 | tf_op jit(solution)/shard_map/pooling/ppermute | solution.py:304
  200.7 10.6 %collective-permute-start.10 = (bf16[512,256]{1,0:T(8,128)(2,1)S(1)}, bf16[512,256]{1,0:T(8,128)(2,1)S(1)}, u32[]{:S(2)}, u32[]{:S(2)}) collective-permute-start(bf16[512,256]{1,0:T(8,128)(2,1)S(1)} %get-tuple-element.35), channel_id=1, source_target_pairs={{0,2},{1,3},{2,0},{3,1},{4,6},{5,7},{6,4},{7,5},{8,10},{9,11},{10,... | collective-permute-start | bytes 786440 | tf_op jit(solution)/shard_map/pooling/ppermute | solution.py:304
  204.6 12.3 %collective-permute-start.11 = (bf16[512,256]{1,0:T(8,128)(2,1)S(1)}, bf16[512,256]{1,0:T(8,128)(2,1)S(1)}, u32[]{:S(2)}, u32[]{:S(2)}) collective-permute-start(bf16[512,256]{1,0:T(8,128)(2,1)S(1)} %get-tuple-element.36), channel_id=1, source_target_pairs={{0,3},{1,2},{2,1},{3,0},{4,7},{5,6},{6,5},{7,4},{8,11},{9,10},{10,... | collective-permute-start | bytes 786440 | tf_op jit(solution)/shard_map/pooling/ppermute | solution.py:304
  219.6 15.4 %copy-start.15 = (f32[512]{0:T(512)S(1)}, f32[512]{0:T(512)}, u32[]{:S(2)}) copy-start(f32[512]{0:T(512)} %param.13) | copy-start | bytes 6148
  219.6 16.0 %copy-start.13 = (f32[512,256]{1,0:T(8,128)S(1)}, f32[512,256]{1,0:T(8,128)}, u32[]{:S(2)}) copy-start(f32[512,256]{1,0:T(8,128)} %param.12) | copy-start | bytes 1572868
  (3 other events, 2.0 us)
Sparse Core Ops, SparseCore 0:
  36.3 57.4 all-gather.3

commit v5 on v4

--- a/solution.py
+++ b/solution.py
@@ -17,17 +17,11 @@
     return (fresh_table, fresh_accum)
 
 
-def pack(place, blocks, grads, owners, numbers, entries, weights, targets, parts, columns, block_count):
+def pack_blocks(grads, owners, numbers, parts, block_count):
     count, rows, width = grads.shape
     part = rows // parts
-    span = 96
-    per_tile, owner_count = blocks.shape
-    lanes = entries.shape[1] // owner_count
-    side = width // lanes
-
-    def kernel(
-        place_ref, blocks_ref, grads_ref, owners_ref, numbers_ref, entries_ref, weights_ref, targets_ref, out_ref, row_ref
-    ):
+
+    def kernel(grads_ref, owners_ref, numbers_ref, out_ref, row_ref):
         def cut(n, carry):
             for j in range(parts):
                 out_ref[j, n] = grads_ref[n, pl.ds(j * part, part), :]
@@ -37,14 +31,36 @@
         row_ref[...] = jnp.zeros_like(row_ref)
         row_ref[0:1, 0:count] = (owners_ref[...] * block_count + numbers_ref[...]).astype(jnp.float32)
         slots = row_ref[...].astype(out_ref.dtype)
-        shift = lax.broadcasted_iota(jnp.int32, (entries_ref.shape[0], lanes), 0) * span
+        for j in range(parts):
+            out_ref[j, count] = slots
+
+    whole = pl.BlockSpec(memory_space=pltpu.VMEM)
+    return pl.pallas_call(
+        kernel,
+        out_shape=jax.ShapeDtypeStruct((parts, count + 1, part, width), grads.dtype),
+        in_specs=[whole] * 3,
+        out_specs=whole,
+        scratch_shapes=[pltpu.VMEM((part, width), jnp.float32)],
+        compiler_params=pltpu.CompilerParams(vmem_limit_bytes=VMEM_LIMIT),
+        cost_estimate=pl.CostEstimate(flops=0, bytes_accessed=2 * grads.size * 2, transcendentals=0),
+        name="pack_blocks",
+    )(grads, owners, numbers)
+
+
+def pack_bags(place, blocks, entries, weights, targets, columns):
+    per_tile, owner_count = blocks.shape
+    rows = owner_count // columns
+    lanes = entries.shape[1] // owner_count
+    entry_count = entries.shape[0]
+    span = per_tile * lanes // entry_count
+
+    def kernel(place_ref, blocks_ref, entries_ref, weights_ref, targets_ref, *out_refs):
+        shift = lax.broadcasted_iota(jnp.int32, (entry_count, lanes), 0) * span
         lane = lax.broadcasted_iota(jnp.int32, (1, lanes), 1)
 
-        def bags(j, carry):
-            out_ref[j, count] = slots
-            z = lax.rem(j - place_ref[1] + parts, parts)
+        def bags(q, carry):
             for p in range(columns):
-                d = z * columns + (place_ref[2] ^ p)
+                d = (place_ref[1] ^ q) * columns + (place_ref[2] ^ p)
                 at = pl.ds(pl.multiple_of(d * lanes, lanes), lanes)
                 chosen = jnp.zeros((1, lanes), jnp.int32)
                 for b in range(per_tile):
@@ -55,47 +71,47 @@
                         weights_ref[:, at],
                         (targets_ref[:, at] - 256).astype(jnp.float32),
                         chosen.astype(jnp.float32),
-                        jnp.zeros((BAG_ROWS - 10, lanes), jnp.float32),
+                        jnp.zeros((BAG_ROWS - 2 * entry_count - 2, lanes), jnp.float32),
                     ],
                     axis=0,
                 )
-                out_ref[j, count + 1 + p // side, :, pl.ds(p % side * lanes, lanes)] = bag.astype(out_ref.dtype)
+                out_refs[p][q] = bag.astype(jnp.bfloat16)
             return carry
 
-        lax.fori_loop(0, parts, bags, 0)
+        lax.fori_loop(0, rows, bags, 0)
 
     whole = pl.BlockSpec(memory_space=pltpu.VMEM)
     scalars = pl.BlockSpec(memory_space=pltpu.SMEM)
     return pl.pallas_call(
         kernel,
-        out_shape=jax.ShapeDtypeStruct((parts, count + 1 + columns // side, part, width), grads.dtype),
-        in_specs=[scalars] * 2 + [whole] * 6,
-        out_specs=whole,
-        scratch_shapes=[pltpu.VMEM((part, width), jnp.float32)],
+        out_shape=[jax.ShapeDtypeStruct((rows, BAG_ROWS, lanes), jnp.bfloat16)] * columns,
+        in_specs=[scalars] * 2 + [whole] * 3,
+        out_specs=[whole] * columns,
         compiler_params=pltpu.CompilerParams(vmem_limit_bytes=VMEM_LIMIT),
-        cost_estimate=pl.CostEstimate(flops=0, bytes_accessed=2 * grads.size * 2, transcendentals=0),
-        name="pack",
-    )(place, blocks, grads, owners, numbers, entries, weights, targets)
-
-
-def split_bags(bags, columns):
-    parts, blocks, part, width = bags.shape
-    side = columns // blocks
-    lanes = width // side
-
-    def kernel(bags_ref, *out_refs):
-        for p in range(columns):
-            out_refs[p][...] = bags_ref[:, p // side, :, pl.ds(p % side * lanes, lanes)]
-
-    whole = pl.BlockSpec(memory_space=pltpu.VMEM)
-    return pl.pallas_call(
-        kernel,
-        out_shape=[jax.ShapeDtypeStruct((parts, part, lanes), bags.dtype)] * columns,
-        in_specs=[whole],
-        out_specs=[whole] * columns,
+        cost_estimate=pl.CostEstimate(flops=0, bytes_accessed=1024 * 1024, transcendentals=0),
+        name="pack_bags",
+    )(place, blocks, entries, weights, targets)
+
+
+def turn_bags(place, bags):
+    columns = len(bags)
+    rows, part, lanes = bags[0].shape
+
+    def kernel(place_ref, *refs):
+        for k in range(rows):
+            for p in range(columns):
+                refs[columns + k][p] = refs[p][place_ref[0] ^ k]
+
+    whole = pl.BlockSpec(memory_space=pltpu.VMEM)
+    return pl.pallas_call(
+        kernel,
+        out_shape=[jax.ShapeDtypeStruct((columns, part, lanes), bags[0].dtype)] * rows,
+        in_specs=[pl.BlockSpec(memory_space=pltpu.SMEM)] + [whole] * columns,
+        out_specs=[whole] * rows,
+        compiler_params=pltpu.CompilerParams(vmem_limit_bytes=VMEM_LIMIT),
         cost_estimate=pl.CostEstimate(flops=0, bytes_accessed=512 * 1024, transcendentals=0),
-        name="split_bags",
-    )(bags)
+        name="turn_bags",
+    )(place, *bags)
 
 
 def add_blocks(arrived, count, owner_count, block_count):
@@ -145,26 +161,27 @@
     )(arrived)
 
 
-def pool_parts(first, many, place, table, bags):
+def pool_parts(place, table, bags):
     owner_count, block_count, width, lanes = table.shape
-    parts = bags[0].shape[0]
+    many = len(bags)
     per_tile = 3
     entry_count = 4
     span = per_tile * lanes // entry_count
     samples = SAMPLES
 
     def kernel(place_ref, table_ref, *refs):
-        bag_refs, out_refs = refs[:owner_count], refs[owner_count : owner_count + many]
-        numbers_ref, blocks_ref, sem = refs[owner_count + many :]
+        bag_refs, out_refs = refs[:many], refs[many : 2 * many]
+        bags_ref, numbers_ref, blocks_ref, sem = refs[2 * many :]
         step = pl.program_id(0)
-        replica = place_ref[0] ^ (step + first)
 
         @pl.when(step == 0)
         def _():
-            for p in range(owner_count):
-                for r in range(parts):
-                    numbers_ref[pl.ds(p * parts + r, 1), :] = (
-                        bag_refs[p][r].astype(jnp.float32)[2 * entry_count + 1 : 2 * entry_count + 2].astype(jnp.int32)
+            for i in range(many):
+                for p in range(owner_count):
+                    bag = bag_refs[i][p]
+                    bags_ref[i, p] = bag
+                    numbers_ref[pl.ds(i * owner_count + p, 1), :] = (
+                        bag.astype(jnp.float32)[2 * entry_count + 1 : 2 * entry_count + 2].astype(jnp.int32)
                     )
             copy = pltpu.make_async_copy(numbers_ref, blocks_ref, sem)
             copy.start()
@@ -174,7 +191,7 @@
         sample = lax.broadcasted_iota(jnp.int32, (samples, owner_count * lanes), 0)
         partials, targets = [], []
         for p in range(owner_count):
-            bag = bag_refs[p][replica].astype(jnp.float32)
+            bag = bags_ref[step, p].astype(jnp.float32)
             entries = bag[0:entry_count].astype(jnp.int32)
             weights = bag[entry_count : 2 * entry_count]
             targets.append(bag[2 * entry_count : 2 * entry_count + 1].astype(jnp.int32) + 256)
@@ -186,7 +203,7 @@
                 axis=0,
             ).astype(jnp.bfloat16)
             owner = place_ref[2] ^ p
-            chosen = [blocks_ref[p * parts + replica, j] for j in range(per_tile)]
+            chosen = [blocks_ref[step * owner_count + p, j] for j in range(per_tile)]
             slab = jnp.concatenate([table_ref[owner, b] for b in chosen], axis=1)
             partials.append(
                 jnp.dot(slab, incidence, preferred_element_type=jnp.float32).astype(jnp.bfloat16)
@@ -209,11 +226,12 @@
         kernel,
         out_shape=[jax.ShapeDtypeStruct((samples, width), jnp.bfloat16)] * many,
         grid=(many,),
-        in_specs=[pl.BlockSpec(memory_space=pltpu.SMEM), whole] + [whole] * owner_count,
+        in_specs=[pl.BlockSpec(memory_space=pltpu.SMEM), whole] + [whole] * many,
         out_specs=[whole] * many,
         scratch_shapes=[
-            pltpu.VMEM((owner_count * parts, lanes), jnp.int32),
-            pltpu.SMEM((owner_count * parts, lanes), jnp.int32),
+            pltpu.VMEM((many, owner_count, BAG_ROWS, lanes), jnp.bfloat16),
+            pltpu.VMEM((many * owner_count, lanes), jnp.int32),
+            pltpu.SMEM((many * owner_count, lanes), jnp.int32),
             pltpu.SemaphoreType.DMA(()),
         ],
         compiler_params=pltpu.CompilerParams(
@@ -291,12 +309,15 @@
     columns = owner_count // parts
     position = lax.axis_index("mp")
     place = jnp.stack([lax.axis_index("replica"), position // columns, position % columns]).astype(jnp.int32)
-    along_z = [
-        ((z * columns + y) * parts + r, ((r - z) % parts * columns + y) * parts + r)
-        for z in range(parts)
-        for y in range(columns)
-        for r in range(parts)
-    ]
+
+    def along_z(k):
+        return [
+            ((z * columns + y) * parts + r, ((z ^ r ^ k) * columns + y) * parts + r)
+            for z in range(parts)
+            for y in range(columns)
+            for r in range(parts)
+        ]
+
     rows_of_z = [[z * columns + y for y in range(columns)] for z in range(parts)]
 
     def to_replica(arrays, first):
@@ -313,43 +334,34 @@
             for k, array in enumerate(arrays)
         ]
 
+    with jax.named_scope("table_gather"):
+        slab = lax.optimization_barrier(table).astype(jnp.bfloat16)
+        slab = slab.reshape(block_count, block_rows, width).transpose(0, 2, 1)
+        moved = lax.ppermute(slab, ("mp", "replica"), along_z(0))
+        slabs = lax.all_gather(moved, "mp", axis=0, axis_index_groups=rows_of_z)
+
     with jax.named_scope("packing"):
-        slab = table.astype(jnp.bfloat16).reshape(block_count, block_rows, width).transpose(0, 2, 1)
-        sent = pack(
-            place,
-            bag_blocks[0].T,
-            evict_grads[0],
-            evict_owner[:, :, 0],
-            evict_block,
-            bag_entries[0].T,
-            bag_weights[0].T,
-            bag_target,
-            parts,
-            columns,
-            block_count,
-        )
-        sent, slab = lax.optimization_barrier((sent, slab))
-
-    with jax.named_scope("table_gather"):
-        moved = lax.ppermute(slab, ("mp", "replica"), along_z)
-        slabs = lax.all_gather(moved, "mp", axis=0, axis_index_groups=rows_of_z)
+        bags = pack_bags(place, bag_blocks[0].T, bag_entries[0].T, bag_weights[0].T, bag_target, columns)
+        sent = pack_blocks(evict_grads[0], evict_owner[:, :, 0], evict_block, parts, block_count)
+        sent, bags = lax.optimization_barrier((sent, bags))
+
+    with jax.named_scope("bags_over_mp"):
+        bags = turn_bags(place, to_column(bags))
+        bags = [lax.ppermute(bag, ("mp", "replica"), along_z(k)) for k, bag in enumerate(bags)]
 
     with jax.named_scope("over_replica"):
         arrived = lax.all_to_all(sent, "replica", split_axis=0, concat_axis=0, tiled=True)
 
     with jax.named_scope("parts_over_mp"):
         payload = add_blocks(arrived, count, owner_count, block_count)
+        payload, bags = lax.optimization_barrier((payload, bags))
         received = lax.all_to_all(payload, "mp", split_axis=0, concat_axis=0, tiled=True)
 
-    with jax.named_scope("bags_over_mp"):
-        bags = lax.ppermute(arrived[:, count + 1 :], ("mp", "replica"), along_z)
-        bags, _ = lax.optimization_barrier((bags, payload))
-        bags = to_column(split_bags(bags, columns))
-
     with jax.named_scope("pooling"):
+        bags = to_replica(bags, 0)
         pooled = []
         for first in range(0, parts, parts // 2):
-            pooled += to_replica(pool_parts(first, parts // 2, place, slabs, bags), first)
+            pooled += to_replica(pool_parts(place, slabs, bags[first : first + parts // 2]), first)
 
     with jax.named_scope("table_update"):
         grad_part = jnp.sum(received.astype(jnp.float32), axis=0).astype(jnp.bfloat16)

time: 244 us -> 211 us (0.86)
  waiting for transfers between devices: 98.3 us -> 16.4 us
  starting transfers between devices: 80.7 us -> 135 us
  local copies, waits for them, and re-layouts: 13.3 us -> 9.3 us
  other arithmetic: 4.78 us -> 2.09 us
    ppermute x2 -> x9, waiting for transfers between devices: 56.9 us -> 5.5 us  [the longest x1 5.48 us: local(): moved = lax.ppermute(slab, ('mp', 'replica'), along_z(0))]
    ppermute x7 -> x14, starting transfers between devices: 24.6 us -> 58.5 us  [to_replica(): lax.ppermute(array, 'replica', [(r, r ^ k) for r in range(parts)])]
    ppermute x2 -> x9, starting transfers between devices: 4.76 us -> 33.1 us  [the longest x8 31.2 us: local(): lax.ppermute(bag, ('mp', 'replica'), along_z(k))]
    all_to_all x1, waiting for transfers between devices: 27.2 us -> 0.01 us  [local(): lax.all_to_all(sent, 'replica', split_axis=0, concat_axis=0, tiled=True)]
    unnamed x33 -> x31, local copies, waits for them, and re-layouts: 12.3 us -> 7.3 us
    ppermute x7, starting transfers between devices: 29 us -> 25 us  [to_column(): lax.ppermute(array, 'mp', [(row[y], row[y ^ k]) for row in rows_of_z for...]
    all_to_all x1, starting transfers between devices: 11.9 us -> 8.27 us  [local(): lax.all_to_all(payload, 'mp', split_axis=0, concat_axis=0, tiled=True)]
    ppermute x7, waiting for transfers between devices: 3.86 us -> 1.26 us  [to_column(): lax.ppermute(array, 'mp', [(row[y], row[y ^ k]) for row in rows_of_z for...]
  transfers between devices with their start and end apart: 19 -> 33, of which waited for: 7 -> 5; matrix products, arithmetic and copies ran while one was open for 0% -> 1% of each run, Pallas kernels for 7% -> 8%
where the time goes in v5:
time: 211 us; the launch traced here: 209 us
  starting transfers between devices  135 us (64%)
  Pallas kernels  18.6 us (9%)
  waiting for transfers between devices  16.4 us (8%)
  between operations  14.6 us (7%)
  blocking collectives  12.9 us (6%)
  local copies, waits for them, and re-layouts  9.3 us (4%)
    ppermute x14, starting transfers between devices, to_replica(): lax.ppermute(array, 'replica', [(r, r ^ k) for r in range(parts)])  58.5 us
    ppermute x8, starting transfers between devices, local(): lax.ppermute(bag, ('mp', 'replica'), along_z(k))  31.2 us
    ppermute x7, starting transfers between devices, to_column(): lax.ppermute(array, 'mp', [(row[y], row[y ^ k]) for row in rows_of_z for...  25 us
    all_gather x1, blocking collectives, local(): grads = lax.all_gather(grad_part, 'replica', axis=0)  12.9 us
    all_to_all x1, starting transfers between devices, local(): lax.all_to_all(sent, 'replica', split_axis=0, concat_axis=0, tiled=True)  10.6 us
    pallas_call x2, Pallas kernels, pool_parts(): pl.pallas_call(kernel, out_shape=[jax.ShapeDtypeStruct((samples, width),...  10.1 us
    ppermute x14, waiting for transfers between devices, to_replica(): lax.ppermute(array, 'replica', [(r, r ^ k) for r in range(parts)])  9.59 us
    all_to_all x1, starting transfers between devices, local(): lax.all_to_all(payload, 'mp', split_axis=0, concat_axis=0, tiled=True)  8.27 us
  transfers between devices with their start and end apart: 33, of which 5 were waited for; matrix products, arithmetic and copies ran while one was open for 1% of the time, Pallas kernels for 8%

profile of v5, /device:TPU:1, one launch (start us, length us, event | category | flops | bytes accessed | tf_op | source)
XLA Modules:
  0.0 209.3 jit_solution(14991813254792563746)
XLA Ops:
  13.8 10.6 %all-to-all-start = ((bf16[8,41,16,256]{3,2,1,0:T(8,128)(2,1)}), bf16[8,41,16,256]{3,2,1,0:T(8,128)(2,1)S(1)}, u32[]{:S(2)}, u32[]{:S(2)}) async-start(bf16[8,41,16,256]{3,2,1,0:T(8,128)(2,1)} %pack_blocks.1), calls=%async_computation | async-start | bytes 5373952 | tf_op jit(solution)/shard_map/over_replica/all_to_all | solution.py:353
  24.4 1.9 collective-permute-start
  26.3 5.5 %collective-permute-done = bf16[4,256,128]{1,2,0:T(8,128)(2,1)} collective-permute-done((bf16[4,256,128]{1,2,0:T(8,128)(2,1)S(1)}, bf16[4,256,128]{1,2,0:T(8,128)(2,1)}, u32[]{:S(2)}, u32[]{:S(2)}) %collective-permute-start) | collective-permute-done | bytes 262176 | tf_op jit(solution)/shard_map/table_gather/ppermute | solution.py:340
  37.5 5.4 %collective-permute-start.3 = (bf16[8,16,128]{2,1,0:T(8,128)(2,1)S(1)}, bf16[8,16,128]{2,1,0:T(8,128)(2,1)S(1)}, u32[]{:S(2)}, u32[]{:S(2)}) collective-permute-start(bf16[8,16,128]{2,1,0:T(8,128)(2,1)S(1)} %get-tuple-element.57), channel_id=1, source_target_pairs={{0,24},{8,16},{16,8},{24,0},{32,56},{40,48},{48,40},{56,32},{64,88... | collective-permute-start | bytes 98312 | tf_op jit(solution)/shard_map/bags_over_mp/ppermute | solution.py:331
  42.9 3.5 %collective-permute-start.4 = (bf16[8,16,128]{2,1,0:T(8,128)(2,1)S(1)}, bf16[8,16,128]{2,1,0:T(8,128)(2,1)S(1)}, u32[]{:S(2)}, u32[]{:S(2)}) collective-permute-start(bf16[8,16,128]{2,1,0:T(8,128)(2,1)S(1)} %get-tuple-element.58), channel_id=1, source_target_pairs={{0,32},{8,40},{16,48},{24,56},{32,0},{40,8},{48,16},{56,24},{64,96... | collective-permute-start | bytes 98312 | tf_op jit(solution)/shard_map/bags_over_mp/ppermute | solution.py:331
  46.4 3.6 %collective-permute-start.5 = (bf16[8,16,128]{2,1,0:T(8,128)(2,1)S(1)}, bf16[8,16,128]{2,1,0:T(8,128)(2,1)S(1)}, u32[]{:S(2)}, u32[]{:S(2)}) collective-permute-start(bf16[8,16,128]{2,1,0:T(8,128)(2,1)S(1)} %get-tuple-element.59), channel_id=1, source_target_pairs={{0,40},{8,32},{16,56},{24,48},{32,8},{40,0},{48,24},{56,16},{64,10... | collective-permute-start | bytes 98312 | tf_op jit(solution)/shard_map/bags_over_mp/ppermute | solution.py:331
  50.0 3.2 %collective-permute-start.6 = (bf16[8,16,128]{2,1,0:T(8,128)(2,1)S(1)}, bf16[8,16,128]{2,1,0:T(8,128)(2,1)S(1)}, u32[]{:S(2)}, u32[]{:S(2)}) collective-permute-start(bf16[8,16,128]{2,1,0:T(8,128)(2,1)S(1)} %get-tuple-element.60), channel_id=1, source_target_pairs={{0,48},{8,56},{16,32},{24,40},{32,16},{40,24},{48,0},{56,8},{64,11... | collective-permute-start | bytes 98312 | tf_op jit(solution)/shard_map/bags_over_mp/ppermute | solution.py:331
  53.3 5.4 %collective-permute-start.7 = (bf16[8,16,128]{2,1,0:T(8,128)(2,1)S(1)}, bf16[8,16,128]{2,1,0:T(8,128)(2,1)S(1)}, u32[]{:S(2)}, u32[]{:S(2)}) collective-permute-start(bf16[8,16,128]{2,1,0:T(8,128)(2,1)S(1)} %get-tuple-element.61), channel_id=1, source_target_pairs={{0,56},{8,48},{16,40},{24,32},{32,24},{40,16},{48,8},{56,0},{64,12... | collective-permute-start | bytes 98312 | tf_op jit(solution)/shard_map/bags_over_mp/ppermute | solution.py:331
  60.5 6.2 %collective-permute-start.10 = (bf16[8,16,128]{2,1,0:T(8,128)(2,1)S(1)}, bf16[8,16,128]{2,1,0:T(8,128)(2,1)S(1)}, u32[]{:S(2)}, u32[]{:S(2)}) collective-permute-start(bf16[8,16,128]{2,1,0:T(8,128)(2,1)S(1)} %get-tuple-element.64), channel_id=1, source_target_pairs={{0,128},{1,193},{2,2},{3,67},{4,388},{5,453},{6,262},{7,327},{8,13... | collective-permute-start | bytes 98312 | tf_op jit(solution)/shard_map/bags_over_mp/ppermute | solution.py:350
  68.6 7.9 %collective-permute-start.12 = (bf16[8,16,128]{2,1,0:T(8,128)(2,1)S(1)}, bf16[8,16,128]{2,1,0:T(8,128)(2,1)S(1)}, u32[]{:S(2)}, u32[]{:S(2)}) collective-permute-start(bf16[8,16,128]{2,1,0:T(8,128)(2,1)S(1)} %get-tuple-element.66), channel_id=1, source_target_pairs={{0,256},{1,321},{2,386},{3,451},{4,4},{5,69},{6,134},{7,199},{8,26... | collective-permute-start | bytes 98312 | tf_op jit(solution)/shard_map/bags_over_mp/ppermute | solution.py:350
  76.6 2.8 %collective-permute-start.13 = (bf16[8,16,128]{2,1,0:T(8,128)(2,1)S(1)}, bf16[8,16,128]{2,1,0:T(8,128)(2,1)}, u32[]{:S(2)}, u32[]{:S(2)}) collective-permute-start(bf16[8,16,128]{2,1,0:T(8,128)(2,1)S(1)} %get-tuple-element.67), channel_id=1, source_target_pairs={{0,320},{1,257},{2,450},{3,387},{4,68},{5,5},{6,198},{7,135},{8,32... | collective-permute-start | bytes 98312 | tf_op jit(solution)/shard_map/bags_over_mp/ppermute | solution.py:350
  79.4 6.6 %collective-permute-start.14 = (bf16[8,16,128]{2,1,0:T(8,128)(2,1)S(1)}, bf16[8,16,128]{2,1,0:T(8,128)(2,1)S(1)}, u32[]{:S(2)}, u32[]{:S(2)}) collective-permute-start(bf16[8,16,128]{2,1,0:T(8,128)(2,1)S(1)} %get-tuple-element.68), channel_id=1, source_target_pairs={{0,384},{1,449},{2,258},{3,323},{4,132},{5,197},{6,6},{7,71},{8,39... | collective-permute-start | bytes 98312 | tf_op jit(solution)/shard_map/bags_over_mp/ppermute | solution.py:350
  86.1 1.9 collective-permute-start.15
  88.0 3.1 %collective-permute-start.8 = (bf16[8,16,128]{2,1,0:T(8,128)(2,1)S(1)}, bf16[8,16,128]{2,1,0:T(8,128)(2,1)S(1)}, u32[]{:S(2)}, u32[]{:S(2)}) collective-permute-start(bf16[8,16,128]{2,1,0:T(8,128)(2,1)S(1)} %get-tuple-element.62), channel_id=1, source_target_pairs={{0,0},{1,65},{2,130},{3,195},{4,260},{5,325},{6,390},{7,455},{8,8}... | collective-permute-start | bytes 98312 | tf_op jit(solution)/shard_map/bags_over_mp/ppermute | solution.py:350
  92.4 2.5 %add_blocks.1 = bf16[64,64,256]{2,1,0:T(8,128)(2,1)S(1)} custom-call(bf16[8,41,16,256]{3,2,1,0:T(8,128)(2,1)S(1)} %all-to-all-done.recv_ref), custom_call_target="tpu_custom_call" | custom-call | bytes 10485760 | tf_op jit(solution)/shard_map/parts_over_mp/add_blocks/pallas_call | solution.py:147
  96.3 8.3 %all-to-all-start.1 = ((bf16[64,64,256]{2,1,0:T(8,128)(2,1)}), bf16[64,64,256]{2,1,0:T(8,128)(2,1)S(1)}, u32[]{:S(2)}, u32[]{:S(2)}) async-start(bf16[64,64,256]{2,1,0:T(8,128)(2,1)} %copy-done), calls=%async_computation.1 | async-start | bytes 4194304 | tf_op jit(solution)/shard_map/parts_over_mp/all_to_all | solution.py:358
  104.6 16.8 %collective-permute-start.22 = (bf16[8,16,128]{2,1,0:T(8,128)(2,1)S(1)}, bf16[8,16,128]{2,1,0:T(8,128)(2,1)S(1)}, u32[]{:S(2)}, u32[]{:S(2)}) collective-permute-start(bf16[8,16,128]{2,1,0:T(8,128)(2,1)S(1)} %copy-done.14), channel_id=1, source_target_pairs={{0,4},{1,5},{2,6},{3,7},{4,0},{5,1},{6,2},{7,3},{8,12},{9,13},{10,... | collective-permute-start | bytes 98312 | tf_op jit(solution)/shard_map/pooling/ppermute | solution.py:325
  121.4 4.9 %collective-permute-start.23 = (bf16[8,16,128]{2,1,0:T(8,128)(2,1)}, bf16[8,16,128]{2,1,0:T(8,128)(2,1)S(1)}, u32[]{:S(2)}, u32[]{:S(2)}) collective-permute-start(bf16[8,16,128]{2,1,0:T(8,128)(2,1)} %collective-permute-done.13), channel_id=1, source_target_pairs={{0,5},{1,4},{2,7},{3,6},{4,1},{5,0},{6,3},{7,2},{8,13},{9,12},{10,... | collective-permute-start | bytes 98312 | tf_op jit(solution)/shard_map/pooling/ppermute | solution.py:325
  126.3 5.0 %collective-permute-start.24 = (bf16[8,16,128]{2,1,0:T(8,128)(2,1)S(1)}, bf16[8,16,128]{2,1,0:T(8,128)(2,1)S(1)}, u32[]{:S(2)}, u32[]{:S(2)}) collective-permute-start(bf16[8,16,128]{2,1,0:T(8,128)(2,1)S(1)} %collective-permute-done.14), channel_id=1, source_target_pairs={{0,6},{1,7},{2,4},{3,5},{4,2},{5,3},{6,0},{7,1},{8,14},{9,15},{10,... | collective-permute-start | bytes 98312 | tf_op jit(solution)/shard_map/pooling/ppermute | solution.py:325
  131.3 2.1 collective-permute-start.25
  133.4 2.1 %collective-permute-start.16 = (bf16[8,16,128]{2,1,0:T(8,128)(2,1)S(1)}, bf16[8,16,128]{2,1,0:T(8,128)(2,1)S(1)}, u32[]{:S(2)}, u32[]{:S(2)}) collective-permute-start(bf16[8,16,128]{2,1,0:T(8,128)(2,1)S(1)} %collective-permute-done.9), channel_id=1, source_target_pairs={{0,1},{1,0},{2,3},{3,2},{4,5},{5,4},{6,7},{7,6},{8,9},{9,8},{10,11... | collective-permute-start | bytes 98312 | tf_op jit(solution)/shard_map/pooling/ppermute | solution.py:325
  137.5 3.8 %collective-permute-start.18 = (bf16[8,16,128]{2,1,0:T(8,128)(2,1)S(1)}, bf16[8,16,128]{2,1,0:T(8,128)(2,1)S(1)}, u32[]{:S(2)}, u32[]{:S(2)}) collective-permute-start(bf16[8,16,128]{2,1,0:T(8,128)(2,1)S(1)} %collective-permute-done.11), channel_id=1, source_target_pairs={{0,3},{1,2},{2,1},{3,0},{4,7},{5,6},{6,5},{7,4},{8,11},{9,10},{10,... | collective-permute-start | bytes 98312 | tf_op jit(solution)/shard_map/pooling/ppermute | solution.py:325
  142.9 5.0 %pool_parts.3 = (bf16[512,256]{1,0:T(8,128)(2,1)S(1)}, bf16[512,256]{1,0:T(8,128)(2,1)S(1)}, bf16[512,256]{1,0:T(8,128)(2,1)S(1)}, bf16[512,256]{1,0:T(8,128)(2,1)S(1)}) custom-call(s32[3]{0:T(128)S(1)} %pad_add_fusion.place_ref, bf16[8,4,256,128]{3,2,1,0:T(8,128)(2,1)S(1)} %bitcast.36, bf16[8,16,128]{2,1,0:T(8,128)(2,1)S(1)} %collective-permute-done.22.refs_0_, ...), custom_call_target="tpu_custom_call" | custom-call | flops 4000000000 | bytes 5242880 | tf_op jit(solution)/shard_map/pooling/pool_parts/pallas_call | solution.py:225
  148.0 3.8 %collective-permute-start.26 = (bf16[512,256]{1,0:T(8,128)(2,1)S(1)}, bf16[512,256]{1,0:T(8,128)(2,1)S(1)}, u32[]{:S(2)}, u32[]{:S(2)}) collective-permute-start(bf16[512,256]{1,0:T(8,128)(2,1)S(1)} %get-tuple-element.82), channel_id=1, source_target_pairs={{0,4},{1,5},{2,6},{3,7},{4,0},{5,1},{6,2},{7,3},{8,12},{9,13},{10,... | collective-permute-start | bytes 786440 | tf_op jit(solution)/shard_map/pooling/ppermute | solution.py:325
  151.8 3.0 %collective-permute-start.27 = (bf16[512,256]{1,0:T(8,128)(2,1)S(1)}, bf16[512,256]{1,0:T(8,128)(2,1)S(1)}, u32[]{:S(2)}, u32[]{:S(2)}) collective-permute-start(bf16[512,256]{1,0:T(8,128)(2,1)S(1)} %get-tuple-element.83), channel_id=1, source_target_pairs={{0,5},{1,4},{2,7},{3,6},{4,1},{5,0},{6,3},{7,2},{8,13},{9,12},{10,... | collective-permute-start | bytes 786440 | tf_op jit(solution)/shard_map/pooling/ppermute | solution.py:325
  154.9 4.6 %collective-permute-start.28 = (bf16[512,256]{1,0:T(8,128)(2,1)S(1)}, bf16[512,256]{1,0:T(8,128)(2,1)S(1)}, u32[]{:S(2)}, u32[]{:S(2)}) collective-permute-start(bf16[512,256]{1,0:T(8,128)(2,1)S(1)} %get-tuple-element.84), channel_id=1, source_target_pairs={{0,6},{1,7},{2,4},{3,5},{4,2},{5,3},{6,0},{7,1},{8,14},{9,15},{10,... | collective-permute-start | bytes 786440 | tf_op jit(solution)/shard_map/pooling/ppermute | solution.py:325
  159.5 2.5 %collective-permute-start.29 = (bf16[512,256]{1,0:T(8,128)(2,1)S(1)}, bf16[512,256]{1,0:T(8,128)(2,1)S(1)}, u32[]{:S(2)}, u32[]{:S(2)}) collective-permute-start(bf16[512,256]{1,0:T(8,128)(2,1)S(1)} %get-tuple-element.85), channel_id=1, source_target_pairs={{0,7},{1,6},{2,5},{3,4},{4,3},{5,2},{6,1},{7,0},{8,15},{9,14},{10,... | collective-permute-start | bytes 786440 | tf_op jit(solution)/shard_map/pooling/ppermute | solution.py:325
  162.0 5.1 %pool_parts.2 = (bf16[512,256]{1,0:T(8,128)(2,1)S(1)}, bf16[512,256]{1,0:T(8,128)(2,1)S(1)}, bf16[512,256]{1,0:T(8,128)(2,1)S(1)}, bf16[512,256]{1,0:T(8,128)(2,1)S(1)}) custom-call(s32[3]{0:T(128)S(1)} %pad_add_fusion.place_ref, bf16[8,4,256,128]{3,2,1,0:T(8,128)(2,1)S(1)} %bitcast.37, bf16[8,16,128]{2,1,0:T(8,128)(2,1)S(1)} %collective-permute-done.8.refs_0_, ...), custom_call_target="tpu_custom_call" | custom-call | flops 4000000000 | bytes 5242880 | tf_op jit(solution)/shard_map/pooling/pool_parts/pallas_call | solution.py:225
  171.0 4.0 %collective-permute-start.21 = (bf16[512,256]{1,0:T(8,128)(2,1)S(1)}, bf16[512,256]{1,0:T(8,128)(2,1)S(1)}, u32[]{:S(2)}, u32[]{:S(2)}) collective-permute-start(bf16[512,256]{1,0:T(8,128)(2,1)S(1)} %get-tuple-element.77), channel_id=1, source_target_pairs={{0,3},{1,2},{2,1},{3,0},{4,7},{5,6},{6,5},{7,4},{8,11},{9,10},{10,... | collective-permute-start | bytes 786440 | tf_op jit(solution)/shard_map/pooling/ppermute | solution.py:325
  178.3 6.3 %collective-permute-done.21.refs_3_ = bf16[512,256]{1,0:T(8,128)(2,1)S(1)} collective-permute-done((bf16[512,256]{1,0:T(8,128)(2,1)S(1)}, bf16[512,256]{1,0:T(8,128)(2,1)S(1)}, u32[]{:S(2)}, u32[]{:S(2)}) %collective-permute-start.21) | collective-permute-done | bytes 262176 | tf_op jit(solution)/shard_map/pooling/ppermute | solution.py:325
  184.6 2.7 %cross_layers.1 = bf16[512,512]{1,0:T(8,128)(2,1)} custom-call(bf16[512,256]{1,0:T(8,128)(2,1)S(1)} %get-tuple-element.74.refs_0_, bf16[512,256]{1,0:T(8,128)(2,1)S(1)} %collective-permute-done.19.refs_1_, bf16[512,256]{1,0:T(8,128)(2,1)S(1)} %collective-permute-done.20.refs_2_, bf16[512,256]{1,0:T(8,128)(2,1)S(1)} %collective-permute-done.21.refs_3_, ...), custom_call_target="tpu_custom_call" | custom-call | flops 536870912 | bytes 5242880 | tf_op jit(solution)/shard_map/cross/cross_layers/pallas_call | solution.py:268
  187.6 12.9 %all-gather.1 = bf16[512,256]{1,0:T(8,128)(2,1)S(1)} all-gather(bf16[64,256]{1,0:T(8,128)(2,1)S(1)} %reduce_sum.23), channel_id=3, replica_groups=mesh['mp'=64,'replica'=8] {'replica'}, dimensions={0}, use_global_device_ids=true | all-gather | bytes 294912 | tf_op jit(solution)/shard_map/table_update/all_gather | solution.py:368
  (86 shorter events, 31.5 us)
Async XLA Ops:
  13.8 78.6 %all-to-all-start = ((bf16[8,41,16,256]{3,2,1,0:T(8,128)(2,1)}), bf16[8,41,16,256]{3,2,1,0:T(8,128)(2,1)S(1)}, u32[]{:S(2)}, u32[]{:S(2)}) async-start(bf16[8,41,16,256]{3,2,1,0:T(8,128)(2,1)} %pack_blocks.1), calls=%async_computation | async-start | bytes 5373952 | tf_op jit(solution)/shard_map/over_replica/all_to_all | solution.py:353
  24.3 117.0 %all-gather.4.cloned.1.call-start = ((), (), s32[]{:S(2)}) async-start(), calls=%async_computation.2 | async-start | bytes 2359296 | tf_op jit(solution)/shard_map/table_gather/all_gather | solution.py:341
  24.4 7.4 %collective-permute-start = (bf16[4,256,128]{1,2,0:T(8,128)(2,1)S(1)}, bf16[4,256,128]{1,2,0:T(8,128)(2,1)}, u32[]{:S(2)}, u32[]{:S(2)}) collective-permute-start(bf16[4,256,128]{1,2,0:T(8,128)(2,1)S(1)} %bitcast.40), channel_id=1, source_target_pairs={{0,0},{1,65},{2,130},{3,195},{4,260},{5,325},{6,390},{7,455},{8,8}... | collective-permute-start | bytes 786440 | tf_op jit(solution)/shard_map/table_gather/ppermute | solution.py:340
  33.6 16.4 %collective-permute-start.1 = (bf16[8,16,128]{2,1,0:T(8,128)(2,1)S(1)}, bf16[8,16,128]{2,1,0:T(8,128)(2,1)S(1)}, u32[]{:S(2)}, u32[]{:S(2)}) collective-permute-start(bf16[8,16,128]{2,1,0:T(8,128)(2,1)S(1)} %get-tuple-element.55), channel_id=1, source_target_pairs={{0,8},{8,0},{16,24},{24,16},{32,40},{40,32},{48,56},{56,48},{64,72... | collective-permute-start | bytes 98312 | tf_op jit(solution)/shard_map/bags_over_mp/ppermute | solution.py:331
  35.5 17.7 %collective-permute-start.2 = (bf16[8,16,128]{2,1,0:T(8,128)(2,1)S(1)}, bf16[8,16,128]{2,1,0:T(8,128)(2,1)S(1)}, u32[]{:S(2)}, u32[]{:S(2)}) collective-permute-start(bf16[8,16,128]{2,1,0:T(8,128)(2,1)S(1)} %get-tuple-element.56), channel_id=1, source_target_pairs={{0,16},{8,24},{16,0},{24,8},{32,48},{40,56},{48,32},{56,40},{64,80... | collective-permute-start | bytes 98312 | tf_op jit(solution)/shard_map/bags_over_mp/ppermute | solution.py:331
  37.5 21.2 %collective-permute-start.3 = (bf16[8,16,128]{2,1,0:T(8,128)(2,1)S(1)}, bf16[8,16,128]{2,1,0:T(8,128)(2,1)S(1)}, u32[]{:S(2)}, u32[]{:S(2)}) collective-permute-start(bf16[8,16,128]{2,1,0:T(8,128)(2,1)S(1)} %get-tuple-element.57), channel_id=1, source_target_pairs={{0,24},{8,16},{16,8},{24,0},{32,56},{40,48},{48,40},{56,32},{64,88... | collective-permute-start | bytes 98312 | tf_op jit(solution)/shard_map/bags_over_mp/ppermute | solution.py:331
  42.9 15.7 %collective-permute-start.4 = (bf16[8,16,128]{2,1,0:T(8,128)(2,1)S(1)}, bf16[8,16,128]{2,1,0:T(8,128)(2,1)S(1)}, u32[]{:S(2)}, u32[]{:S(2)}) collective-permute-start(bf16[8,16,128]{2,1,0:T(8,128)(2,1)S(1)} %get-tuple-element.58), channel_id=1, source_target_pairs={{0,32},{8,40},{16,48},{24,56},{32,0},{40,8},{48,16},{56,24},{64,96... | collective-permute-start | bytes 98312 | tf_op jit(solution)/shard_map/bags_over_mp/ppermute | solution.py:331
  46.4 12.3 %collective-permute-start.5 = (bf16[8,16,128]{2,1,0:T(8,128)(2,1)S(1)}, bf16[8,16,128]{2,1,0:T(8,128)(2,1)S(1)}, u32[]{:S(2)}, u32[]{:S(2)}) collective-permute-start(bf16[8,16,128]{2,1,0:T(8,128)(2,1)S(1)} %get-tuple-element.59), channel_id=1, source_target_pairs={{0,40},{8,32},{16,56},{24,48},{32,8},{40,0},{48,24},{56,16},{64,10... | collective-permute-start | bytes 98312 | tf_op jit(solution)/shard_map/bags_over_mp/ppermute | solution.py:331
  50.0 8.6 %collective-permute-start.6 = (bf16[8,16,128]{2,1,0:T(8,128)(2,1)S(1)}, bf16[8,16,128]{2,1,0:T(8,128)(2,1)S(1)}, u32[]{:S(2)}, u32[]{:S(2)}) collective-permute-start(bf16[8,16,128]{2,1,0:T(8,128)(2,1)S(1)} %get-tuple-element.60), channel_id=1, source_target_pairs={{0,48},{8,56},{16,32},{24,40},{32,16},{40,24},{48,0},{56,8},{64,11... | collective-permute-start | bytes 98312 | tf_op jit(solution)/shard_map/bags_over_mp/ppermute | solution.py:331
  53.3 6.7 %collective-permute-start.7 = (bf16[8,16,128]{2,1,0:T(8,128)(2,1)S(1)}, bf16[8,16,128]{2,1,0:T(8,128)(2,1)S(1)}, u32[]{:S(2)}, u32[]{:S(2)}) collective-permute-start(bf16[8,16,128]{2,1,0:T(8,128)(2,1)S(1)} %get-tuple-element.61), channel_id=1, source_target_pairs={{0,56},{8,48},{16,40},{24,32},{32,24},{40,16},{48,8},{56,0},{64,12... | collective-permute-start | bytes 98312 | tf_op jit(solution)/shard_map/bags_over_mp/ppermute | solution.py:331
  60.5 25.6 %collective-permute-start.10 = (bf16[8,16,128]{2,1,0:T(8,128)(2,1)S(1)}, bf16[8,16,128]{2,1,0:T(8,128)(2,1)S(1)}, u32[]{:S(2)}, u32[]{:S(2)}) collective-permute-start(bf16[8,16,128]{2,1,0:T(8,128)(2,1)S(1)} %get-tuple-element.64), channel_id=1, source_target_pairs={{0,128},{1,193},{2,2},{3,67},{4,388},{5,453},{6,262},{7,327},{8,13... | collective-permute-start | bytes 98312 | tf_op jit(solution)/shard_map/bags_over_mp/ppermute | solution.py:350
  66.7 21.3 %collective-permute-start.11 = (bf16[8,16,128]{2,1,0:T(8,128)(2,1)S(1)}, bf16[8,16,128]{2,1,0:T(8,128)(2,1)S(1)}, u32[]{:S(2)}, u32[]{:S(2)}) collective-permute-start(bf16[8,16,128]{2,1,0:T(8,128)(2,1)S(1)} %get-tuple-element.65), channel_id=1, source_target_pairs={{0,192},{1,129},{2,66},{3,3},{4,452},{5,389},{6,326},{7,263},{8,20... | collective-permute-start | bytes 98312 | tf_op jit(solution)/shard_map/bags_over_mp/ppermute | solution.py:350
  68.6 22.5 %collective-permute-start.12 = (bf16[8,16,128]{2,1,0:T(8,128)(2,1)S(1)}, bf16[8,16,128]{2,1,0:T(8,128)(2,1)S(1)}, u32[]{:S(2)}, u32[]{:S(2)}) collective-permute-start(bf16[8,16,128]{2,1,0:T(8,128)(2,1)S(1)} %get-tuple-element.66), channel_id=1, source_target_pairs={{0,256},{1,321},{2,386},{3,451},{4,4},{5,69},{6,134},{7,199},{8,26... | collective-permute-start | bytes 98312 | tf_op jit(solution)/shard_map/bags_over_mp/ppermute | solution.py:350
  76.6 19.7 %collective-permute-start.13 = (bf16[8,16,128]{2,1,0:T(8,128)(2,1)S(1)}, bf16[8,16,128]{2,1,0:T(8,128)(2,1)}, u32[]{:S(2)}, u32[]{:S(2)}) collective-permute-start(bf16[8,16,128]{2,1,0:T(8,128)(2,1)S(1)} %get-tuple-element.67), channel_id=1, source_target_pairs={{0,320},{1,257},{2,450},{3,387},{4,68},{5,5},{6,198},{7,135},{8,32... | collective-permute-start | bytes 98312 | tf_op jit(solution)/shard_map/bags_over_mp/ppermute | solution.py:350
  79.4 16.8 %collective-permute-start.14 = (bf16[8,16,128]{2,1,0:T(8,128)(2,1)S(1)}, bf16[8,16,128]{2,1,0:T(8,128)(2,1)S(1)}, u32[]{:S(2)}, u32[]{:S(2)}) collective-permute-start(bf16[8,16,128]{2,1,0:T(8,128)(2,1)S(1)} %get-tuple-element.68), channel_id=1, source_target_pairs={{0,384},{1,449},{2,258},{3,323},{4,132},{5,197},{6,6},{7,71},{8,39... | collective-permute-start | bytes 98312 | tf_op jit(solution)/shard_map/bags_over_mp/ppermute | solution.py:350
  86.1 10.2 %collective-permute-start.15 = (bf16[8,16,128]{2,1,0:T(8,128)(2,1)S(1)}, bf16[8,16,128]{2,1,0:T(8,128)(2,1)}, u32[]{:S(2)}, u32[]{:S(2)}) collective-permute-start(bf16[8,16,128]{2,1,0:T(8,128)(2,1)S(1)} %get-tuple-element.69), channel_id=1, source_target_pairs={{0,448},{1,385},{2,322},{3,259},{4,196},{5,133},{6,70},{7,7},{8,45... | collective-permute-start | bytes 98312 | tf_op jit(solution)/shard_map/bags_over_mp/ppermute | solution.py:350
  88.0 8.3 %collective-permute-start.8 = (bf16[8,16,128]{2,1,0:T(8,128)(2,1)S(1)}, bf16[8,16,128]{2,1,0:T(8,128)(2,1)S(1)}, u32[]{:S(2)}, u32[]{:S(2)}) collective-permute-start(bf16[8,16,128]{2,1,0:T(8,128)(2,1)S(1)} %get-tuple-element.62), channel_id=1, source_target_pairs={{0,0},{1,65},{2,130},{3,195},{4,260},{5,325},{6,390},{7,455},{8,8}... | collective-permute-start | bytes 98312 | tf_op jit(solution)/shard_map/bags_over_mp/ppermute | solution.py:350
  96.3 91.0 %all-to-all-start.1 = ((bf16[64,64,256]{2,1,0:T(8,128)(2,1)}), bf16[64,64,256]{2,1,0:T(8,128)(2,1)S(1)}, u32[]{:S(2)}, u32[]{:S(2)}) async-start(bf16[64,64,256]{2,1,0:T(8,128)(2,1)} %copy-done), calls=%async_computation.1 | async-start | bytes 4194304 | tf_op jit(solution)/shard_map/parts_over_mp/all_to_all | solution.py:358
  104.6 30.9 %collective-permute-start.22 = (bf16[8,16,128]{2,1,0:T(8,128)(2,1)S(1)}, bf16[8,16,128]{2,1,0:T(8,128)(2,1)S(1)}, u32[]{:S(2)}, u32[]{:S(2)}) collective-permute-start(bf16[8,16,128]{2,1,0:T(8,128)(2,1)S(1)} %copy-done.14), channel_id=1, source_target_pairs={{0,4},{1,5},{2,6},{3,7},{4,0},{5,1},{6,2},{7,3},{8,12},{9,13},{10,... | collective-permute-start | bytes 98312 | tf_op jit(solution)/shard_map/pooling/ppermute | solution.py:325
  121.4 16.0 %collective-permute-start.23 = (bf16[8,16,128]{2,1,0:T(8,128)(2,1)}, bf16[8,16,128]{2,1,0:T(8,128)(2,1)S(1)}, u32[]{:S(2)}, u32[]{:S(2)}) collective-permute-start(bf16[8,16,128]{2,1,0:T(8,128)(2,1)} %collective-permute-done.13), channel_id=1, source_target_pairs={{0,5},{1,4},{2,7},{3,6},{4,1},{5,0},{6,3},{7,2},{8,13},{9,12},{10,... | collective-permute-start | bytes 98312 | tf_op jit(solution)/shard_map/pooling/ppermute | solution.py:325
  126.3 15.0 %collective-permute-start.24 = (bf16[8,16,128]{2,1,0:T(8,128)(2,1)S(1)}, bf16[8,16,128]{2,1,0:T(8,128)(2,1)S(1)}, u32[]{:S(2)}, u32[]{:S(2)}) collective-permute-start(bf16[8,16,128]{2,1,0:T(8,128)(2,1)S(1)} %collective-permute-done.14), channel_id=1, source_target_pairs={{0,6},{1,7},{2,4},{3,5},{4,2},{5,3},{6,0},{7,1},{8,14},{9,15},{10,... | collective-permute-start | bytes 98312 | tf_op jit(solution)/shard_map/pooling/ppermute | solution.py:325
  131.3 10.0 %collective-permute-start.25 = (bf16[8,16,128]{2,1,0:T(8,128)(2,1)}, bf16[8,16,128]{2,1,0:T(8,128)(2,1)S(1)}, u32[]{:S(2)}, u32[]{:S(2)}) collective-permute-start(bf16[8,16,128]{2,1,0:T(8,128)(2,1)} %collective-permute-done.15), channel_id=1, source_target_pairs={{0,7},{1,6},{2,5},{3,4},{4,3},{5,2},{6,1},{7,0},{8,15},{9,14},{10,... | collective-permute-start | bytes 98312 | tf_op jit(solution)/shard_map/pooling/ppermute | solution.py:325
  133.4 21.5 %collective-permute-start.16 = (bf16[8,16,128]{2,1,0:T(8,128)(2,1)S(1)}, bf16[8,16,128]{2,1,0:T(8,128)(2,1)S(1)}, u32[]{:S(2)}, u32[]{:S(2)}) collective-permute-start(bf16[8,16,128]{2,1,0:T(8,128)(2,1)S(1)} %collective-permute-done.9), channel_id=1, source_target_pairs={{0,1},{1,0},{2,3},{3,2},{4,5},{5,4},{6,7},{7,6},{8,9},{9,8},{10,11... | collective-permute-start | bytes 98312 | tf_op jit(solution)/shard_map/pooling/ppermute | solution.py:325
  135.5 23.9 %collective-permute-start.17 = (bf16[8,16,128]{2,1,0:T(8,128)(2,1)S(1)}, bf16[8,16,128]{2,1,0:T(8,128)(2,1)S(1)}, u32[]{:S(2)}, u32[]{:S(2)}) collective-permute-start(bf16[8,16,128]{2,1,0:T(8,128)(2,1)S(1)} %collective-permute-done.10), channel_id=1, source_target_pairs={{0,2},{1,3},{2,0},{3,1},{4,6},{5,7},{6,4},{7,5},{8,10},{9,11},{10,... | collective-permute-start | bytes 98312 | tf_op jit(solution)/shard_map/pooling/ppermute | solution.py:325
  137.5 24.5 %collective-permute-start.18 = (bf16[8,16,128]{2,1,0:T(8,128)(2,1)S(1)}, bf16[8,16,128]{2,1,0:T(8,128)(2,1)S(1)}, u32[]{:S(2)}, u32[]{:S(2)}) collective-permute-start(bf16[8,16,128]{2,1,0:T(8,128)(2,1)S(1)} %collective-permute-done.11), channel_id=1, source_target_pairs={{0,3},{1,2},{2,1},{3,0},{4,7},{5,6},{6,5},{7,4},{8,11},{9,10},{10,... | collective-permute-start | bytes 98312 | tf_op jit(solution)/shard_map/pooling/ppermute | solution.py:325
  148.0 21.1 %collective-permute-start.26 = (bf16[512,256]{1,0:T(8,128)(2,1)S(1)}, bf16[512,256]{1,0:T(8,128)(2,1)S(1)}, u32[]{:S(2)}, u32[]{:S(2)}) collective-permute-start(bf16[512,256]{1,0:T(8,128)(2,1)S(1)} %get-tuple-element.82), channel_id=1, source_target_pairs={{0,4},{1,5},{2,6},{3,7},{4,0},{5,1},{6,2},{7,3},{8,12},{9,13},{10,... | collective-permute-start | bytes 786440 | tf_op jit(solution)/shard_map/pooling/ppermute | solution.py:325
  151.8 19.2 %collective-permute-start.27 = (bf16[512,256]{1,0:T(8,128)(2,1)S(1)}, bf16[512,256]{1,0:T(8,128)(2,1)S(1)}, u32[]{:S(2)}, u32[]{:S(2)}) collective-permute-start(bf16[512,256]{1,0:T(8,128)(2,1)S(1)} %get-tuple-element.83), channel_id=1, source_target_pairs={{0,5},{1,4},{2,7},{3,6},{4,1},{5,0},{6,3},{7,2},{8,13},{9,12},{10,... | collective-permute-start | bytes 786440 | tf_op jit(solution)/shard_map/pooling/ppermute | solution.py:325
  154.9 20.1 %collective-permute-start.28 = (bf16[512,256]{1,0:T(8,128)(2,1)S(1)}, bf16[512,256]{1,0:T(8,128)(2,1)S(1)}, u32[]{:S(2)}, u32[]{:S(2)}) collective-permute-start(bf16[512,256]{1,0:T(8,128)(2,1)S(1)} %get-tuple-element.84), channel_id=1, source_target_pairs={{0,6},{1,7},{2,4},{3,5},{4,2},{5,3},{6,0},{7,1},{8,14},{9,15},{10,... | collective-permute-start | bytes 786440 | tf_op jit(solution)/shard_map/pooling/ppermute | solution.py:325
  159.5 17.0 %collective-permute-start.29 = (bf16[512,256]{1,0:T(8,128)(2,1)S(1)}, bf16[512,256]{1,0:T(8,128)(2,1)S(1)}, u32[]{:S(2)}, u32[]{:S(2)}) collective-permute-start(bf16[512,256]{1,0:T(8,128)(2,1)S(1)} %get-tuple-element.85), channel_id=1, source_target_pairs={{0,7},{1,6},{2,5},{3,4},{4,3},{5,2},{6,1},{7,0},{8,15},{9,14},{10,... | collective-permute-start | bytes 786440 | tf_op jit(solution)/shard_map/pooling/ppermute | solution.py:325
  167.1 9.4 %collective-permute-start.19 = (bf16[512,256]{1,0:T(8,128)(2,1)S(1)}, bf16[512,256]{1,0:T(8,128)(2,1)S(1)}, u32[]{:S(2)}, u32[]{:S(2)}) collective-permute-start(bf16[512,256]{1,0:T(8,128)(2,1)S(1)} %get-tuple-element.75), channel_id=1, source_target_pairs={{0,1},{1,0},{2,3},{3,2},{4,5},{5,4},{6,7},{7,6},{8,9},{9,8},{10,11... | collective-permute-start | bytes 786440 | tf_op jit(solution)/shard_map/pooling/ppermute | solution.py:325
  169.0 9.3 %collective-permute-start.20 = (bf16[512,256]{1,0:T(8,128)(2,1)S(1)}, bf16[512,256]{1,0:T(8,128)(2,1)S(1)}, u32[]{:S(2)}, u32[]{:S(2)}) collective-permute-start(bf16[512,256]{1,0:T(8,128)(2,1)S(1)} %get-tuple-element.76), channel_id=1, source_target_pairs={{0,2},{1,3},{2,0},{3,1},{4,6},{5,7},{6,4},{7,5},{8,10},{9,11},{10,... | collective-permute-start | bytes 786440 | tf_op jit(solution)/shard_map/pooling/ppermute | solution.py:325
  171.0 13.6 %collective-permute-start.21 = (bf16[512,256]{1,0:T(8,128)(2,1)S(1)}, bf16[512,256]{1,0:T(8,128)(2,1)S(1)}, u32[]{:S(2)}, u32[]{:S(2)}) collective-permute-start(bf16[512,256]{1,0:T(8,128)(2,1)S(1)} %get-tuple-element.77), channel_id=1, source_target_pairs={{0,3},{1,2},{2,1},{3,0},{4,7},{5,6},{6,5},{7,4},{8,11},{9,10},{10,... | collective-permute-start | bytes 786440 | tf_op jit(solution)/shard_map/pooling/ppermute | solution.py:325
  (16 other events, 124.3 us)
Sparse Core Ops, SparseCore 0:
  33.7 50.7 all-gather.3

commit v6 on v5

v6 whole, which is shorter than its diff:
```python
import jax
import jax.numpy as jnp
from jax import lax
from jax.experimental import pallas as pl
from jax.experimental.pallas import tpu as pltpu
from jax.sharding import Mesh
from jax.sharding import PartitionSpec as P

VMEM_LIMIT = 48 * 1024 * 1024
learn_rate = 0.3
TILE = 16
SAMPLES = 512
LOWS = ("zl", "yl")
HIGHS = ("zh", "yh")
MP = ("zh", "zl", "yh", "yl")
SIDE = 4
HIGH = SIDE * SIDE
LOW = 4


def owner_of(e, u):
    return e // SIDE * 16 + u // 2 * 8 + e % SIDE * 2 + u % 2


def adagrad(gradient, old_accum, old_table):
    fresh_accum = old_accum + jnp.mean(gradient * gradient, axis=1)
    fresh_table = old_table - learn_rate * gradient / jnp.sqrt(fresh_accum)[:, None]
    return (fresh_table, fresh_accum)


def pack_bags(blocks, entries, weights, targets):
    per_tile, owner_count = blocks.shape
    lanes = entries.shape[1] // owner_count
    entry_count = entries.shape[0]
    span = per_tile * lanes // entry_count

    def kernel(blocks_ref, entries_ref, weights_ref, targets_ref, out_ref):
        shift = lax.broadcasted_iota(jnp.int32, (entry_count, lanes), 0) * span
        lane = lax.broadcasted_iota(jnp.int32, (1, lanes), 1)

        def bags(e, carry):
            for u in range(LOW):
                d = owner_of(e, u)
                at = pl.ds(pl.multiple_of(d * lanes, lanes), lanes)
                chosen = jnp.zeros((1, lanes), jnp.int32)
                for b in range(per_tile):
                    chosen = jnp.where(lane == b, blocks_ref[b, d], chosen)
                bag = jnp.concatenate(
                    [
                        (entries_ref[:, at] - shift).astype(jnp.float32),
                        weights_ref[:, at],
                        (targets_ref[:, at] - 256).astype(jnp.float32),
                        chosen.astype(jnp.float32),
                        jnp.zeros((TILE - 2 * entry_count - 2, lanes), jnp.float32),
                    ],
                    axis=0,
                )
                out_ref[e, u] = bag.astype(out_ref.dtype)
            return carry

        lax.fori_loop(0, HIGH, bags, 0)

    whole = pl.BlockSpec(memory_space=pltpu.VMEM)
    return pl.pallas_call(
        kernel,
        out_shape=jax.ShapeDtypeStruct((HIGH, LOW, TILE, lanes), jnp.bfloat16),
        in_specs=[pl.BlockSpec(memory_space=pltpu.SMEM)] + [whole] * 3,
        out_specs=whole,
        compiler_params=pltpu.CompilerParams(vmem_limit_bytes=VMEM_LIMIT),
        cost_estimate=pl.CostEstimate(flops=0, bytes_accessed=1024 * 1024, transcendentals=0),
        name="pack_bags",
    )(blocks, entries, weights, targets)


def pack_parts(grads, owners, numbers, bags, parts, block_count):
    count, rows, width = grads.shape
    lanes = bags.shape[3]
    sides = width // lanes
    pairs = count // 2
    kept = HIGH // parts

    def kernel(grads_ref, owners_ref, numbers_ref, bags_ref, out_ref, row_ref):
        def cut(i, carry):
            for g in range(rows // TILE):
                for h in range(sides):
                    at = (pl.ds(g * TILE, TILE), pl.ds(h * lanes, lanes))
                    one = grads_ref[(2 * i, *at)].astype(jnp.float32)
                    two = grads_ref[(2 * i + 1, *at)].astype(jnp.float32)
                    for s in range(2):
                        half = slice(s * TILE // 2, (s + 1) * TILE // 2)
                        out_ref[(g * sides + h) * 2 + s, i] = jnp.concatenate([one[half], two[half]], axis=0).astype(
                            out_ref.dtype
                        )
            return carry

        lax.fori_loop(0, pairs, cut, 0)
        row_ref[...] = jnp.zeros_like(row_ref)
        row_ref[0:1, 0:count] = (owners_ref[...] * block_count + numbers_ref[...]).astype(jnp.float32)
        slots = row_ref[...].astype(out_ref.dtype)
        for t in range(LOW * parts):
            out_ref[t, pairs] = slots
            for b in range(kept):
                out_ref[t, pairs + 1 + b] = bags_ref[t % parts * kept + b, t // parts]

    whole = pl.BlockSpec(memory_space=pltpu.VMEM)
    return pl.pallas_call(
        kernel,
        out_shape=jax.ShapeDtypeStruct((LOW * parts, pairs + 1 + kept, TILE, lanes), grads.dtype),
        in_specs=[whole] * 4,
        out_specs=whole,
        scratch_shapes=[pltpu.VMEM((TILE, lanes), jnp.float32)],
        compiler_params=pltpu.CompilerParams(vmem_limit_bytes=VMEM_LIMIT),
        cost_estimate=pl.CostEstimate(flops=0, bytes_accessed=2 * grads.size * 2, transcendentals=0),
        name="pack_parts",
    )(grads, owners, numbers, bags)


def add_parts(arrived, count, parts, block_count):
    sources, tiles, _, lanes = arrived.shape
    pairs = count // 2
    kept = tiles - pairs - 1
    slot_count = HIGH * LOW * block_count
    half = TILE // 2

    def kernel(recv_ref, out_ref, bags_ref, acc_ref, numbers_ref, slots_ref, sem):
        for t in range(sources):
            numbers_ref[pl.ds(t, 1), :] = recv_ref[t, pairs].astype(jnp.float32)[0:1].astype(jnp.int32)
        copy = pltpu.make_async_copy(numbers_ref, slots_ref, sem)
        copy.start()
        acc_ref[...] = jnp.zeros_like(acc_ref)
        for t in range(sources):
            u, r = t // parts, t % parts
            for b in range(kept):
                bags_ref[r, u // 2 * 2 * kept + b * 2 + u % 2] = recv_ref[t, pairs + 1 + b]
        copy.wait()

        def add(i, carry):
            for t in range(sources):
                both = recv_ref[t, i].astype(jnp.float32)
                one, two = slots_ref[t, 2 * i], slots_ref[t, 2 * i + 1]
                acc_ref[one] = acc_ref[one] + both[0:half]
                acc_ref[two] = acc_ref[two] + both[half:TILE]
            return carry

        lax.fori_loop(0, pairs, add, 0)

        def place(e, carry):
            for u in range(LOW):
                for b in range(0, block_count, 2):
                    slot = owner_of(e, u) * block_count + b
                    out_ref[e, pl.ds((u * block_count + b) * half, TILE), :] = jnp.concatenate(
                        [acc_ref[slot], acc_ref[slot + 1]], axis=0
                    ).astype(out_ref.dtype)
            return carry

        lax.fori_loop(0, HIGH, place, 0)

    whole = pl.BlockSpec(memory_space=pltpu.VMEM)
    return pl.pallas_call(
        kernel,
        out_shape=[
            jax.ShapeDtypeStruct((HIGH, LOW * block_count * half, lanes), jnp.bfloat16),
            jax.ShapeDtypeStruct((parts, LOW * kept, TILE, lanes), jnp.bfloat16),
        ],
        in_specs=[whole],
        out_specs=[whole] * 2,
        scratch_shapes=[
            pltpu.VMEM((slot_count, half, lanes), jnp.float32),
            pltpu.VMEM((sources, lanes), jnp.int32),
            pltpu.SMEM((sources, lanes), jnp.int32),
            pltpu.SemaphoreType.DMA(()),
        ],
        compiler_params=pltpu.CompilerParams(vmem_limit_bytes=VMEM_LIMIT),
        cost_estimate=pl.CostEstimate(flops=0, bytes_accessed=10 * 1024 * 1024, transcendentals=0),
        name="add_parts",
    )(arrived)


def add_sources(received, parts):
    sources, rows, lanes = received.shape
    each = rows // LOW

    def kernel(recv_ref, out_ref):
        for u in range(LOW):
            at = pl.ds(u * each, each)
            total = recv_ref[0, at, :].astype(jnp.float32)
            for e in range(1, sources):
                total = total + recv_ref[e, at, :].astype(jnp.float32)
            total = total.astype(out_ref.dtype)
            for r in range(parts):
                out_ref[u * parts + r] = total

    whole = pl.BlockSpec(memory_space=pltpu.VMEM)
    return pl.pallas_call(
        kernel,
        out_shape=jax.ShapeDtypeStruct((LOW * parts, each, lanes), jnp.bfloat16),
        in_specs=[whole],
        out_specs=whole,
        compiler_params=pltpu.CompilerParams(vmem_limit_bytes=VMEM_LIMIT),
        cost_estimate=pl.CostEstimate(flops=0, bytes_accessed=1024 * 1024, transcendentals=0),
        name="add_sources",
    )(received)


def pool_parts(first, many, place, table, bags):
    owner_count, block_count, width, lanes = table.shape
    parts = bags.shape[0]
    per_tile = 3
    entry_count = 4
    span = per_tile * lanes // entry_count
    samples = SAMPLES

    def kernel(place_ref, table_ref, bags_ref, *refs):
        out_refs = refs[:many]
        numbers_ref, blocks_ref, sem = refs[many:]
        step = pl.program_id(0)
        replica = place_ref[0] ^ (step + first)

        @pl.when(step == 0)
        def _():
            for r in range(parts):
                for p in range(owner_count):
                    numbers_ref[pl.ds(r * owner_count + p, 1), :] = (
                        bags_ref[r, p].astype(jnp.float32)[2 * entry_count + 1 : 2 * entry_count + 2].astype(jnp.int32)
                    )
            copy = pltpu.make_async_copy(numbers_ref, blocks_ref, sem)
            copy.start()
            copy.wait()

        position = lax.broadcasted_iota(jnp.int32, (span, lanes), 0)
        sample = lax.broadcasted_iota(jnp.int32, (samples, owner_count * lanes), 0)
        partials, targets = [], []
        for p in range(owner_count):
            bag = bags_ref[replica, p].astype(jnp.float32)
            entries = bag[0:entry_count].astype(jnp.int32)
            weights = bag[entry_count : 2 * entry_count]
            targets.append(bag[2 * entry_count : 2 * entry_count + 1].astype(jnp.int32) + 256)
            incidence = jnp.concatenate(
                [
                    jnp.where(position == entries[l : l + 1], weights[l : l + 1], 0.0)
                    for l in range(entry_count)
                ],
                axis=0,
            ).astype(jnp.bfloat16)
            chosen = [blocks_ref[replica * owner_count + p, j] for j in range(per_tile)]
            slab = jnp.concatenate([table_ref[p, b] for b in chosen], axis=1)
            partials.append(
                jnp.dot(slab, incidence, preferred_element_type=jnp.float32).astype(jnp.bfloat16)
            )
        selector = jnp.where(sample == jnp.concatenate(targets, axis=1), 1.0, 0.0).astype(jnp.bfloat16)
        pooled = lax.dot_general(
            selector,
            jnp.concatenate(partials, axis=1),
            (((1,), (1,)), ((), ())),
            preferred_element_type=jnp.float32,
        ).astype(jnp.bfloat16)
        for i in range(many):

            @pl.when(step == i)
            def _(i=i):
                out_refs[i][...] = pooled

    whole = pl.BlockSpec(memory_space=pltpu.VMEM)
    return pl.pallas_call(
        kernel,
        out_shape=[jax.ShapeDtypeStruct((samples, width), jnp.bfloat16)] * many,
        grid=(many,),
        in_specs=[pl.BlockSpec(memory_space=pltpu.SMEM), whole, whole],
        out_specs=[whole] * many,
        scratch_shapes=[
            pltpu.VMEM((parts * owner_count, lanes), jnp.int32),
            pltpu.SMEM((parts * owner_count, lanes), jnp.int32),
            pltpu.SemaphoreType.DMA(()),
        ],
        compiler_params=pltpu.CompilerParams(
            dimension_semantics=("arbitrary",), vmem_limit_bytes=VMEM_LIMIT
        ),
        cost_estimate=pl.CostEstimate(
            flops=many * 1_000_000_000, bytes_accessed=5 * 1024 * 1024, transcendentals=0
        ),
        name="pool_parts",
    )(place, table, bags)


def cross_layers(pooled_parts, other_feats, cross_w, cross_b):
    parts = len(pooled_parts)
    samples, width = pooled_parts[0].shape
    layers, full, _ = cross_w.shape
    tile = 128

    def kernel(*refs):
        feats_ref, w_ref, b_ref, out_ref = refs[parts:]
        pooled = refs[0][...].astype(jnp.float32)
        for j in range(1, parts):
            pooled = pooled + refs[j][...].astype(jnp.float32)
        first = jnp.concatenate([pooled, feats_ref[...].astype(jnp.float32)], axis=1)
        crossed = first
        for layer in range(layers):
            mixing = (
                jnp.dot(crossed.astype(jnp.bfloat16), w_ref[layer], preferred_element_type=jnp.float32)
                + b_ref[layer : layer + 1, :]
            )
            crossed = first * mixing + crossed
        out_ref[...] = crossed.astype(out_ref.dtype)

    return pl.pallas_call(
        kernel,
        out_shape=jax.ShapeDtypeStruct((samples, full), jnp.bfloat16),
        grid=(samples // tile,),
        in_specs=[
            *[pl.BlockSpec((tile, width), lambda i: (i, 0))] * parts,
            pl.BlockSpec((tile, full - width), lambda i: (i, 0)),
            pl.BlockSpec((layers, full, full), lambda i: (0, 0, 0)),
            pl.BlockSpec((layers, full), lambda i: (0, 0)),
        ],
        out_specs=pl.BlockSpec((tile, full), lambda i: (i, 0)),
        compiler_params=pltpu.CompilerParams(
            dimension_semantics=("arbitrary",), vmem_limit_bytes=VMEM_LIMIT
        ),
        cost_estimate=pl.CostEstimate(
            flops=2 * layers * samples * full * full, bytes_accessed=5 * 1024 * 1024, transcendentals=0
        ),
        name="cross_layers",
    )(*pooled_parts, other_feats, cross_w, cross_b)


def local(
    table,
    accum,
    bag_blocks,
    bag_entries,
    bag_weights,
    bag_target,
    other_feats,
    cross_w,
    cross_b,
    evict_grads,
    evict_owner,
    evict_block,
):
    parts = lax.axis_size("replica")
    count, block_rows, width = evict_grads.shape[1:]
    slab_rows = table.shape[0]
    block_count = slab_rows // block_rows
    place = lax.axis_index("replica").astype(jnp.int32).reshape(1)
    lows = (*LOWS, "replica")

    def to_replica(arrays, first):
        return [
            lax.ppermute(array, "replica", [(r, r ^ k) for r in range(parts)]) if k else array
            for k, array in enumerate(arrays, first)
        ]

    with jax.named_scope("table_gather"):
        slab = lax.optimization_barrier(table).astype(jnp.bfloat16)
        slab = slab.reshape(block_count, block_rows, width).transpose(0, 2, 1)
        moves = []
        for owner in range(HIGH * LOW):
            z, y = owner // 8, owner % 8
            pooler, number = z // 2 * 2 + y // 4, z % 2 * 4 + y % 4
            moves += [(owner * parts + r, (r * 8 + number) * parts + pooler) for r in range(parts)]
        moved = lax.ppermute(slab, (*MP, "replica"), moves)
        slabs = lax.all_gather(moved, ("yh", "yl"), axis=0)

    with jax.named_scope("bags_over_high"):
        bags = pack_bags(bag_blocks[0].T, bag_entries[0].T, bag_weights[0].T, bag_target)
        bags = lax.all_to_all(bags, HIGHS, split_axis=0, concat_axis=0, tiled=True)
        bags, _ = lax.optimization_barrier((bags, moved))

    with jax.named_scope("parts_over_low"):
        sent = pack_parts(evict_grads[0], evict_owner[:, :, 0], evict_block, bags, parts, block_count)
        arrived = lax.all_to_all(sent, lows, split_axis=0, concat_axis=0, tiled=True)

    with jax.named_scope("sums_over_high"):
        sums, bags = add_parts(arrived, count, parts, block_count)
        received = lax.all_to_all(sums, HIGHS, split_axis=0, concat_axis=0, tiled=True)

    with jax.named_scope("pooling"):
        pooled = []
        for first in range(0, parts, parts // 2):
            pooled += to_replica(pool_parts(first, parts // 2, place, slabs, bags), first)

    with jax.named_scope("sums_to_owners"):
        shared = add_sources(received, parts)
        pooled, _ = lax.optimization_barrier((pooled, shared))
        grads = lax.all_to_all(shared, lows, split_axis=0, concat_axis=0, tiled=True)

    with jax.named_scope("table_update"):
        half = TILE // 2
        lanes = shared.shape[2]
        table_grad = (
            grads.reshape(block_rows // TILE, width // lanes, 2, block_count, half, lanes)
            .transpose(3, 0, 2, 4, 1, 5)
            .reshape(slab_rows, width)
            .astype(jnp.float32)
        )
        new_table, new_accum = adagrad(table_grad, accum, table)

    with jax.named_scope("cross"):
        cross_out = cross_layers(pooled, other_feats[0], cross_w, cross_b)
    return (cross_out[None], new_table, new_accum)


def solution(mesh):
    parts = mesh.shape["replica"]
    fine = Mesh(mesh.devices.reshape(SIDE, 2, SIDE, 2, parts), (*MP, "replica"))
    in_specs = (
        P(MP, None),
        P(MP),
        P("replica", MP, None),
        P("replica", MP, None),
        P("replica", MP, None),
        P("replica", MP),
        P("replica", MP, None),
        P(),
        P(),
        P("replica", MP, None, None),
        P("replica", MP, None),
        P("replica", MP),
    )
    out_specs = (P("replica", MP, None), P(MP, None), P(MP))
    return jax.shard_map(local, mesh=fine, in_specs=in_specs, out_specs=out_specs, check_vma=False)
```

time: 211 us -> 201 us (0.953)
  starting transfers between devices: 135 us -> 73.5 us
  waiting for transfers between devices: 16.4 us -> 76.7 us
  blocking collectives: 12.9 us -> 0 us
  local copies, waits for them, and re-layouts: 9.3 us -> 12.2 us
    all_to_all x2 -> x4, waiting for transfers between devices: 0.01 us -> 54.7 us  [the longest x1 54.7 us: local(): lax.all_to_all(sent, lows, split_axis=0, concat_axis=0, tiled=True)]
    ppermute x16 -> x1, starting transfers between devices: 58.1 us -> 3.94 us  [local(): moved = lax.ppermute(slab, (*MP, 'replica'), moves)]
    ppermute x14 -> x7, starting transfers between devices: 58.5 us -> 21.7 us  [to_replica(): lax.ppermute(array, 'replica', [(r, r ^ k) for r in range(parts)])]
    all_to_all x2 -> x4, starting transfers between devices: 18.8 us -> 47.8 us  [the longest x1 18.8 us: local(): lax.all_to_all(sent, lows, split_axis=0, concat_axis=0, tiled=True)]
    all_gather x1 -> x0, blocking collectives: 12.9 us -> none  [local(): grads = lax.all_gather(grad_part, 'replica', axis=0)]
    ppermute x16 -> x1, waiting for transfers between devices: 6.77 us -> 12 us  [local(): moved = lax.ppermute(slab, (*MP, 'replica'), moves)]
    unnamed x31 -> x29, local copies, waits for them, and re-layouts: 7.3 us -> 11.1 us
    pallas_call x4, Pallas kernels: 5.83 us -> 8.46 us  [the longest x1 5.33 us: add_parts(): pl.pallas_call(kernel, out_shape=[jax.ShapeDtypeStruct((HIGH, LOW * block...]
  transfers between devices with their start and end apart: 33 -> 13, of which waited for: 5 -> 4; matrix products, arithmetic and copies ran while one was open for 1% -> 1% of each run, Pallas kernels for 8% -> 9%
where the time goes in v6:
time: 201 us; the launch traced here: 200 us
  waiting for transfers between devices  76.7 us (38%)
  starting transfers between devices  73.5 us (37%)
  Pallas kernels  20.5 us (10%)
  between operations  14.3 us (7%)
  local copies, waits for them, and re-layouts  12.2 us (6%)
  other arithmetic  2.83 us (1%)
    all_to_all x1, waiting for transfers between devices, local(): lax.all_to_all(sent, lows, split_axis=0, concat_axis=0, tiled=True)  54.7 us
    ppermute x7, starting transfers between devices, to_replica(): lax.ppermute(array, 'replica', [(r, r ^ k) for r in range(parts)])  21.7 us
    all_to_all x1, starting transfers between devices, local(): lax.all_to_all(sent, lows, split_axis=0, concat_axis=0, tiled=True)  18.8 us
    all_to_all x1, starting transfers between devices, local(): bags = lax.all_to_all(bags, HIGHS, split_axis=0, concat_axis=0, tiled=True)  16.2 us
    ppermute x1, waiting for transfers between devices, local(): moved = lax.ppermute(slab, (*MP, 'replica'), moves)  12 us
    unnamed x29, local copies, waits for them, and re-layouts  11.1 us
    ppermute x7, waiting for transfers between devices, to_replica(): lax.ppermute(array, 'replica', [(r, r ^ k) for r in range(parts)])  9.88 us
    pallas_call x2, Pallas kernels, pool_parts(): pl.pallas_call(kernel, out_shape=[jax.ShapeDtypeStruct((samples, width),...  9.41 us
  transfers between devices with their start and end apart: 13, of which 4 were waited for; matrix products, arithmetic and copies ran while one was open for 1% of the time, Pallas kernels for 9%

profile of v6, /device:TPU:1, one launch (start us, length us, event | category | flops | bytes accessed | tf_op | source)
XLA Modules:
  0.0 200.1 jit_solution(13627875125978161428)
XLA Ops:
  7.8 0.9 copy-done.4
  8.8 0.9 copy-done.5
  9.7 0.8 copy-done.6
  10.4 1.8 pack_bags.1
  12.2 16.2 %all-to-all-start = ((bf16[16,4,16,128]{3,2,1,0:T(8,128)(2,1)}), bf16[16,4,16,128]{3,2,1,0:T(8,128)(2,1)S(1)}, u32[]{:S(2)}, u32[]{:S(2)}) async-start(bf16[16,4,16,128]{3,2,1,0:T(8,128)(2,1)} %pack_bags.1), calls=%async_computation | async-start | bytes 524288 | tf_op jit(solution)/shard_map/bags_over_high/all_to_all | solution.py:367
  28.4 1.1 convert_element_type.12
  29.5 3.9 %collective-permute-start = (bf16[4,256,128]{1,2,0:T(8,128)(2,1)S(1)}, bf16[4,256,128]{1,2,0:T(8,128)(2,1)S(1)}, u32[]{:S(2)}, u32[]{:S(2)}) collective-permute-start(bf16[4,256,128]{1,2,0:T(8,128)(2,1)S(1)} %bitcast.37), channel_id=1, source_target_pairs={{0,0},{1,64},{2,128},{3,192},{4,256},{5,320},{6,384},{7,448},{8,8}... | collective-permute-start | bytes 786440 | tf_op jit(solution)/shard_map/table_gather/ppermute | solution.py:362
  33.4 12.0 %collective-permute-done = bf16[4,256,128]{1,2,0:T(8,128)(2,1)S(1)} collective-permute-done((bf16[4,256,128]{1,2,0:T(8,128)(2,1)S(1)}, bf16[4,256,128]{1,2,0:T(8,128)(2,1)S(1)}, u32[]{:S(2)}, u32[]{:S(2)}) %collective-permute-start) | collective-permute-done | bytes 262176 | tf_op jit(solution)/shard_map/table_gather/ppermute | solution.py:362
  45.5 1.7 copy-done.1
  49.1 1.6 copy-done
  50.7 18.8 %all-to-all-start.1 = ((bf16[32,23,16,128]{3,2,1,0:T(8,128)(2,1)}), bf16[32,23,16,128]{3,2,1,0:T(8,128)(2,1)S(1)}, u32[]{:S(2)}, u32[]{:S(2)}) async-start(bf16[32,23,16,128]{3,2,1,0:T(8,128)(2,1)} %copy-done), calls=%async_computation.1 | async-start | bytes 6029312 | tf_op jit(solution)/shard_map/parts_over_low/all_to_all | solution.py:372
  69.6 0.8 copy.25
  70.4 54.7 %all-to-all-done.1.recv_ref = bf16[32,23,16,128]{3,2,1,0:T(8,128)(2,1)S(1)} async-done(((bf16[32,23,16,128]{3,2,1,0:T(8,128)(2,1)}), bf16[32,23,16,128]{3,2,1,0:T(8,128)(2,1)S(1)}, u32[]{:S(2)}, u32[]{:S(2)}) %all-to-all-start.1) | async-done | bytes 3014688 | tf_op jit(solution)/shard_map/parts_over_low/all_to_all | solution.py:372
  125.2 5.3 %add_parts.1 = (bf16[16,128,128]{2,1,0:T(8,128)(2,1)}, bf16[8,8,16,128]{3,2,1,0:T(8,128)(2,1)S(1)}) custom-call(bf16[32,23,16,128]{3,2,1,0:T(8,128)(2,1)S(1)} %all-to-all-done.1.recv_ref), custom_call_target="tpu_custom_call" | custom-call | bytes 10485760 | tf_op jit(solution)/shard_map/sums_over_high/add_parts/pallas_call | solution.py:159
  130.5 8.9 %all-to-all-start.2 = ((bf16[16,128,128]{2,1,0:T(8,128)(2,1)}), bf16[16,128,128]{2,1,0:T(8,128)(2,1)S(1)}, u32[]{:S(2)}, u32[]{:S(2)}) async-start(bf16[16,128,128]{2,1,0:T(8,128)(2,1)} %get-tuple-element.32), calls=%async_computation.2 | async-start | bytes 1048576 | tf_op jit(solution)/shard_map/sums_over_high/all_to_all | solution.py:376
  139.5 1.6 copy-done.10
  141.1 4.7 %pool_parts.3 = (bf16[512,256]{1,0:T(8,128)(2,1)S(1)}, bf16[512,256]{1,0:T(8,128)(2,1)S(1)}, bf16[512,256]{1,0:T(8,128)(2,1)S(1)}, bf16[512,256]{1,0:T(8,128)(2,1)S(1)}) custom-call(s32[1]{0:T(128)} %bitcast.place_ref, bf16[8,4,256,128]{3,2,1,0:T(8,128)(2,1)S(1)} %bitcast.32, bf16[8,8,16,128]{3,2,1,0:T(8,128)(2,1)S(1)} %get-tuple-element.23.bags_ref), custom_call_target="tpu_custom_call" | custom-call | flops 4000000000 | bytes 5242880 | tf_op jit(solution)/shard_map/pooling/pool_parts/pallas_call | solution.py:264
  145.8 1.9 collective-permute-start.4
  147.7 4.3 %collective-permute-start.5 = (bf16[512,256]{1,0:T(8,128)(2,1)S(1)}, bf16[512,256]{1,0:T(8,128)(2,1)S(1)}, u32[]{:S(2)}, u32[]{:S(2)}) collective-permute-start(bf16[512,256]{1,0:T(8,128)(2,1)S(1)} %get-tuple-element.29), channel_id=1, source_target_pairs={{0,5},{1,4},{2,7},{3,6},{4,1},{5,0},{6,3},{7,2},{8,13},{9,12},{10,... | collective-permute-start | bytes 786440 | tf_op jit(solution)/shard_map/pooling/ppermute | solution.py:350
  152.0 2.0 collective-permute-start.6
  154.0 5.7 %collective-permute-start.7 = (bf16[512,256]{1,0:T(8,128)(2,1)S(1)}, bf16[512,256]{1,0:T(8,128)(2,1)S(1)}, u32[]{:S(2)}, u32[]{:S(2)}) collective-permute-start(bf16[512,256]{1,0:T(8,128)(2,1)S(1)} %get-tuple-element.31), channel_id=1, source_target_pairs={{0,7},{1,6},{2,5},{3,4},{4,3},{5,2},{6,1},{7,0},{8,15},{9,14},{10,... | collective-permute-start | bytes 786440 | tf_op jit(solution)/shard_map/pooling/ppermute | solution.py:350
  159.7 0.8 add_sources.1
  160.5 3.8 %all-to-all-start.3 = ((bf16[32,32,128]{2,1,0:T(8,128)(2,1)}), bf16[32,32,128]{2,1,0:T(8,128)(2,1)S(1)}, u32[]{:S(2)}, u32[]{:S(2)}) async-start(bf16[32,32,128]{2,1,0:T(8,128)(2,1)} %add_sources.1), calls=%async_computation.3 | async-start | bytes 524288 | tf_op jit(solution)/shard_map/sums_to_owners/all_to_all | solution.py:386
  164.3 1.6 copy-done.11
  165.9 4.7 %pool_parts.2 = (bf16[512,256]{1,0:T(8,128)(2,1)S(1)}, bf16[512,256]{1,0:T(8,128)(2,1)S(1)}, bf16[512,256]{1,0:T(8,128)(2,1)S(1)}, bf16[512,256]{1,0:T(8,128)(2,1)S(1)}) custom-call(s32[1]{0:T(128)} %bitcast.place_ref, bf16[8,4,256,128]{3,2,1,0:T(8,128)(2,1)S(1)} %bitcast.33, bf16[8,8,16,128]{3,2,1,0:T(8,128)(2,1)S(1)} %get-tuple-element.23.bags_ref), custom_call_target="tpu_custom_call" | custom-call | flops 4000000000 | bytes 5242880 | tf_op jit(solution)/shard_map/pooling/pool_parts/pallas_call | solution.py:264
  170.6 2.2 %collective-permute-start.1 = (bf16[512,256]{1,0:T(8,128)(2,1)S(1)}, bf16[512,256]{1,0:T(8,128)(2,1)S(1)}, u32[]{:S(2)}, u32[]{:S(2)}) collective-permute-start(bf16[512,256]{1,0:T(8,128)(2,1)S(1)} %get-tuple-element.25), channel_id=1, source_target_pairs={{0,1},{1,0},{2,3},{3,2},{4,5},{5,4},{6,7},{7,6},{8,9},{9,8},{10,11... | collective-permute-start | bytes 786440 | tf_op jit(solution)/shard_map/pooling/ppermute | solution.py:350
  172.9 3.3 %collective-permute-start.2 = (bf16[512,256]{1,0:T(8,128)(2,1)S(1)}, bf16[512,256]{1,0:T(8,128)(2,1)S(1)}, u32[]{:S(2)}, u32[]{:S(2)}) collective-permute-start(bf16[512,256]{1,0:T(8,128)(2,1)S(1)} %get-tuple-element.26), channel_id=1, source_target_pairs={{0,2},{1,3},{2,0},{3,1},{4,6},{5,7},{6,4},{7,5},{8,10},{9,11},{10,... | collective-permute-start | bytes 786440 | tf_op jit(solution)/shard_map/pooling/ppermute | solution.py:350
  176.2 2.3 %collective-permute-start.3 = (bf16[512,256]{1,0:T(8,128)(2,1)S(1)}, bf16[512,256]{1,0:T(8,128)(2,1)S(1)}, u32[]{:S(2)}, u32[]{:S(2)}) collective-permute-start(bf16[512,256]{1,0:T(8,128)(2,1)S(1)} %get-tuple-element.27), channel_id=1, source_target_pairs={{0,3},{1,2},{2,1},{3,0},{4,7},{5,6},{6,5},{7,4},{8,11},{9,10},{10,... | collective-permute-start | bytes 786440 | tf_op jit(solution)/shard_map/pooling/ppermute | solution.py:350
  178.5 4.0 %collective-permute-done.2.refs_2_ = bf16[512,256]{1,0:T(8,128)(2,1)S(1)} collective-permute-done((bf16[512,256]{1,0:T(8,128)(2,1)S(1)}, bf16[512,256]{1,0:T(8,128)(2,1)S(1)}, u32[]{:S(2)}, u32[]{:S(2)}) %collective-permute-start.2) | collective-permute-done | bytes 262176 | tf_op jit(solution)/shard_map/pooling/ppermute | solution.py:350
  182.5 5.9 %collective-permute-done.3.refs_3_ = bf16[512,256]{1,0:T(8,128)(2,1)S(1)} collective-permute-done((bf16[512,256]{1,0:T(8,128)(2,1)S(1)}, bf16[512,256]{1,0:T(8,128)(2,1)S(1)}, u32[]{:S(2)}, u32[]{:S(2)}) %collective-permute-start.3) | collective-permute-done | bytes 262176 | tf_op jit(solution)/shard_map/pooling/ppermute | solution.py:350
  188.4 2.7 %cross_layers.1 = bf16[512,512]{1,0:T(8,128)(2,1)} custom-call(bf16[512,256]{1,0:T(8,128)(2,1)S(1)} %get-tuple-element.33.refs_0_, bf16[512,256]{1,0:T(8,128)(2,1)S(1)} %collective-permute-done.1.refs_1_, bf16[512,256]{1,0:T(8,128)(2,1)S(1)} %collective-permute-done.2.refs_2_, bf16[512,256]{1,0:T(8,128)(2,1)S(1)} %collective-permute-done.3.refs_3_, ...), custom_call_target="tpu_custom_call" | custom-call | flops 536870912 | bytes 5242880 | tf_op jit(solution)/shard_map/cross/cross_layers/pallas_call | solution.py:306
  192.3 0.9 divide_subtract_fusion
  (42 shorter events, 3.8 us)
Async XLA Ops:
  7.8 0.9 copy-start.4
  8.8 0.9 copy-start.5
  9.7 0.8 copy-start.6
  12.2 33.3 %all-to-all-start = ((bf16[16,4,16,128]{3,2,1,0:T(8,128)(2,1)}), bf16[16,4,16,128]{3,2,1,0:T(8,128)(2,1)S(1)}, u32[]{:S(2)}, u32[]{:S(2)}) async-start(bf16[16,4,16,128]{3,2,1,0:T(8,128)(2,1)} %pack_bags.1), calls=%async_computation | async-start | bytes 524288 | tf_op jit(solution)/shard_map/bags_over_high/all_to_all | solution.py:367
  29.5 16.0 %collective-permute-start = (bf16[4,256,128]{1,2,0:T(8,128)(2,1)S(1)}, bf16[4,256,128]{1,2,0:T(8,128)(2,1)S(1)}, u32[]{:S(2)}, u32[]{:S(2)}) collective-permute-start(bf16[4,256,128]{1,2,0:T(8,128)(2,1)S(1)} %bitcast.37), channel_id=1, source_target_pairs={{0,0},{1,64},{2,128},{3,192},{4,256},{5,320},{6,384},{7,448},{8,8}... | collective-permute-start | bytes 786440 | tf_op jit(solution)/shard_map/table_gather/ppermute | solution.py:362
  45.5 1.7 copy-start.1
  47.2 0.7 copy-start.8
  47.9 0.7 copy-start.9
  49.1 1.6 copy-start
  50.7 74.5 %all-to-all-start.1 = ((bf16[32,23,16,128]{3,2,1,0:T(8,128)(2,1)}), bf16[32,23,16,128]{3,2,1,0:T(8,128)(2,1)S(1)}, u32[]{:S(2)}, u32[]{:S(2)}) async-start(bf16[32,23,16,128]{3,2,1,0:T(8,128)(2,1)} %copy-done), calls=%async_computation.1 | async-start | bytes 6029312 | tf_op jit(solution)/shard_map/parts_over_low/all_to_all | solution.py:372
  69.5 70.0 %all-gather.3.cloned.1.call-start = ((), (), s32[]{:S(2)}) async-start(), calls=%async_computation.4 | async-start | bytes 2359296 | tf_op jit(solution)/shard_map/table_gather/all_gather | solution.py:363
  130.5 29.2 %all-to-all-start.2 = ((bf16[16,128,128]{2,1,0:T(8,128)(2,1)}), bf16[16,128,128]{2,1,0:T(8,128)(2,1)S(1)}, u32[]{:S(2)}, u32[]{:S(2)}) async-start(bf16[16,128,128]{2,1,0:T(8,128)(2,1)} %get-tuple-element.32), calls=%async_computation.2 | async-start | bytes 1048576 | tf_op jit(solution)/shard_map/sums_over_high/all_to_all | solution.py:376
  139.5 1.6 copy-start.10
  145.8 27.1 %collective-permute-start.4 = (bf16[512,256]{1,0:T(8,128)(2,1)S(1)}, bf16[512,256]{1,0:T(8,128)(2,1)S(1)}, u32[]{:S(2)}, u32[]{:S(2)}) collective-permute-start(bf16[512,256]{1,0:T(8,128)(2,1)S(1)} %get-tuple-element.28), channel_id=1, source_target_pairs={{0,4},{1,5},{2,6},{3,7},{4,0},{5,1},{6,2},{7,3},{8,12},{9,13},{10,... | collective-permute-start | bytes 786440 | tf_op jit(solution)/shard_map/pooling/ppermute | solution.py:350
  147.7 28.5 %collective-permute-start.5 = (bf16[512,256]{1,0:T(8,128)(2,1)S(1)}, bf16[512,256]{1,0:T(8,128)(2,1)S(1)}, u32[]{:S(2)}, u32[]{:S(2)}) collective-permute-start(bf16[512,256]{1,0:T(8,128)(2,1)S(1)} %get-tuple-element.29), channel_id=1, source_target_pairs={{0,5},{1,4},{2,7},{3,6},{4,1},{5,0},{6,3},{7,2},{8,13},{9,12},{10,... | collective-permute-start | bytes 786440 | tf_op jit(solution)/shard_map/pooling/ppermute | solution.py:350
  152.0 26.5 %collective-permute-start.6 = (bf16[512,256]{1,0:T(8,128)(2,1)S(1)}, bf16[512,256]{1,0:T(8,128)(2,1)S(1)}, u32[]{:S(2)}, u32[]{:S(2)}) collective-permute-start(bf16[512,256]{1,0:T(8,128)(2,1)S(1)} %get-tuple-element.30), channel_id=1, source_target_pairs={{0,6},{1,7},{2,4},{3,5},{4,2},{5,3},{6,0},{7,1},{8,14},{9,15},{10,... | collective-permute-start | bytes 786440 | tf_op jit(solution)/shard_map/pooling/ppermute | solution.py:350
  154.0 24.5 %collective-permute-start.7 = (bf16[512,256]{1,0:T(8,128)(2,1)S(1)}, bf16[512,256]{1,0:T(8,128)(2,1)S(1)}, u32[]{:S(2)}, u32[]{:S(2)}) collective-permute-start(bf16[512,256]{1,0:T(8,128)(2,1)S(1)} %get-tuple-element.31), channel_id=1, source_target_pairs={{0,7},{1,6},{2,5},{3,4},{4,3},{5,2},{6,1},{7,0},{8,15},{9,14},{10,... | collective-permute-start | bytes 786440 | tf_op jit(solution)/shard_map/pooling/ppermute | solution.py:350
  160.5 30.7 %all-to-all-start.3 = ((bf16[32,32,128]{2,1,0:T(8,128)(2,1)}), bf16[32,32,128]{2,1,0:T(8,128)(2,1)S(1)}, u32[]{:S(2)}, u32[]{:S(2)}) async-start(bf16[32,32,128]{2,1,0:T(8,128)(2,1)} %add_sources.1), calls=%async_computation.3 | async-start | bytes 524288 | tf_op jit(solution)/shard_map/sums_to_owners/all_to_all | solution.py:386
  164.3 1.6 copy-start.11
  165.9 22.5 %copy-start.2 = (bf16[2,512,512]{2,1,0:T(8,128)(2,1)S(1)}, bf16[2,512,512]{2,1,0:T(8,128)(2,1)}, u32[]{:S(2)}) copy-start(bf16[2,512,512]{2,1,0:T(8,128)(2,1)} %refs_9_.1) | copy-start | bytes 3145732
  165.9 22.5 %copy-start.3 = (bf16[1,512,256]{2,1,0:T(8,128)(2,1)S(1)}, bf16[1,512,256]{2,1,0:T(8,128)(2,1)}, u32[]{:S(2)}) copy-start(bf16[1,512,256]{2,1,0:T(8,128)(2,1)} %param.18) | copy-start | bytes 786436
  165.9 22.5 %copy-start.7 = (f32[2,512]{1,0:T(2,128)S(1)}, f32[2,512]{1,0:T(2,128)}, u32[]{:S(2)}) copy-start(f32[2,512]{1,0:T(2,128)} %refs_10_.1) | copy-start | bytes 12292
  170.6 7.9 %collective-permute-start.1 = (bf16[512,256]{1,0:T(8,128)(2,1)S(1)}, bf16[512,256]{1,0:T(8,128)(2,1)S(1)}, u32[]{:S(2)}, u32[]{:S(2)}) collective-permute-start(bf16[512,256]{1,0:T(8,128)(2,1)S(1)} %get-tuple-element.25), channel_id=1, source_target_pairs={{0,1},{1,0},{2,3},{3,2},{4,5},{5,4},{6,7},{7,6},{8,9},{9,8},{10,11... | collective-permute-start | bytes 786440 | tf_op jit(solution)/shard_map/pooling/ppermute | solution.py:350
  172.9 9.6 %collective-permute-start.2 = (bf16[512,256]{1,0:T(8,128)(2,1)S(1)}, bf16[512,256]{1,0:T(8,128)(2,1)S(1)}, u32[]{:S(2)}, u32[]{:S(2)}) collective-permute-start(bf16[512,256]{1,0:T(8,128)(2,1)S(1)} %get-tuple-element.26), channel_id=1, source_target_pairs={{0,2},{1,3},{2,0},{3,1},{4,6},{5,7},{6,4},{7,5},{8,10},{9,11},{10,... | collective-permute-start | bytes 786440 | tf_op jit(solution)/shard_map/pooling/ppermute | solution.py:350
  176.2 12.2 %collective-permute-start.3 = (bf16[512,256]{1,0:T(8,128)(2,1)S(1)}, bf16[512,256]{1,0:T(8,128)(2,1)S(1)}, u32[]{:S(2)}, u32[]{:S(2)}) collective-permute-start(bf16[512,256]{1,0:T(8,128)(2,1)S(1)} %get-tuple-element.27), channel_id=1, source_target_pairs={{0,3},{1,2},{2,1},{3,0},{4,7},{5,6},{6,5},{7,4},{8,11},{9,10},{10,... | collective-permute-start | bytes 786440 | tf_op jit(solution)/shard_map/pooling/ppermute | solution.py:350
  188.4 3.3 %copy-start.13 = (f32[512]{0:T(512)S(1)}, f32[512]{0:T(512)}, u32[]{:S(2)}) copy-start(f32[512]{0:T(512)} %param.13) | copy-start | bytes 6148
  188.4 3.9 %copy-start.12 = (f32[512,256]{1,0:T(8,128)S(1)}, f32[512,256]{1,0:T(8,128)}, u32[]{:S(2)}) copy-start(f32[512,256]{1,0:T(8,128)} %param.12) | copy-start | bytes 1572868
Sparse Core Ops, SparseCore 0:
  73.0 52.6 all-gather.2

commit v7 on v6

v7 whole, which is shorter than its diff:
```python
import jax
import jax.numpy as jnp
from jax import lax
from jax.experimental import pallas as pl
from jax.experimental.pallas import tpu as pltpu
from jax.sharding import Mesh
from jax.sharding import PartitionSpec as P

VMEM_LIMIT = 48 * 1024 * 1024
learn_rate = 0.3
TILE = 16
SMALL = pl.CostEstimate(flops=1000, bytes_accessed=1000, transcendentals=0)
TAIL = 5
SAMPLES = 512
LOWS = ("yl", "replica")
HIGHS = ("z", "yh")
MP = ("z", "yh", "yl")
SIDE = 8


def adagrad(gradient, old_accum, old_table):
    fresh_accum = old_accum + jnp.mean(gradient * gradient, axis=1)
    fresh_table = old_table - learn_rate * gradient / jnp.sqrt(fresh_accum)[:, None]
    return (fresh_table, fresh_accum)


def pack_bags(blocks, entries, weights, targets):
    per_tile, owner_count = blocks.shape
    lanes = entries.shape[1] // owner_count
    entry_count = entries.shape[0]
    span = per_tile * lanes // entry_count

    def kernel(blocks_ref, entries_ref, weights_ref, targets_ref, out_ref):
        shift = lax.broadcasted_iota(jnp.int32, (entry_count, lanes), 0) * span
        lane = lax.broadcasted_iota(jnp.int32, (1, lanes), 1)

        def bags(e, carry):
            for u in range(4):
                d = 4 * e + u
                at = pl.ds(pl.multiple_of(d * lanes, lanes), lanes)
                chosen = jnp.zeros((1, lanes), jnp.int32)
                for b in range(per_tile):
                    chosen = jnp.where(lane == b, blocks_ref[b, d], chosen)
                bag = jnp.concatenate(
                    [
                        (entries_ref[:, at] - shift).astype(jnp.float32),
                        weights_ref[:, at],
                        (targets_ref[:, at] - 256).astype(jnp.float32),
                        chosen.astype(jnp.float32),
                        jnp.zeros((TILE - 2 * entry_count - 2, lanes), jnp.float32),
                    ],
                    axis=0,
                )
                out_ref[d] = bag.astype(out_ref.dtype)
            return carry

        lax.fori_loop(0, owner_count // 4, bags, 0)

    whole = pl.BlockSpec(memory_space=pltpu.VMEM)
    return pl.pallas_call(
        kernel,
        out_shape=jax.ShapeDtypeStruct((owner_count, TILE, lanes), jnp.bfloat16),
        in_specs=[pl.BlockSpec(memory_space=pltpu.SMEM)] + [whole] * 3,
        out_specs=whole,
        compiler_params=pltpu.CompilerParams(vmem_limit_bytes=VMEM_LIMIT),
        cost_estimate=SMALL,
        name="pack_bags",
    )(blocks, entries, weights, targets)


def pack_parts(grads):
    count, rows, width = grads.shape
    lanes = 128
    sides = width // lanes
    receivers = rows // TILE * sides

    def kernel(grads_ref, out_ref):
        def cut(i, carry):
            for g in range(rows // TILE):
                for h in range(sides):
                    out_ref[g * sides + h, i] = grads_ref[i, pl.ds(g * TILE, TILE), pl.ds(h * lanes, lanes)]
            return carry

        lax.fori_loop(0, TAIL, cut, 0)

    return pl.pallas_call(
        kernel,
        out_shape=jax.ShapeDtypeStruct((receivers, count + TAIL, TILE, lanes), grads.dtype),
        grid=(count // TAIL,),
        in_specs=[pl.BlockSpec((TAIL, rows, width), lambda i: (i, 0, 0))],
        out_specs=pl.BlockSpec((receivers, TAIL, TILE, lanes), lambda i: (0, i, 0, 0)),
        compiler_params=pltpu.CompilerParams(
            dimension_semantics=("arbitrary",), vmem_limit_bytes=VMEM_LIMIT
        ),
        cost_estimate=SMALL,
        name="pack_parts",
    )(grads)


def add_bags(place, packed, owners, numbers, bags, parts, block_count):
    receivers, tiles, _, lanes = packed.shape
    count = owners.shape[1]
    kept = TAIL - 1

    def kernel(place_ref, packed_ref, owners_ref, numbers_ref, bags_ref, out_ref, row_ref):
        row_ref[...] = jnp.zeros_like(row_ref)
        row_ref[0:1, 0:count] = (owners_ref[...] * block_count + numbers_ref[...]).astype(jnp.float32)
        slots = row_ref[...].astype(out_ref.dtype)
        for t in range(receivers):
            u, j = t // parts, t % parts
            z = j ^ (place_ref[2] + u)
            out_ref[t, 0] = slots
            for b in range(kept):
                out_ref[t, 1 + b] = bags_ref[z * kept + b, u]

    whole = pl.BlockSpec(memory_space=pltpu.VMEM)
    return pl.pallas_call(
        kernel,
        out_shape=jax.ShapeDtypeStruct(packed.shape, packed.dtype),
        grid=(1,),
        in_specs=[pl.BlockSpec(memory_space=pltpu.SMEM), pl.BlockSpec(memory_space=pl.ANY), whole, whole, whole],
        out_specs=pl.BlockSpec((receivers, TAIL, TILE, lanes), lambda i: (0, tiles // TAIL - 1, 0, 0)),
        scratch_shapes=[pltpu.VMEM((TILE, lanes), jnp.float32)],
        input_output_aliases={1: 0},
        compiler_params=pltpu.CompilerParams(vmem_limit_bytes=VMEM_LIMIT),
        cost_estimate=SMALL,
        name="add_bags",
    )(place, packed, owners, numbers, bags)


def add_parts(arrived, count, parts, slot_count, highs):
    sources, _, _, lanes = arrived.shape
    kept = TAIL - 1
    lows = sources // parts
    each = slot_count // highs

    def kernel(recv_ref, out_ref, bags_ref, acc_ref, numbers_ref, slots_ref, sem):
        for t in range(sources):
            numbers_ref[pl.ds(t, 1), :] = recv_ref[t, count].astype(jnp.float32)[0:1].astype(jnp.int32)
        copy = pltpu.make_async_copy(numbers_ref, slots_ref, sem)
        copy.start()
        acc_ref[...] = jnp.zeros_like(acc_ref)
        for t in range(sources):
            for b in range(kept):
                bags_ref[t % parts, b * lows + t // parts] = recv_ref[t, count + 1 + b]
        copy.wait()

        def add(i, carry):
            for t in range(sources):
                slot = slots_ref[t, i]
                acc_ref[slot] = acc_ref[slot] + recv_ref[t, i].astype(jnp.float32)
            return carry

        lax.fori_loop(0, count, add, 0)

        def place(e, carry):
            for i in range(each):
                out_ref[e, pl.ds(i * TILE, TILE), :] = acc_ref[e * each + i].astype(out_ref.dtype)
            return carry

        lax.fori_loop(0, highs, place, 0)

    whole = pl.BlockSpec(memory_space=pltpu.VMEM)
    return pl.pallas_call(
        kernel,
        out_shape=[
            jax.ShapeDtypeStruct((highs, each * TILE, lanes), jnp.bfloat16),
            jax.ShapeDtypeStruct((parts, lows * kept, TILE, lanes), jnp.bfloat16),
        ],
        in_specs=[whole],
        out_specs=[whole] * 2,
        scratch_shapes=[
            pltpu.VMEM((slot_count, TILE, lanes), jnp.float32),
            pltpu.VMEM((sources, lanes), jnp.int32),
            pltpu.SMEM((sources, lanes), jnp.int32),
            pltpu.SemaphoreType.DMA(()),
        ],
        compiler_params=pltpu.CompilerParams(vmem_limit_bytes=VMEM_LIMIT),
        cost_estimate=SMALL,
        name="add_parts",
    )(arrived)


def add_sources(received, lows, parts):
    sources, rows, lanes = received.shape
    each = rows // lows
    tile = 32

    def kernel(recv_ref, out_ref):
        for u in range(lows):
            for first in range(0, each, tile):
                at = pl.ds(u * each + first, tile)
                total = recv_ref[0, at, :].astype(jnp.float32)
                for e in range(1, sources):
                    total = total + recv_ref[e, at, :].astype(jnp.float32)
                total = total.astype(out_ref.dtype)
                for r in range(parts):
                    out_ref[u * parts + r, pl.ds(first, tile), :] = total

    whole = pl.BlockSpec(memory_space=pltpu.VMEM)
    return pl.pallas_call(
        kernel,
        out_shape=jax.ShapeDtypeStruct((lows * parts, each, lanes), jnp.bfloat16),
        in_specs=[whole],
        out_specs=whole,
        compiler_params=pltpu.CompilerParams(vmem_limit_bytes=VMEM_LIMIT),
        cost_estimate=SMALL,
        name="add_sources",
    )(received)


def pool_parts(place, table, bags):
    owner_count, block_count, width, lanes = table.shape
    parts = bags.shape[0]
    many = parts // 2
    per_tile = 3
    entry_count = 4
    span = per_tile * lanes // entry_count
    samples = SAMPLES

    def kernel(place_ref, table_ref, bags_ref, others_ref, mine_ref, numbers_ref, blocks_ref, sem):
        step = pl.program_id(0)
        replica = place_ref[0] ^ jnp.where(step < many, 2 * step + 1, 2 * (step - many))

        @pl.when(step == 0)
        def _():
            for r in range(parts):
                for p in range(owner_count):
                    numbers_ref[pl.ds(r * owner_count + p, 1), :] = (
                        bags_ref[r, p].astype(jnp.float32)[2 * entry_count + 1 : 2 * entry_count + 2].astype(jnp.int32)
                    )
            copy = pltpu.make_async_copy(numbers_ref, blocks_ref, sem)
            copy.start()
            copy.wait()

        position = lax.broadcasted_iota(jnp.int32, (span, lanes), 0)
        sample = lax.broadcasted_iota(jnp.int32, (samples, owner_count * lanes), 0)
        partials, targets = [], []
        for p in range(owner_count):
            bag = bags_ref[replica, p].astype(jnp.float32)
            entries = bag[0:entry_count].astype(jnp.int32)
            weights = bag[entry_count : 2 * entry_count]
            targets.append(bag[2 * entry_count : 2 * entry_count + 1].astype(jnp.int32) + 256)
            incidence = jnp.concatenate(
                [
                    jnp.where(position == entries[l : l + 1], weights[l : l + 1], 0.0)
                    for l in range(entry_count)
                ],
                axis=0,
            ).astype(jnp.bfloat16)
            chosen = [blocks_ref[replica * owner_count + p, j] for j in range(per_tile)]
            owner = p ^ place_ref[1]
            slab = jnp.concatenate([table_ref[owner, b] for b in chosen], axis=1)
            partials.append(
                jnp.dot(slab, incidence, preferred_element_type=jnp.float32).astype(jnp.bfloat16)
            )
        selector = jnp.where(sample == jnp.concatenate(targets, axis=1), 1.0, 0.0).astype(jnp.bfloat16)
        pooled = lax.dot_general(
            selector,
            jnp.concatenate(partials, axis=1),
            (((1,), (1,)), ((), ())),
            preferred_element_type=jnp.float32,
        )

        @pl.when(step < many)
        def _():
            others_ref[0] = pooled

        @pl.when(step >= many)
        def _():
            mine_ref[0] = pooled

    whole = pl.BlockSpec(memory_space=pltpu.VMEM)
    return pl.pallas_call(
        kernel,
        out_shape=[jax.ShapeDtypeStruct((many, samples, width), jnp.float32)] * 2,
        grid=(parts,),
        in_specs=[pl.BlockSpec(memory_space=pltpu.SMEM), whole, whole],
        out_specs=[
            pl.BlockSpec((1, samples, width), lambda i: (jnp.minimum(i, many - 1), 0, 0)),
            pl.BlockSpec((1, samples, width), lambda i: (jnp.maximum(i - many, 0), 0, 0)),
        ],
        scratch_shapes=[
            pltpu.VMEM((parts * owner_count, lanes), jnp.int32),
            pltpu.SMEM((parts * owner_count, lanes), jnp.int32),
            pltpu.SemaphoreType.DMA(()),
        ],
        compiler_params=pltpu.CompilerParams(
            dimension_semantics=("arbitrary",), vmem_limit_bytes=VMEM_LIMIT
        ),
        cost_estimate=SMALL,
        name="pool_parts",
    )(place, table, bags)


def join(mine, theirs):
    many, samples, width = mine.shape
    tile = samples // 4

    def kernel(mine_ref, theirs_ref, *out_refs):
        for i in range(many):
            out_refs[i][...] = (mine_ref[i] + theirs_ref[i]).astype(jnp.bfloat16)

    block = pl.BlockSpec((many, tile, width), lambda i: (0, i, 0))
    return pl.pallas_call(
        kernel,
        out_shape=[jax.ShapeDtypeStruct((samples, width), jnp.bfloat16)] * many,
        grid=(samples // tile,),
        in_specs=[block] * 2,
        out_specs=[pl.BlockSpec((tile, width), lambda i: (i, 0))] * many,
        compiler_params=pltpu.CompilerParams(
            dimension_semantics=("arbitrary",), vmem_limit_bytes=VMEM_LIMIT
        ),
        cost_estimate=SMALL,
        name="join",
    )(mine, theirs)


def cross_layers(pooled_parts, other_feats, cross_w, cross_b):
    parts = len(pooled_parts)
    samples, width = pooled_parts[0].shape
    layers, full, _ = cross_w.shape
    tile = 128

    def kernel(*refs):
        feats_ref, w_ref, b_ref, out_ref = refs[parts:]
        pooled = refs[0][...].astype(jnp.float32)
        for j in range(1, parts):
            pooled = pooled + refs[j][...].astype(jnp.float32)
        first = jnp.concatenate([pooled, feats_ref[...].astype(jnp.float32)], axis=1)
        crossed = first
        for layer in range(layers):
            mixing = (
                jnp.dot(crossed.astype(jnp.bfloat16), w_ref[layer], preferred_element_type=jnp.float32)
                + b_ref[layer : layer + 1, :]
            )
            crossed = first * mixing + crossed
        out_ref[...] = crossed.astype(out_ref.dtype)

    return pl.pallas_call(
        kernel,
        out_shape=jax.ShapeDtypeStruct((samples, full), jnp.bfloat16),
        grid=(samples // tile,),
        in_specs=[
            *[pl.BlockSpec((tile, width), lambda i: (i, 0))] * parts,
            pl.BlockSpec((tile, full - width), lambda i: (i, 0)),
            pl.BlockSpec((layers, full, full), lambda i: (0, 0, 0)),
            pl.BlockSpec((layers, full), lambda i: (0, 0)),
        ],
        out_specs=pl.BlockSpec((tile, full), lambda i: (i, 0)),
        compiler_params=pltpu.CompilerParams(
            dimension_semantics=("arbitrary",), vmem_limit_bytes=VMEM_LIMIT
        ),
        cost_estimate=SMALL,
        name="cross_layers",
    )(*pooled_parts, other_feats, cross_w, cross_b)


def local(
    table,
    accum,
    bag_blocks,
    bag_entries,
    bag_weights,
    bag_target,
    other_feats,
    cross_w,
    cross_b,
    evict_grads,
    evict_owner,
    evict_block,
):
    parts = lax.axis_size("replica")
    count, block_rows, width = evict_grads.shape[1:]
    slab_rows = table.shape[0]
    block_count = slab_rows // block_rows
    highs = lax.axis_size(HIGHS)
    lows = lax.axis_size("yl")
    me = lax.axis_index("replica").astype(jnp.int32)
    y = lax.axis_index(("yh", "yl")).astype(jnp.int32)
    place = jnp.stack([me, me ^ y, y - y % lows])

    def to_replica(array, k):
        return lax.ppermute(array, "replica", [(r, r ^ k) for r in range(parts)])

    with jax.named_scope("table_gather"):
        slab = lax.optimization_barrier(table).astype(jnp.bfloat16)
        slab = slab.reshape(block_count, block_rows, width).transpose(0, 2, 1)
        moves = []
        for owner in range(SIDE * SIDE):
            own_z, own_y = owner // SIDE, owner % SIDE
            for r in range(parts):
                to_z, to_y = own_y ^ own_z, own_y ^ r
                moves.append((owner * parts + r, (to_z * SIDE + to_y) * parts + (own_z ^ to_y)))
        moved = lax.ppermute(slab, (*MP, "replica"), moves)
        slabs = lax.all_gather(moved, "z", axis=0)

    with jax.named_scope("bags_over_high"):
        bags = pack_bags(bag_blocks[0].T, bag_entries[0].T, bag_weights[0].T, bag_target)
        bags, _ = lax.optimization_barrier((bags, moved))
        bags = bags.reshape(highs, lows, TILE, bags.shape[2])
        bags = lax.all_to_all(bags, HIGHS, split_axis=0, concat_axis=0, tiled=True)

    with jax.named_scope("parts_over_low"):
        packed = pack_parts(evict_grads[0])
        sent = add_bags(place, packed, evict_owner[:, :, 0], evict_block, bags, parts, block_count)
        arrived = lax.all_to_all(sent, LOWS, split_axis=0, concat_axis=0, tiled=True)

    with jax.named_scope("sums_over_high"):
        sums, bags = add_parts(arrived, count, parts, highs * lows * block_count, highs)
        received = lax.all_to_all(sums, HIGHS, split_axis=0, concat_axis=0, tiled=True)

    with jax.named_scope("pooling"):
        others, mine = pool_parts(place, slabs, bags)
        joined = join(mine, to_replica(others, 1))
        pooled = [joined[0]] + [to_replica(joined[i], 2 * i) for i in range(1, parts // 2)]

    with jax.named_scope("sums_to_owners"):
        received, _ = lax.optimization_barrier((received, others))
        shared = add_sources(received, lows, parts)
        grads = lax.all_to_all(shared, LOWS, split_axis=0, concat_axis=0, tiled=True)

    with jax.named_scope("table_update"):
        lanes = shared.shape[2]
        table_grad = (
            grads.reshape(block_rows // TILE, width // lanes, block_count, TILE, lanes)
            .transpose(2, 0, 3, 1, 4)
            .reshape(slab_rows, width)
            .astype(jnp.float32)
        )
        new_table, new_accum = adagrad(table_grad, accum, table)

    with jax.named_scope("cross"):
        cross_out = cross_layers(pooled, other_feats[0], cross_w, cross_b)
    return (cross_out[None], new_table, new_accum)


def solution(mesh):
    parts = mesh.shape["replica"]
    fine = Mesh(mesh.devices.reshape(SIDE, SIDE // 2, 2, parts), (*MP, "replica"))
    in_specs = (
        P(MP, None),
        P(MP),
        P("replica", MP, None),
        P("replica", MP, None),
        P("replica", MP, None),
        P("replica", MP),
        P("replica", MP, None),
        P(),
        P(),
        P("replica", MP, None, None),
        P("replica", MP, None),
        P("replica", MP),
    )
    out_specs = (P("replica", MP, None), P(MP, None), P(MP))
    return jax.shard_map(local, mesh=fine, in_specs=in_specs, out_specs=out_specs, check_vma=False)
```

time: 201 us -> 196 us (0.975)
  starting transfers between devices: 73.5 us -> 67.6 us
  Pallas kernels: 20.5 us -> 26.3 us
  local copies, waits for them, and re-layouts: 12.2 us -> 7.42 us
    all_to_all x1, waiting for transfers between devices: 0.01 us -> 18.6 us  [local(): lax.all_to_all(sums, HIGHS, split_axis=0, concat_axis=0, tiled=True)]
    all_to_all x2, waiting for transfers between devices: 54.7 us -> 36.5 us  [the longest x1 36.5 us: local(): lax.all_to_all(sent, LOWS, split_axis=0, concat_axis=0, tiled=True)]
    all_to_all x1, starting transfers between devices: 16.2 us -> 29 us  [local(): bags = lax.all_to_all(bags, HIGHS, split_axis=0, concat_axis=0, tiled=True)]
    ppermute x1, waiting for transfers between devices: 12 us -> 0.62 us  [local(): moved = lax.ppermute(slab, (*MP, 'replica'), moves)]
    ppermute x7 -> x4, starting transfers between devices: 21.7 us -> 12.5 us  [to_replica(): return lax.ppermute(array, 'replica', [(r, r ^ k) for r in range(parts)])]
    all_to_all x1, waiting for transfers between devices: 0.01 us -> 6.48 us  [local(): bags = lax.all_to_all(bags, HIGHS, split_axis=0, concat_axis=0, tiled=True)]
    pallas_call x6 -> x7, Pallas kernels: 17.9 us -> 23.7 us  [the longest x1 10.9 us: pool_parts(): pl.pallas_call(kernel, out_shape=[jax.ShapeDtypeStruct((many, samples, wi...]
    all_to_all x2, starting transfers between devices: 22.6 us -> 17.5 us  [the longest x1 9.32 us: local(): lax.all_to_all(shared, LOWS, split_axis=0, concat_axis=0, tiled=True)]
  transfers between devices with their start and end apart: 13 -> 10, of which waited for: 4 -> 6; matrix products, arithmetic and copies ran while one was open for 1% -> 1% of each run, Pallas kernels for 9% -> 13%
where the time goes in v7:
time: 196 us
  waiting for transfers between devices  76.3 us (39%)
  starting transfers between devices  67.6 us (34%)
  Pallas kernels  26.3 us (13%)
  between operations  14.2 us (7%)
  local copies, waits for them, and re-layouts  7.42 us (4%)
  other arithmetic  3.85 us (2%)
    all_to_all x1, waiting for transfers between devices, local(): lax.all_to_all(sent, LOWS, split_axis=0, concat_axis=0, tiled=True)  36.5 us
    all_to_all x1, starting transfers between devices, local(): bags = lax.all_to_all(bags, HIGHS, split_axis=0, concat_axis=0, tiled=True)  29 us
    all_to_all x1, waiting for transfers between devices, local(): lax.all_to_all(sums, HIGHS, split_axis=0, concat_axis=0, tiled=True)  18.6 us
    ppermute x4, waiting for transfers between devices, to_replica(): return lax.ppermute(array, 'replica', [(r, r ^ k) for r in range(parts)])  14.1 us
    ppermute x4, starting transfers between devices, to_replica(): return lax.ppermute(array, 'replica', [(r, r ^ k) for r in range(parts)])  12.5 us
    pallas_call x1, Pallas kernels, pool_parts(): pl.pallas_call(kernel, out_shape=[jax.ShapeDtypeStruct((many, samples, wi...  10.9 us
    all_to_all x1, starting transfers between devices, local(): lax.all_to_all(shared, LOWS, split_axis=0, concat_axis=0, tiled=True)  9.32 us
    all_to_all x1, starting transfers between devices, local(): lax.all_to_all(sent, LOWS, split_axis=0, concat_axis=0, tiled=True)  8.18 us
  transfers between devices with their start and end apart: 10, of which 6 were waited for; matrix products, arithmetic and copies ran while one was open for 1% of the time, Pallas kernels for 13%

profile of v7, /device:TPU:1, one launch (start us, length us, event | category | flops | bytes accessed | tf_op | source)
XLA Modules:
  0.0 195.6 jit_solution(7786729469824354523)
XLA Ops:
  7.2 1.1 convert_element_type.12
  8.2 4.0 %collective-permute-start = (bf16[4,256,128]{1,2,0:T(8,128)(2,1)S(1)}, bf16[4,256,128]{1,2,0:T(8,128)(2,1)S(1)}, u32[]{:S(2)}, u32[]{:S(2)}) collective-permute-start(bf16[4,256,128]{1,2,0:T(8,128)(2,1)S(1)} %bitcast.44), channel_id=1, source_target_pairs={{0,0},{1,9},{2,18},{3,27},{4,36},{5,45},{6,54},{7,63},{8,73},{9,64... | collective-permute-start | bytes 786440 | tf_op jit(solution)/shard_map/table_gather/ppermute | solution.py:395
  12.3 0.7 copy.36
  13.0 0.9 copy-done.4
  13.9 0.9 copy-done.5
  14.8 0.8 copy-done.6
  15.5 1.7 pack_bags.1
  17.8 29.0 %all-to-all-start = ((bf16[32,2,16,128]{3,2,1,0:T(8,128)(2,1)}), bf16[32,2,16,128]{3,2,1,0:T(8,128)(2,1)S(1)}, u32[]{:S(2)}, u32[]{:S(2)}) async-start(bf16[32,2,16,128]{3,2,1,0:T(8,128)(2,1)} %bitcast.13), calls=%async_computation | async-start | bytes 524288 | tf_op jit(solution)/shard_map/bags_over_high/all_to_all | solution.py:402
  46.9 1.7 copy-done
  48.6 3.5 %pack_parts.1.packed_ref = bf16[16,45,16,128]{3,2,1,0:T(8,128)(2,1)} custom-call(bf16[40,128,256]{2,1,0:T(8,128)(2,1)S(1)} %bitcast.34), custom_call_target="tpu_custom_call" | custom-call | flops 1000 | bytes 1000 | tf_op jit(solution)/shard_map/parts_over_low/pack_parts/pallas_call | solution.py:86
  52.2 6.5 %all-to-all-done.bags_ref = bf16[32,2,16,128]{3,2,1,0:T(8,128)(2,1)S(1)} async-done(((bf16[32,2,16,128]{3,2,1,0:T(8,128)(2,1)}), bf16[32,2,16,128]{3,2,1,0:T(8,128)(2,1)S(1)}, u32[]{:S(2)}, u32[]{:S(2)}) %all-to-all-start) | async-done | bytes 262176 | tf_op jit(solution)/shard_map/bags_over_high/all_to_all | solution.py:402
  58.7 1.3 add_bags.1
  60.0 8.2 %all-to-all-start.1 = ((bf16[16,45,16,128]{3,2,1,0:T(8,128)(2,1)}), bf16[16,45,16,128]{3,2,1,0:T(8,128)(2,1)S(1)}, u32[]{:S(2)}, u32[]{:S(2)}) async-start(bf16[16,45,16,128]{3,2,1,0:T(8,128)(2,1)} %add_bags.1), calls=%async_computation.1 | async-start | bytes 5898240 | tf_op jit(solution)/shard_map/parts_over_low/all_to_all | solution.py:407
  68.2 0.8 copy.25
  69.1 36.5 %all-to-all-done.1.recv_ref = bf16[16,45,16,128]{3,2,1,0:T(8,128)(2,1)S(1)} async-done(((bf16[16,45,16,128]{3,2,1,0:T(8,128)(2,1)}), bf16[16,45,16,128]{3,2,1,0:T(8,128)(2,1)S(1)}, u32[]{:S(2)}, u32[]{:S(2)}) %all-to-all-start.1) | async-done | bytes 2949152 | tf_op jit(solution)/shard_map/parts_over_low/all_to_all | solution.py:407
  105.5 2.9 %add_parts.1 = (bf16[32,128,128]{2,1,0:T(8,128)(2,1)S(1)}, bf16[8,8,16,128]{3,2,1,0:T(8,128)(2,1)S(1)}) custom-call(bf16[16,45,16,128]{3,2,1,0:T(8,128)(2,1)S(1)} %all-to-all-done.1.recv_ref), custom_call_target="tpu_custom_call" | custom-call | flops 1000 | bytes 1000 | tf_op jit(solution)/shard_map/sums_over_high/add_parts/pallas_call | solution.py:164
  108.5 1.0 copy-done.2
  109.5 4.5 %all-to-all-start.2 = ((bf16[32,128,128]{2,1,0:T(8,128)(2,1)}), bf16[32,128,128]{2,1,0:T(8,128)(2,1)S(1)}, u32[]{:S(2)}, u32[]{:S(2)}) async-start(bf16[32,128,128]{2,1,0:T(8,128)(2,1)} %copy-done.2), calls=%async_computation.2 | async-start | bytes 2097152 | tf_op jit(solution)/shard_map/sums_over_high/all_to_all | solution.py:411
  114.0 10.9 %pool_parts.1 = (f32[4,512,256]{2,1,0:T(8,128)}, f32[4,512,256]{2,1,0:T(8,128)S(1)}) custom-call(s32[3]{0:T(128)S(1)} %pad_add_fusion.place_ref, bf16[8,4,256,128]{3,2,1,0:T(8,128)(2,1)} %bitcast.40, bf16[8,8,16,128]{3,2,1,0:T(8,128)(2,1)S(1)} %get-tuple-element.14.bags_ref), custom_call_target="tpu_custom_call" | custom-call | flops 1000 | bytes 1000 | tf_op jit(solution)/shard_map/pooling/pool_parts/pallas_call | solution.py:274
  124.9 2.8 %collective-permute-start.1 = (f32[4,512,256]{2,1,0:T(8,128)}, f32[4,512,256]{2,1,0:T(8,128)}, u32[]{:S(2)}, u32[]{:S(2)}) collective-permute-start(f32[4,512,256]{2,1,0:T(8,128)} %get-tuple-element.16), channel_id=1, source_target_pairs={{0,1},{1,0},{2,3},{3,2},{4,5},{5,4},{6,7},{7,6},{8,9},{9,8},{10,11... | collective-permute-start | bytes 6291464 | tf_op jit(solution)/shard_map/pooling/ppermute | solution.py:384
  127.7 18.6 %all-to-all-done.2.recv_ref = bf16[32,128,128]{2,1,0:T(8,128)(2,1)S(1)} async-done(((bf16[32,128,128]{2,1,0:T(8,128)(2,1)}), bf16[32,128,128]{2,1,0:T(8,128)(2,1)S(1)}, u32[]{:S(2)}, u32[]{:S(2)}) %all-to-all-start.2) | async-done | bytes 1048608 | tf_op jit(solution)/shard_map/sums_over_high/all_to_all | solution.py:411
  146.4 0.9 add_sources.1
  147.2 9.3 %all-to-all-start.3 = ((bf16[16,64,128]{2,1,0:T(8,128)(2,1)}), bf16[16,64,128]{2,1,0:T(8,128)(2,1)}, u32[]{:S(2)}, u32[]{:S(2)}) async-start(bf16[16,64,128]{2,1,0:T(8,128)(2,1)} %add_sources.1), calls=%async_computation.3 | async-start | bytes 524288 | tf_op jit(solution)/shard_map/sums_to_owners/all_to_all | solution.py:421
  156.5 2.5 %join.1 = (bf16[512,256]{1,0:T(8,128)(2,1)S(1)}, bf16[512,256]{1,0:T(8,128)(2,1)S(1)}, bf16[512,256]{1,0:T(8,128)(2,1)S(1)}, bf16[512,256]{1,0:T(8,128)(2,1)S(1)}) custom-call(f32[4,512,256]{2,1,0:T(8,128)S(1)} %get-tuple-element.15.mine_ref, f32[4,512,256]{2,1,0:T(8,128)} %collective-permute-done.1.theirs_ref), custom_call_target="tpu_custom_call" | custom-call | flops 1000 | bytes 1000 | tf_op jit(solution)/shard_map/pooling/join/pallas_call | solution.py:305
  159.1 3.4 %collective-permute-start.2 = (bf16[512,256]{1,0:T(8,128)(2,1)S(1)}, bf16[512,256]{1,0:T(8,128)(2,1)S(1)}, u32[]{:S(2)}, u32[]{:S(2)}) collective-permute-start(bf16[512,256]{1,0:T(8,128)(2,1)S(1)} %get-tuple-element.18), channel_id=1, source_target_pairs={{0,2},{1,3},{2,0},{3,1},{4,6},{5,7},{6,4},{7,5},{8,10},{9,11},{10,... | collective-permute-start | bytes 786440 | tf_op jit(solution)/shard_map/pooling/ppermute | solution.py:384
  162.5 4.3 %collective-permute-start.3 = (bf16[512,256]{1,0:T(8,128)(2,1)S(1)}, bf16[512,256]{1,0:T(8,128)(2,1)S(1)}, u32[]{:S(2)}, u32[]{:S(2)}) collective-permute-start(bf16[512,256]{1,0:T(8,128)(2,1)S(1)} %get-tuple-element.19), channel_id=1, source_target_pairs={{0,4},{1,5},{2,6},{3,7},{4,0},{5,1},{6,2},{7,3},{8,12},{9,13},{10,... | collective-permute-start | bytes 786440 | tf_op jit(solution)/shard_map/pooling/ppermute | solution.py:384
  166.8 2.0 %collective-permute-start.4 = (bf16[512,256]{1,0:T(8,128)(2,1)S(1)}, bf16[512,256]{1,0:T(8,128)(2,1)S(1)}, u32[]{:S(2)}, u32[]{:S(2)}) collective-permute-start(bf16[512,256]{1,0:T(8,128)(2,1)S(1)} %get-tuple-element.20), channel_id=1, source_target_pairs={{0,6},{1,7},{2,4},{3,5},{4,2},{5,3},{6,0},{7,1},{8,14},{9,15},{10,... | collective-permute-start | bytes 786440 | tf_op jit(solution)/shard_map/pooling/ppermute | solution.py:384
  168.9 7.7 %collective-permute-done.3.refs_2_ = bf16[512,256]{1,0:T(8,128)(2,1)S(1)} collective-permute-done((bf16[512,256]{1,0:T(8,128)(2,1)S(1)}, bf16[512,256]{1,0:T(8,128)(2,1)S(1)}, u32[]{:S(2)}, u32[]{:S(2)}) %collective-permute-start.3) | collective-permute-done | bytes 262176 | tf_op jit(solution)/shard_map/pooling/ppermute | solution.py:384
  176.6 6.3 %collective-permute-done.4.refs_3_ = bf16[512,256]{1,0:T(8,128)(2,1)S(1)} collective-permute-done((bf16[512,256]{1,0:T(8,128)(2,1)S(1)}, bf16[512,256]{1,0:T(8,128)(2,1)S(1)}, u32[]{:S(2)}, u32[]{:S(2)}) %collective-permute-start.4) | collective-permute-done | bytes 262176 | tf_op jit(solution)/shard_map/pooling/ppermute | solution.py:384
  182.9 2.6 %cross_layers.1 = bf16[512,512]{1,0:T(8,128)(2,1)} custom-call(bf16[512,256]{1,0:T(8,128)(2,1)S(1)} %get-tuple-element.17.refs_0_, bf16[512,256]{1,0:T(8,128)(2,1)S(1)} %collective-permute-done.2.refs_1_, bf16[512,256]{1,0:T(8,128)(2,1)S(1)} %collective-permute-done.3.refs_2_, bf16[512,256]{1,0:T(8,128)(2,1)S(1)} %collective-permute-done.4.refs_3_, ...), custom_call_target="tpu_custom_call" | custom-call | flops 1000 | bytes 1000 | tf_op jit(solution)/shard_map/cross/cross_layers/pallas_call | solution.py:340
  185.5 1.2 fusion
  187.8 0.9 fusion.1
  (33 shorter events, 2.0 us)
Async XLA Ops:
  8.2 9.6 %collective-permute-start = (bf16[4,256,128]{1,2,0:T(8,128)(2,1)S(1)}, bf16[4,256,128]{1,2,0:T(8,128)(2,1)S(1)}, u32[]{:S(2)}, u32[]{:S(2)}) collective-permute-start(bf16[4,256,128]{1,2,0:T(8,128)(2,1)S(1)} %bitcast.44), channel_id=1, source_target_pairs={{0,0},{1,9},{2,18},{3,27},{4,36},{5,45},{6,54},{7,63},{8,73},{9,64... | collective-permute-start | bytes 786440 | tf_op jit(solution)/shard_map/table_gather/ppermute | solution.py:395
  13.0 0.9 copy-start.4
  13.9 0.9 copy-start.5
  14.8 0.8 copy-start.6
  17.8 40.9 %all-to-all-start = ((bf16[32,2,16,128]{3,2,1,0:T(8,128)(2,1)}), bf16[32,2,16,128]{3,2,1,0:T(8,128)(2,1)S(1)}, u32[]{:S(2)}, u32[]{:S(2)}) async-start(bf16[32,2,16,128]{3,2,1,0:T(8,128)(2,1)} %bitcast.13), calls=%async_computation | async-start | bytes 524288 | tf_op jit(solution)/shard_map/bags_over_high/all_to_all | solution.py:402
  46.9 1.7 copy-start
  48.6 10.1 %copy-start.8 = (s32[1,40,1]{1,2,0:T(1,128)S(1)}, s32[1,40,1]{1,2,0:T(1,128)}, u32[]{:S(2)}) copy-start(s32[1,40,1]{1,2,0:T(1,128)} %param.22) | copy-start | bytes 484
  48.6 10.1 %copy-start.9 = (s32[1,40]{1,0:T(1,128)S(1)}, s32[1,40]{1,0:T(1,128)}, u32[]{:S(2)}) copy-start(s32[1,40]{1,0:T(1,128)} %numbers_ref.1) | copy-start | bytes 484
  60.0 45.5 %all-to-all-start.1 = ((bf16[16,45,16,128]{3,2,1,0:T(8,128)(2,1)}), bf16[16,45,16,128]{3,2,1,0:T(8,128)(2,1)S(1)}, u32[]{:S(2)}, u32[]{:S(2)}) async-start(bf16[16,45,16,128]{3,2,1,0:T(8,128)(2,1)} %add_bags.1), calls=%async_computation.1 | async-start | bytes 5898240 | tf_op jit(solution)/shard_map/parts_over_low/all_to_all | solution.py:407
  68.2 45.8 %all-gather.3.cloned.1.call-start = ((), (), s32[]{:S(2)}) async-start(), calls=%async_computation.4 | async-start | bytes 2359296 | tf_op jit(solution)/shard_map/table_gather/all_gather | solution.py:396
  108.5 1.0 copy-start.2
  109.5 36.9 %all-to-all-start.2 = ((bf16[32,128,128]{2,1,0:T(8,128)(2,1)}), bf16[32,128,128]{2,1,0:T(8,128)(2,1)S(1)}, u32[]{:S(2)}, u32[]{:S(2)}) async-start(bf16[32,128,128]{2,1,0:T(8,128)(2,1)} %copy-done.2), calls=%async_computation.2 | async-start | bytes 2097152 | tf_op jit(solution)/shard_map/sums_over_high/all_to_all | solution.py:411
  124.9 31.6 %collective-permute-start.1 = (f32[4,512,256]{2,1,0:T(8,128)}, f32[4,512,256]{2,1,0:T(8,128)}, u32[]{:S(2)}, u32[]{:S(2)}) collective-permute-start(f32[4,512,256]{2,1,0:T(8,128)} %get-tuple-element.16), channel_id=1, source_target_pairs={{0,1},{1,0},{2,3},{3,2},{4,5},{5,4},{6,7},{7,6},{8,9},{9,8},{10,11... | collective-permute-start | bytes 6291464 | tf_op jit(solution)/shard_map/pooling/ppermute | solution.py:384
  147.2 35.7 %copy-start.1 = (bf16[2,512,512]{2,1,0:T(8,128)(2,1)S(1)}, bf16[2,512,512]{2,1,0:T(8,128)(2,1)}, u32[]{:S(2)}) copy-start(bf16[2,512,512]{2,1,0:T(8,128)(2,1)} %refs_5_.1) | copy-start | bytes 3145732
  147.2 35.7 %copy-start.3 = (bf16[1,512,256]{2,1,0:T(8,128)(2,1)S(1)}, bf16[1,512,256]{2,1,0:T(8,128)(2,1)}, u32[]{:S(2)}) copy-start(bf16[1,512,256]{2,1,0:T(8,128)(2,1)} %param.18) | copy-start | bytes 786436
  147.2 35.7 %copy-start.7 = (f32[2,512]{1,0:T(2,128)S(1)}, f32[2,512]{1,0:T(2,128)}, u32[]{:S(2)}) copy-start(f32[2,512]{1,0:T(2,128)} %refs_6_.1) | copy-start | bytes 12292
  147.2 38.3 %all-to-all-start.3 = ((bf16[16,64,128]{2,1,0:T(8,128)(2,1)}), bf16[16,64,128]{2,1,0:T(8,128)(2,1)}, u32[]{:S(2)}, u32[]{:S(2)}) async-start(bf16[16,64,128]{2,1,0:T(8,128)(2,1)} %add_sources.1), calls=%async_computation.3 | async-start | bytes 524288 | tf_op jit(solution)/shard_map/sums_to_owners/all_to_all | solution.py:421
  159.1 28.2 %copy-start.11 = (f32[512]{0:T(512)S(1)}, f32[512]{0:T(512)}, u32[]{:S(2)}) copy-start(f32[512]{0:T(512)} %param.13) | copy-start | bytes 6148
  159.1 28.8 %copy-start.10 = (f32[512,256]{1,0:T(8,128)S(1)}, f32[512,256]{1,0:T(8,128)}, u32[]{:S(2)}) copy-start(f32[512,256]{1,0:T(8,128)} %param.12) | copy-start | bytes 1572868
  159.1 9.8 %collective-permute-start.2 = (bf16[512,256]{1,0:T(8,128)(2,1)S(1)}, bf16[512,256]{1,0:T(8,128)(2,1)S(1)}, u32[]{:S(2)}, u32[]{:S(2)}) collective-permute-start(bf16[512,256]{1,0:T(8,128)(2,1)S(1)} %get-tuple-element.18), channel_id=1, source_target_pairs={{0,2},{1,3},{2,0},{3,1},{4,6},{5,7},{6,4},{7,5},{8,10},{9,11},{10,... | collective-permute-start | bytes 786440 | tf_op jit(solution)/shard_map/pooling/ppermute | solution.py:384
  162.5 14.1 %collective-permute-start.3 = (bf16[512,256]{1,0:T(8,128)(2,1)S(1)}, bf16[512,256]{1,0:T(8,128)(2,1)S(1)}, u32[]{:S(2)}, u32[]{:S(2)}) collective-permute-start(bf16[512,256]{1,0:T(8,128)(2,1)S(1)} %get-tuple-element.19), channel_id=1, source_target_pairs={{0,4},{1,5},{2,6},{3,7},{4,0},{5,1},{6,2},{7,3},{8,12},{9,13},{10,... | collective-permute-start | bytes 786440 | tf_op jit(solution)/shard_map/pooling/ppermute | solution.py:384
  166.8 16.1 %collective-permute-start.4 = (bf16[512,256]{1,0:T(8,128)(2,1)S(1)}, bf16[512,256]{1,0:T(8,128)(2,1)S(1)}, u32[]{:S(2)}, u32[]{:S(2)}) collective-permute-start(bf16[512,256]{1,0:T(8,128)(2,1)S(1)} %get-tuple-element.20), channel_id=1, source_target_pairs={{0,6},{1,7},{2,4},{3,5},{4,2},{5,3},{6,0},{7,1},{8,14},{9,15},{10,... | collective-permute-start | bytes 786440 | tf_op jit(solution)/shard_map/pooling/ppermute | solution.py:384
Sparse Core Ops, SparseCore 0:
  71.7 34.4 all-gather.2

commit v8 on v7

--- a/solution.py
+++ b/solution.py
@@ -7,6 +7,7 @@
 from jax.sharding import PartitionSpec as P
 
 VMEM_LIMIT = 48 * 1024 * 1024
+ALL_VMEM = 60 * 1024 * 1024
 learn_rate = 0.3
 TILE = 16
 SMALL = pl.CostEstimate(flops=1000, bytes_accessed=1000, transcendentals=0)
@@ -18,17 +19,61 @@
 SIDE = 8
 
 
-def adagrad(gradient, old_accum, old_table):
-    fresh_accum = old_accum + jnp.mean(gradient * gradient, axis=1)
-    fresh_table = old_table - learn_rate * gradient / jnp.sqrt(fresh_accum)[:, None]
-    return (fresh_table, fresh_accum)
+def adagrad(grads, accum, table):
+    sources, rows, lanes = grads.shape
+    slab_rows, width = table.shape
+    sides = width // lanes
+    block_count = rows // TILE
+    block_rows = slab_rows // block_count
+
+    def kernel(grads_ref, accum_ref, table_ref, new_table_ref, new_accum_ref):
+        block = pl.program_id(0)
+        gradient = jnp.concatenate(
+            [
+                jnp.concatenate([grads_ref[t + h].astype(jnp.float32) for h in range(sides)], axis=1)
+                for t in range(0, sources, sides)
+            ],
+            axis=0,
+        )
+        mean = jnp.sum(gradient * gradient, axis=1, keepdims=True) * (1.0 / width)
+        old = jnp.broadcast_to(accum_ref[pl.ds(block, 1), :], (block_rows, lanes)).T
+        fresh = old + mean
+        new_accum_ref[pl.ds(block, 1), :] = fresh.T[0:1]
+        root = jnp.sqrt(fresh)
+        for h in range(sides):
+            at = slice(h * lanes, (h + 1) * lanes)
+            new_table_ref[:, at] = table_ref[:, at] - learn_rate * gradient[:, at] / root
+
+    return pl.pallas_call(
+        kernel,
+        out_shape=[
+            jax.ShapeDtypeStruct((slab_rows, width), jnp.float32),
+            jax.ShapeDtypeStruct((block_count, lanes), jnp.float32),
+        ],
+        grid=(block_count,),
+        in_specs=[
+            pl.BlockSpec((sources, TILE, lanes), lambda i: (0, i, 0)),
+            pl.BlockSpec((block_count, lanes), lambda i: (0, 0)),
+            pl.BlockSpec((block_rows, width), lambda i: (i, 0)),
+        ],
+        out_specs=[
+            pl.BlockSpec((block_rows, width), lambda i: (i, 0)),
+            pl.BlockSpec((block_count, lanes), lambda i: (0, 0)),
+        ],
+        compiler_params=pltpu.CompilerParams(
+            dimension_semantics=("arbitrary",), vmem_limit_bytes=VMEM_LIMIT
+        ),
+        cost_estimate=SMALL,
+        name="adagrad",
+    )(grads, accum, table)
 
 
 def pack_bags(blocks, entries, weights, targets):
-    per_tile, owner_count = blocks.shape
+    per_tile, _, owner_count = blocks.shape
     lanes = entries.shape[1] // owner_count
     entry_count = entries.shape[0]
     span = per_tile * lanes // entry_count
+    group = owner_count // 4
 
     def kernel(blocks_ref, entries_ref, weights_ref, targets_ref, out_ref):
         shift = lax.broadcasted_iota(jnp.int32, (entry_count, lanes), 0) * span
@@ -36,11 +81,12 @@
 
         def bags(e, carry):
             for u in range(4):
-                d = 4 * e + u
-                at = pl.ds(pl.multiple_of(d * lanes, lanes), lanes)
+                i = 4 * e + u
+                d = pl.program_id(0) * group + i
+                at = pl.ds(pl.multiple_of(i * lanes, lanes), lanes)
                 chosen = jnp.zeros((1, lanes), jnp.int32)
                 for b in range(per_tile):
-                    chosen = jnp.where(lane == b, blocks_ref[b, d], chosen)
+                    chosen = jnp.where(lane == b, blocks_ref[b, 0, d], chosen)
                 bag = jnp.concatenate(
                     [
                         (entries_ref[:, at] - shift).astype(jnp.float32),
@@ -51,18 +97,25 @@
                     ],
                     axis=0,
                 )
-                out_ref[d] = bag.astype(out_ref.dtype)
+                out_ref[i] = bag.astype(out_ref.dtype)
             return carry
 
-        lax.fori_loop(0, owner_count // 4, bags, 0)
-
-    whole = pl.BlockSpec(memory_space=pltpu.VMEM)
+        lax.fori_loop(0, group // 4, bags, 0)
+
     return pl.pallas_call(
         kernel,
         out_shape=jax.ShapeDtypeStruct((owner_count, TILE, lanes), jnp.bfloat16),
-        in_specs=[pl.BlockSpec(memory_space=pltpu.SMEM)] + [whole] * 3,
-        out_specs=whole,
-        compiler_params=pltpu.CompilerParams(vmem_limit_bytes=VMEM_LIMIT),
+        grid=(owner_count // group,),
+        in_specs=[
+            pl.BlockSpec(memory_space=pltpu.SMEM),
+            pl.BlockSpec((entry_count, group * lanes), lambda i: (0, i)),
+            pl.BlockSpec((entry_count, group * lanes), lambda i: (0, i)),
+            pl.BlockSpec((1, group * lanes), lambda i: (0, i)),
+        ],
+        out_specs=pl.BlockSpec((group, TILE, lanes), lambda i: (i, 0, 0)),
+        compiler_params=pltpu.CompilerParams(
+            dimension_semantics=("arbitrary",), vmem_limit_bytes=ALL_VMEM
+        ),
         cost_estimate=SMALL,
         name="pack_bags",
     )(blocks, entries, weights, targets)
@@ -108,10 +161,10 @@
         slots = row_ref[...].astype(out_ref.dtype)
         for t in range(receivers):
             u, j = t // parts, t % parts
-            z = j ^ (place_ref[2] + u)
+            group = (j + parts - place_ref[1] - u) % parts
             out_ref[t, 0] = slots
             for b in range(kept):
-                out_ref[t, 1 + b] = bags_ref[z * kept + b, u]
+                out_ref[t, 1 + b] = bags_ref[(2 * b + group % 2) * kept + group // 2, u]
 
     whole = pl.BlockSpec(memory_space=pltpu.VMEM)
     return pl.pallas_call(
@@ -209,7 +262,7 @@
     )(received)
 
 
-def pool_parts(place, table, bags):
+def pool_parts(first, kind, place, table, bags):
     owner_count, block_count, width, lanes = table.shape
     parts = bags.shape[0]
     many = parts // 2
@@ -218,9 +271,9 @@
     span = per_tile * lanes // entry_count
     samples = SAMPLES
 
-    def kernel(place_ref, table_ref, bags_ref, others_ref, mine_ref, numbers_ref, blocks_ref, sem):
+    def kernel(place_ref, table_ref, bags_ref, out_ref, numbers_ref, blocks_ref, sem):
         step = pl.program_id(0)
-        replica = place_ref[0] ^ jnp.where(step < many, 2 * step + 1, 2 * (step - many))
+        replica = place_ref[0] ^ (2 * step + first)
 
         @pl.when(step == 0)
         def _():
@@ -249,37 +302,25 @@
                 axis=0,
             ).astype(jnp.bfloat16)
             chosen = [blocks_ref[replica * owner_count + p, j] for j in range(per_tile)]
-            owner = p ^ place_ref[1]
-            slab = jnp.concatenate([table_ref[owner, b] for b in chosen], axis=1)
+            slab = jnp.concatenate([table_ref[p, b] for b in chosen], axis=1)
             partials.append(
                 jnp.dot(slab, incidence, preferred_element_type=jnp.float32).astype(jnp.bfloat16)
             )
         selector = jnp.where(sample == jnp.concatenate(targets, axis=1), 1.0, 0.0).astype(jnp.bfloat16)
-        pooled = lax.dot_general(
+        out_ref[0] = lax.dot_general(
             selector,
             jnp.concatenate(partials, axis=1),
             (((1,), (1,)), ((), ())),
             preferred_element_type=jnp.float32,
-        )
-
-        @pl.when(step < many)
-        def _():
-            others_ref[0] = pooled
-
-        @pl.when(step >= many)
-        def _():
-            mine_ref[0] = pooled
+        ).astype(kind)
 
     whole = pl.BlockSpec(memory_space=pltpu.VMEM)
     return pl.pallas_call(
         kernel,
-        out_shape=[jax.ShapeDtypeStruct((many, samples, width), jnp.float32)] * 2,
-        grid=(parts,),
+        out_shape=jax.ShapeDtypeStruct((many, samples, width), kind),
+        grid=(many,),
         in_specs=[pl.BlockSpec(memory_space=pltpu.SMEM), whole, whole],
-        out_specs=[
-            pl.BlockSpec((1, samples, width), lambda i: (jnp.minimum(i, many - 1), 0, 0)),
-            pl.BlockSpec((1, samples, width), lambda i: (jnp.maximum(i - many, 0), 0, 0)),
-        ],
+        out_specs=pl.BlockSpec((1, samples, width), lambda i: (i, 0, 0)),
         scratch_shapes=[
             pltpu.VMEM((parts * owner_count, lanes), jnp.int32),
             pltpu.SMEM((parts * owner_count, lanes), jnp.int32),
@@ -299,7 +340,7 @@
 
     def kernel(mine_ref, theirs_ref, *out_refs):
         for i in range(many):
-            out_refs[i][...] = (mine_ref[i] + theirs_ref[i]).astype(jnp.bfloat16)
+            out_refs[i][...] = (mine_ref[i] + theirs_ref[i].astype(jnp.float32)).astype(jnp.bfloat16)
 
     block = pl.BlockSpec((many, tile, width), lambda i: (0, i, 0))
     return pl.pallas_call(
@@ -378,7 +419,7 @@
     lows = lax.axis_size("yl")
     me = lax.axis_index("replica").astype(jnp.int32)
     y = lax.axis_index(("yh", "yl")).astype(jnp.int32)
-    place = jnp.stack([me, me ^ y, y - y % lows])
+    place = jnp.stack([me, y - y % lows])
 
     def to_replica(array, k):
         return lax.ppermute(array, "replica", [(r, r ^ k) for r in range(parts)])
@@ -388,18 +429,17 @@
         slab = slab.reshape(block_count, block_rows, width).transpose(0, 2, 1)
         moves = []
         for owner in range(SIDE * SIDE):
-            own_z, own_y = owner // SIDE, owner % SIDE
-            for r in range(parts):
-                to_z, to_y = own_y ^ own_z, own_y ^ r
-                moves.append((owner * parts + r, (to_z * SIDE + to_y) * parts + (own_z ^ to_y)))
+            z, y_own = owner // SIDE, owner % SIDE
+            to_z, group = z // 2 * 2 + y_own % 2, y_own // 2 * 2 + z % 2
+            moves += [(owner * parts + r, (to_z * SIDE + (r - group) % SIDE) * parts + r) for r in range(parts)]
         moved = lax.ppermute(slab, (*MP, "replica"), moves)
         slabs = lax.all_gather(moved, "z", axis=0)
 
     with jax.named_scope("bags_over_high"):
-        bags = pack_bags(bag_blocks[0].T, bag_entries[0].T, bag_weights[0].T, bag_target)
-        bags, _ = lax.optimization_barrier((bags, moved))
+        bags = pack_bags(bag_blocks.transpose(2, 0, 1), bag_entries[0].T, bag_weights[0].T, bag_target)
         bags = bags.reshape(highs, lows, TILE, bags.shape[2])
         bags = lax.all_to_all(bags, HIGHS, split_axis=0, concat_axis=0, tiled=True)
+        bags, _ = lax.optimization_barrier((bags, moved))
 
     with jax.named_scope("parts_over_low"):
         packed = pack_parts(evict_grads[0])
@@ -411,24 +451,19 @@
         received = lax.all_to_all(sums, HIGHS, split_axis=0, concat_axis=0, tiled=True)
 
     with jax.named_scope("pooling"):
-        others, mine = pool_parts(place, slabs, bags)
+        others = pool_parts(1, jnp.bfloat16, place, slabs, bags)
+        mine = pool_parts(0, jnp.float32, place, slabs, bags)
         joined = join(mine, to_replica(others, 1))
-        pooled = [joined[0]] + [to_replica(joined[i], 2 * i) for i in range(1, parts // 2)]
+        pooled = [joined[0]] + [to_replica(joined[i], 2 * i) for i in (2, 3, 1)]
 
     with jax.named_scope("sums_to_owners"):
-        received, _ = lax.optimization_barrier((received, others))
+        received, _ = lax.optimization_barrier((received, pooled))
         shared = add_sources(received, lows, parts)
         grads = lax.all_to_all(shared, LOWS, split_axis=0, concat_axis=0, tiled=True)
 
     with jax.named_scope("table_update"):
-        lanes = shared.shape[2]
-        table_grad = (
-            grads.reshape(block_rows // TILE, width // lanes, block_count, TILE, lanes)
-            .transpose(2, 0, 3, 1, 4)
-            .reshape(slab_rows, width)
-            .astype(jnp.float32)
-        )
-        new_table, new_accum = adagrad(table_grad, accum, table)
+        new_table, new_accum = adagrad(grads, accum.reshape(block_count, block_rows), table)
+        new_accum = new_accum.reshape(slab_rows)
 
     with jax.named_scope("cross"):
         cross_out = cross_layers(pooled, other_feats[0], cross_w, cross_b)

time: 196 us -> 167 us (0.85)
  waiting for transfers between devices: 76.3 us -> 50.8 us
  starting transfers between devices: 67.6 us -> 64.6 us
  other arithmetic: 3.85 us -> 1.15 us
    all_to_all x1, waiting for transfers between devices: 18.6 us -> 0.01 us  [local(): lax.all_to_all(sums, HIGHS, split_axis=0, concat_axis=0, tiled=True)]
    all_to_all x1, starting transfers between devices: 29 us -> 16.5 us  [local(): bags = lax.all_to_all(bags, HIGHS, split_axis=0, concat_axis=0, tiled=True)]
    all_to_all x1, starting transfers between devices: 8.18 us -> 15.8 us  [local(): lax.all_to_all(sent, LOWS, split_axis=0, concat_axis=0, tiled=True)]
    ppermute x4, waiting for transfers between devices: 14.1 us -> 7.54 us  [to_replica(): return lax.ppermute(array, 'replica', [(r, r ^ k) for r in range(parts)])]
    all_to_all x1, waiting for transfers between devices: 6.48 us -> 0.32 us  [local(): bags = lax.all_to_all(bags, HIGHS, split_axis=0, concat_axis=0, tiled=True)]
    ppermute x4, starting transfers between devices: 12.5 us -> 16.6 us  [to_replica(): return lax.ppermute(array, 'replica', [(r, r ^ k) for r in range(parts)])]
    all_to_all x1, starting transfers between devices: 9.32 us -> 5.92 us  [local(): lax.all_to_all(shared, LOWS, split_axis=0, concat_axis=0, tiled=True)]
    ppermute x1, waiting for transfers between devices: 0.62 us -> 3.77 us  [local(): moved = lax.ppermute(slab, (*MP, 'replica'), moves)]
  transfers between devices with their start and end apart: 10 -> 10, of which waited for: 6 -> 5; matrix products, arithmetic and copies ran while one was open for 1% -> 1% of each run, Pallas kernels for 13% -> 12%
where the time goes in v8:
time: 167 us; the launch traced here: 166 us
  starting transfers between devices  64.6 us (39%)
  waiting for transfers between devices  50.8 us (30%)
  Pallas kernels  27.1 us (16%)
  between operations  14.3 us (9%)
  local copies, waits for them, and re-layouts  8.48 us (5%)
    all_to_all x1, waiting for transfers between devices, local(): lax.all_to_all(sent, LOWS, split_axis=0, concat_axis=0, tiled=True)  36.5 us
    ppermute x4, starting transfers between devices, to_replica(): return lax.ppermute(array, 'replica', [(r, r ^ k) for r in range(parts)])  16.6 us
    all_to_all x1, starting transfers between devices, local(): bags = lax.all_to_all(bags, HIGHS, split_axis=0, concat_axis=0, tiled=True)  16.5 us
    all_to_all x1, starting transfers between devices, local(): lax.all_to_all(sent, LOWS, split_axis=0, concat_axis=0, tiled=True)  15.8 us
    pallas_call x2, Pallas kernels, pool_parts(): pl.pallas_call(kernel, out_shape=jax.ShapeDtypeStruct((many, samples, wid...  10.3 us
    unnamed x28, local copies, waits for them, and re-layouts  7.63 us
    ppermute x4, waiting for transfers between devices, to_replica(): return lax.ppermute(array, 'replica', [(r, r ^ k) for r in range(parts)])  7.54 us
    all_to_all x1, starting transfers between devices, local(): lax.all_to_all(sums, HIGHS, split_axis=0, concat_axis=0, tiled=True)  7.33 us
  transfers between devices with their start and end apart: 10, of which 5 were waited for; matrix products, arithmetic and copies ran while one was open for 1% of the time, Pallas kernels for 12%

profile of v8, /device:TPU:1, one launch (start us, length us, event | category | flops | bytes accessed | tf_op | source)
XLA Modules:
  0.0 166.4 jit_solution(14321806293361968082)
XLA Ops:
  7.2 3.1 %pack_bags.1 = bf16[64,16,128]{2,1,0:T(8,128)(2,1)} custom-call(s32[3,1,64]{2,1,0:T(1,128)} %bitcast.31, s32[4,8192]{1,0:T(4,128)} %bitcast.29, f32[4,8192]{1,0:T(4,128)} %bitcast.30, s32[1,8192]{1,0:T(1,128)} %targets_ref.1), custom_call_target="tpu_custom_call" | custom-call | flops 1000 | bytes 1000 | tf_op jit(solution)/shard_map/bags_over_high/pack_bags/pallas_call | solution.py:105
  10.3 16.5 %all-to-all-start = ((bf16[32,2,16,128]{3,2,1,0:T(8,128)(2,1)}), bf16[32,2,16,128]{3,2,1,0:T(8,128)(2,1)S(1)}, u32[]{:S(2)}, u32[]{:S(2)}) async-start(bf16[32,2,16,128]{3,2,1,0:T(8,128)(2,1)} %bitcast.26), calls=%async_computation | async-start | bytes 524288 | tf_op jit(solution)/shard_map/bags_over_high/all_to_all | solution.py:441
  26.8 1.1 convert_element_type.3
  27.9 2.3 %collective-permute-start = (bf16[4,256,128]{1,2,0:T(8,128)(2,1)S(1)}, bf16[4,256,128]{1,2,0:T(8,128)(2,1)S(1)}, u32[]{:S(2)}, u32[]{:S(2)}) collective-permute-start(bf16[4,256,128]{1,2,0:T(8,128)(2,1)S(1)} %bitcast.28), channel_id=1, source_target_pairs={{0,0},{1,9},{2,18},{3,27},{4,36},{5,45},{6,54},{7,63},{8,64},{9,73... | collective-permute-start | bytes 786440 | tf_op jit(solution)/shard_map/table_gather/ppermute | solution.py:435
  30.3 1.7 %copy-done.1 = bf16[1,40,128,256]{3,2,1,0:T(8,128)(2,1)S(1)} copy-done((bf16[1,40,128,256]{3,2,1,0:T(8,128)(2,1)S(1)}, bf16[1,40,128,256]{3,2,1,0:T(8,128)(2,1)}, u32[]{:S(2)}) %copy-start.1) | copy-done | bytes 2621464
  32.0 3.5 %pack_parts.1.packed_ref = bf16[16,45,16,128]{3,2,1,0:T(8,128)(2,1)} custom-call(bf16[40,128,256]{2,1,0:T(8,128)(2,1)S(1)} %bitcast.22), custom_call_target="tpu_custom_call" | custom-call | flops 1000 | bytes 1000 | tf_op jit(solution)/shard_map/parts_over_low/pack_parts/pallas_call | solution.py:139
  35.6 3.8 %collective-permute-done = bf16[4,256,128]{1,2,0:T(8,128)(2,1)S(1)} collective-permute-done((bf16[4,256,128]{1,2,0:T(8,128)(2,1)S(1)}, bf16[4,256,128]{1,2,0:T(8,128)(2,1)S(1)}, u32[]{:S(2)}, u32[]{:S(2)}) %collective-permute-start) | collective-permute-done | bytes 262176 | tf_op jit(solution)/shard_map/table_gather/ppermute | solution.py:435
  39.7 1.4 add_bags.1
  41.1 15.8 %all-to-all-start.1 = ((bf16[16,45,16,128]{3,2,1,0:T(8,128)(2,1)}), bf16[16,45,16,128]{3,2,1,0:T(8,128)(2,1)S(1)}, u32[]{:S(2)}, u32[]{:S(2)}) async-start(bf16[16,45,16,128]{3,2,1,0:T(8,128)(2,1)} %add_bags.1), calls=%async_computation.1 | async-start | bytes 5898240 | tf_op jit(solution)/shard_map/parts_over_low/all_to_all | solution.py:447
  57.0 0.8 copy.17
  57.9 36.5 %all-to-all-done.1.recv_ref = bf16[16,45,16,128]{3,2,1,0:T(8,128)(2,1)S(1)} async-done(((bf16[16,45,16,128]{3,2,1,0:T(8,128)(2,1)}), bf16[16,45,16,128]{3,2,1,0:T(8,128)(2,1)S(1)}, u32[]{:S(2)}, u32[]{:S(2)}) %all-to-all-start.1) | async-done | bytes 2949152 | tf_op jit(solution)/shard_map/parts_over_low/all_to_all | solution.py:447
  94.3 2.9 %add_parts.1 = (bf16[32,128,128]{2,1,0:T(8,128)(2,1)S(1)}, bf16[8,8,16,128]{3,2,1,0:T(8,128)(2,1)S(1)}) custom-call(bf16[16,45,16,128]{3,2,1,0:T(8,128)(2,1)S(1)} %all-to-all-done.1.recv_ref), custom_call_target="tpu_custom_call" | custom-call | flops 1000 | bytes 1000 | tf_op jit(solution)/shard_map/sums_over_high/add_parts/pallas_call | solution.py:217
  97.3 1.0 copy-done.4
  98.3 7.3 %all-to-all-start.2 = ((bf16[32,128,128]{2,1,0:T(8,128)(2,1)}), bf16[32,128,128]{2,1,0:T(8,128)(2,1)S(1)}, u32[]{:S(2)}, u32[]{:S(2)}) async-start(bf16[32,128,128]{2,1,0:T(8,128)(2,1)} %copy-done.4), calls=%async_computation.2 | async-start | bytes 2097152 | tf_op jit(solution)/shard_map/sums_over_high/all_to_all | solution.py:451
  105.6 1.6 copy-done
  107.2 5.1 %pool_parts.3 = bf16[4,512,256]{2,1,0:T(8,128)(2,1)S(1)} custom-call(s32[2]{0:T(128)S(1)} %pad_add_fusion.place_ref, bf16[8,4,256,128]{3,2,1,0:T(8,128)(2,1)S(1)} %bitcast.20, bf16[8,8,16,128]{3,2,1,0:T(8,128)(2,1)S(1)} %get-tuple-element.14.bags_ref), custom_call_target="tpu_custom_call" | custom-call | flops 1000 | bytes 1000 | tf_op jit(solution)/shard_map/pooling/pool_parts/pallas_call | solution.py:318
  112.4 2.8 %collective-permute-start.1 = (bf16[4,512,256]{2,1,0:T(8,128)(2,1)S(1)}, bf16[4,512,256]{2,1,0:T(8,128)(2,1)S(1)}, u32[]{:S(2)}, u32[]{:S(2)}) collective-permute-start(bf16[4,512,256]{2,1,0:T(8,128)(2,1)S(1)} %pool_parts.3), channel_id=1, source_target_pairs={{0,1},{1,0},{2,3},{3,2},{4,5},{5,4},{6,7},{7,6},{8,9},{9,8},{10,11... | collective-permute-start | bytes 3145736 | tf_op jit(solution)/shard_map/pooling/ppermute | solution.py:425
  115.2 5.2 %pool_parts.2.mine_ref = f32[4,512,256]{2,1,0:T(8,128)S(1)} custom-call(s32[2]{0:T(128)S(1)} %pad_add_fusion.place_ref, bf16[8,4,256,128]{3,2,1,0:T(8,128)(2,1)S(1)} %bitcast.21, bf16[8,8,16,128]{3,2,1,0:T(8,128)(2,1)S(1)} %get-tuple-element.14.bags_ref), custom_call_target="tpu_custom_call" | custom-call | flops 1000 | bytes 1000 | tf_op jit(solution)/shard_map/pooling/pool_parts/pallas_call | solution.py:318
  120.4 0.5 join.1
  120.9 4.9 %collective-permute-start.2 = (bf16[512,256]{1,0:T(8,128)(2,1)S(1)}, bf16[512,256]{1,0:T(8,128)(2,1)S(1)}, u32[]{:S(2)}, u32[]{:S(2)}) collective-permute-start(bf16[512,256]{1,0:T(8,128)(2,1)S(1)} %get-tuple-element.16), channel_id=1, source_target_pairs={{0,4},{1,5},{2,6},{3,7},{4,0},{5,1},{6,2},{7,3},{8,12},{9,13},{10,... | collective-permute-start | bytes 786440 | tf_op jit(solution)/shard_map/pooling/ppermute | solution.py:425
  125.8 6.4 %collective-permute-start.3 = (bf16[512,256]{1,0:T(8,128)(2,1)S(1)}, bf16[512,256]{1,0:T(8,128)(2,1)S(1)}, u32[]{:S(2)}, u32[]{:S(2)}) collective-permute-start(bf16[512,256]{1,0:T(8,128)(2,1)S(1)} %get-tuple-element.17), channel_id=1, source_target_pairs={{0,6},{1,7},{2,4},{3,5},{4,2},{5,3},{6,0},{7,1},{8,14},{9,15},{10,... | collective-permute-start | bytes 786440 | tf_op jit(solution)/shard_map/pooling/ppermute | solution.py:425
  132.3 2.5 %collective-permute-start.4 = (bf16[512,256]{1,0:T(8,128)(2,1)S(1)}, bf16[512,256]{1,0:T(8,128)(2,1)S(1)}, u32[]{:S(2)}, u32[]{:S(2)}) collective-permute-start(bf16[512,256]{1,0:T(8,128)(2,1)S(1)} %get-tuple-element.18), channel_id=1, source_target_pairs={{0,2},{1,3},{2,0},{3,1},{4,6},{5,7},{6,4},{7,5},{8,10},{9,11},{10,... | collective-permute-start | bytes 786440 | tf_op jit(solution)/shard_map/pooling/ppermute | solution.py:425
  134.8 7.5 %collective-permute-done.3.refs_2_ = bf16[512,256]{1,0:T(8,128)(2,1)S(1)} collective-permute-done((bf16[512,256]{1,0:T(8,128)(2,1)S(1)}, bf16[512,256]{1,0:T(8,128)(2,1)S(1)}, u32[]{:S(2)}, u32[]{:S(2)}) %collective-permute-start.3) | collective-permute-done | bytes 262176 | tf_op jit(solution)/shard_map/pooling/ppermute | solution.py:425
  142.3 0.7 copy-done.6
  143.0 0.7 copy-done.8
  143.7 0.8 add_sources.1
  144.5 5.9 %all-to-all-start.3 = ((bf16[16,64,128]{2,1,0:T(8,128)(2,1)}), bf16[16,64,128]{2,1,0:T(8,128)(2,1)S(1)}, u32[]{:S(2)}, u32[]{:S(2)}) async-start(bf16[16,64,128]{2,1,0:T(8,128)(2,1)} %add_sources.1), calls=%async_computation.3 | async-start | bytes 524288 | tf_op jit(solution)/shard_map/sums_to_owners/all_to_all | solution.py:462
  150.5 0.9 copy-done.7
  151.5 0.9 copy-done.9
  152.4 2.6 %cross_layers.1 = bf16[512,512]{1,0:T(8,128)(2,1)} custom-call(bf16[512,256]{1,0:T(8,128)(2,1)S(1)} %get-tuple-element.15.refs_0_, bf16[512,256]{1,0:T(8,128)(2,1)S(1)} %collective-permute-done.2.refs_1_, bf16[512,256]{1,0:T(8,128)(2,1)S(1)} %copy-done.7, bf16[512,256]{1,0:T(8,128)(2,1)S(1)} %copy-done.9, bf16[512,256]{1,0:T(8,128)(2,1)S(1)} %bitcast.23, ...), custom_call_target="tpu_custom_call" | custom-call | flops 1000 | bytes 1000 | tf_op jit(solution)/shard_map/cross/cross_layers/pallas_call | solution.py:381
  155.0 2.7 %all-to-all-done.3.grads_ref = bf16[16,64,128]{2,1,0:T(8,128)(2,1)S(1)} async-done(((bf16[16,64,128]{2,1,0:T(8,128)(2,1)}), bf16[16,64,128]{2,1,0:T(8,128)(2,1)S(1)}, u32[]{:S(2)}, u32[]{:S(2)}) %all-to-all-start.3) | async-done | bytes 262176 | tf_op jit(solution)/shard_map/sums_to_owners/all_to_all | solution.py:462
  157.6 1.9 %adagrad.1 = (f32[512,256]{1,0:T(8,128)}, f32[4,128]{1,0:T(4,128)}) custom-call(bf16[16,64,128]{2,1,0:T(8,128)(2,1)S(1)} %all-to-all-done.3.grads_ref, f32[4,128]{1,0:T(4,128)S(1)} %bitcast.24, f32[512,256]{1,0:T(8,128)S(1)} %copy-done.2), custom_call_target="tpu_custom_call" | custom-call | flops 1000 | bytes 1000 | tf_op jit(solution)/shard_map/table_update/adagrad/pallas_call | solution.py:47
  (30 shorter events, 0.5 us)
Async XLA Ops:
  10.3 29.4 %all-to-all-start = ((bf16[32,2,16,128]{3,2,1,0:T(8,128)(2,1)}), bf16[32,2,16,128]{3,2,1,0:T(8,128)(2,1)S(1)}, u32[]{:S(2)}, u32[]{:S(2)}) async-start(bf16[32,2,16,128]{3,2,1,0:T(8,128)(2,1)} %bitcast.26), calls=%async_computation | async-start | bytes 524288 | tf_op jit(solution)/shard_map/bags_over_high/all_to_all | solution.py:441
  27.9 11.8 %copy-start.12 = (s32[1,40,1]{1,2,0:T(1,128)S(1)}, s32[1,40,1]{1,2,0:T(1,128)}, u32[]{:S(2)}) copy-start(s32[1,40,1]{1,2,0:T(1,128)} %param.22) | copy-start | bytes 484
  27.9 11.7 %copy-start.13 = (s32[1,40]{1,0:T(1,128)S(1)}, s32[1,40]{1,0:T(1,128)}, u32[]{:S(2)}) copy-start(s32[1,40]{1,0:T(1,128)} %numbers_ref.1) | copy-start | bytes 484
  27.9 11.4 %collective-permute-start = (bf16[4,256,128]{1,2,0:T(8,128)(2,1)S(1)}, bf16[4,256,128]{1,2,0:T(8,128)(2,1)S(1)}, u32[]{:S(2)}, u32[]{:S(2)}) collective-permute-start(bf16[4,256,128]{1,2,0:T(8,128)(2,1)S(1)} %bitcast.28), channel_id=1, source_target_pairs={{0,0},{1,9},{2,18},{3,27},{4,36},{5,45},{6,54},{7,63},{8,64},{9,73... | collective-permute-start | bytes 786440 | tf_op jit(solution)/shard_map/table_gather/ppermute | solution.py:435
  30.2 1.7 %copy-start.1 = (bf16[1,40,128,256]{3,2,1,0:T(8,128)(2,1)S(1)}, bf16[1,40,128,256]{3,2,1,0:T(8,128)(2,1)}, u32[]{:S(2)}) copy-start(bf16[1,40,128,256]{3,2,1,0:T(8,128)(2,1)} %param.21) | copy-start | bytes 7864324
  41.1 53.2 %all-to-all-start.1 = ((bf16[16,45,16,128]{3,2,1,0:T(8,128)(2,1)}), bf16[16,45,16,128]{3,2,1,0:T(8,128)(2,1)S(1)}, u32[]{:S(2)}, u32[]{:S(2)}) async-start(bf16[16,45,16,128]{3,2,1,0:T(8,128)(2,1)} %add_bags.1), calls=%async_computation.1 | async-start | bytes 5898240 | tf_op jit(solution)/shard_map/parts_over_low/all_to_all | solution.py:447
  57.0 48.7 %all-gather.3.cloned.1.call-start = ((), (), s32[]{:S(2)}) async-start(), calls=%async_computation.4 | async-start | bytes 2359296 | tf_op jit(solution)/shard_map/table_gather/all_gather | solution.py:436
  97.3 1.0 copy-start.4
  98.3 45.4 %all-to-all-start.2 = ((bf16[32,128,128]{2,1,0:T(8,128)(2,1)}), bf16[32,128,128]{2,1,0:T(8,128)(2,1)S(1)}, u32[]{:S(2)}, u32[]{:S(2)}) async-start(bf16[32,128,128]{2,1,0:T(8,128)(2,1)} %copy-done.4), calls=%async_computation.2 | async-start | bytes 2097152 | tf_op jit(solution)/shard_map/sums_over_high/all_to_all | solution.py:451
  105.6 1.6 copy-start
  112.4 8.0 %collective-permute-start.1 = (bf16[4,512,256]{2,1,0:T(8,128)(2,1)S(1)}, bf16[4,512,256]{2,1,0:T(8,128)(2,1)S(1)}, u32[]{:S(2)}, u32[]{:S(2)}) collective-permute-start(bf16[4,512,256]{2,1,0:T(8,128)(2,1)S(1)} %pool_parts.3), channel_id=1, source_target_pairs={{0,1},{1,0},{2,3},{3,2},{4,5},{5,4},{6,7},{7,6},{8,9},{9,8},{10,11... | collective-permute-start | bytes 3145736 | tf_op jit(solution)/shard_map/pooling/ppermute | solution.py:425
  120.4 30.1 %copy-start.3 = (bf16[2,512,512]{2,1,0:T(8,128)(2,1)S(1)}, bf16[2,512,512]{2,1,0:T(8,128)(2,1)}, u32[]{:S(2)}) copy-start(bf16[2,512,512]{2,1,0:T(8,128)(2,1)} %refs_5_.1) | copy-start | bytes 3145732
  120.4 30.1 %copy-start.5 = (bf16[1,512,256]{2,1,0:T(8,128)(2,1)S(1)}, bf16[1,512,256]{2,1,0:T(8,128)(2,1)}, u32[]{:S(2)}) copy-start(bf16[1,512,256]{2,1,0:T(8,128)(2,1)} %param.18) | copy-start | bytes 786436
  120.4 30.1 %copy-start.10 = (f32[2,512]{1,0:T(2,128)S(1)}, f32[2,512]{1,0:T(2,128)}, u32[]{:S(2)}) copy-start(f32[2,512]{1,0:T(2,128)} %refs_6_.1) | copy-start | bytes 12292
  120.9 36.7 %copy-start.2 = (f32[512,256]{1,0:T(8,128)S(1)}, f32[512,256]{1,0:T(8,128)}, u32[]{:S(2)}) copy-start(f32[512,256]{1,0:T(8,128)} %table_ref.1) | copy-start | bytes 1572868
  120.9 36.7 %copy-start.11 = (f32[512]{0:T(512)S(1)}, f32[512]{0:T(512)}, u32[]{:S(2)}) copy-start(f32[512]{0:T(512)} %param.13) | copy-start | bytes 6148
  120.9 13.8 %collective-permute-start.2 = (bf16[512,256]{1,0:T(8,128)(2,1)S(1)}, bf16[512,256]{1,0:T(8,128)(2,1)S(1)}, u32[]{:S(2)}, u32[]{:S(2)}) collective-permute-start(bf16[512,256]{1,0:T(8,128)(2,1)S(1)} %get-tuple-element.16), channel_id=1, source_target_pairs={{0,4},{1,5},{2,6},{3,7},{4,0},{5,1},{6,2},{7,3},{8,12},{9,13},{10,... | collective-permute-start | bytes 786440 | tf_op jit(solution)/shard_map/pooling/ppermute | solution.py:425
  125.8 16.5 %collective-permute-start.3 = (bf16[512,256]{1,0:T(8,128)(2,1)S(1)}, bf16[512,256]{1,0:T(8,128)(2,1)S(1)}, u32[]{:S(2)}, u32[]{:S(2)}) collective-permute-start(bf16[512,256]{1,0:T(8,128)(2,1)S(1)} %get-tuple-element.17), channel_id=1, source_target_pairs={{0,6},{1,7},{2,4},{3,5},{4,2},{5,3},{6,0},{7,1},{8,14},{9,15},{10,... | collective-permute-start | bytes 786440 | tf_op jit(solution)/shard_map/pooling/ppermute | solution.py:425
  132.3 10.7 %collective-permute-start.4 = (bf16[512,256]{1,0:T(8,128)(2,1)S(1)}, bf16[512,256]{1,0:T(8,128)(2,1)S(1)}, u32[]{:S(2)}, u32[]{:S(2)}) collective-permute-start(bf16[512,256]{1,0:T(8,128)(2,1)S(1)} %get-tuple-element.18), channel_id=1, source_target_pairs={{0,2},{1,3},{2,0},{3,1},{4,6},{5,7},{6,4},{7,5},{8,10},{9,11},{10,... | collective-permute-start | bytes 786440 | tf_op jit(solution)/shard_map/pooling/ppermute | solution.py:425
  142.3 0.7 copy-start.6
  143.0 0.7 copy-start.8
  144.5 13.1 %all-to-all-start.3 = ((bf16[16,64,128]{2,1,0:T(8,128)(2,1)}), bf16[16,64,128]{2,1,0:T(8,128)(2,1)S(1)}, u32[]{:S(2)}, u32[]{:S(2)}) async-start(bf16[16,64,128]{2,1,0:T(8,128)(2,1)} %add_sources.1), calls=%async_computation.3 | async-start | bytes 524288 | tf_op jit(solution)/shard_map/sums_to_owners/all_to_all | solution.py:462
  150.5 1.0 copy-start.7
  151.5 0.9 copy-start.9
Sparse Core Ops, SparseCore 0:
  60.5 36.7 all-gather.2

commit v9 on v8

--- a/solution.py
+++ b/solution.py
@@ -73,7 +73,7 @@
     lanes = entries.shape[1] // owner_count
     entry_count = entries.shape[0]
     span = per_tile * lanes // entry_count
-    group = owner_count // 4
+    group = owner_count // 2
 
     def kernel(blocks_ref, entries_ref, weights_ref, targets_ref, out_ref):
         shift = lax.broadcasted_iota(jnp.int32, (entry_count, lanes), 0) * span
@@ -277,9 +277,10 @@
 
         @pl.when(step == 0)
         def _():
-            for r in range(parts):
+            for i in range(many):
+                r = place_ref[0] ^ (2 * i + first)
                 for p in range(owner_count):
-                    numbers_ref[pl.ds(r * owner_count + p, 1), :] = (
+                    numbers_ref[pl.ds(i * owner_count + p, 1), :] = (
                         bags_ref[r, p].astype(jnp.float32)[2 * entry_count + 1 : 2 * entry_count + 2].astype(jnp.int32)
                     )
             copy = pltpu.make_async_copy(numbers_ref, blocks_ref, sem)
@@ -301,7 +302,7 @@
                 ],
                 axis=0,
             ).astype(jnp.bfloat16)
-            chosen = [blocks_ref[replica * owner_count + p, j] for j in range(per_tile)]
+            chosen = [blocks_ref[step * owner_count + p, j] for j in range(per_tile)]
             slab = jnp.concatenate([table_ref[p, b] for b in chosen], axis=1)
             partials.append(
                 jnp.dot(slab, incidence, preferred_element_type=jnp.float32).astype(jnp.bfloat16)
@@ -322,8 +323,8 @@
         in_specs=[pl.BlockSpec(memory_space=pltpu.SMEM), whole, whole],
         out_specs=pl.BlockSpec((1, samples, width), lambda i: (i, 0, 0)),
         scratch_shapes=[
-            pltpu.VMEM((parts * owner_count, lanes), jnp.int32),
-            pltpu.SMEM((parts * owner_count, lanes), jnp.int32),
+            pltpu.VMEM((many * owner_count, lanes), jnp.int32),
+            pltpu.SMEM((many * owner_count, lanes), jnp.int32),
             pltpu.SemaphoreType.DMA(()),
         ],
         compiler_params=pltpu.CompilerParams(

time: 167 us -> 165 us (0.988)
  Pallas kernels: 27.1 us -> 25.4 us
where the time goes in v9:
time: 165 us
  starting transfers between devices  64.6 us (39%)
  waiting for transfers between devices  50.8 us (31%)
  Pallas kernels  25.4 us (15%)
  between operations  14.3 us (9%)
  local copies, waits for them, and re-layouts  8.48 us (5%)
    all_to_all x1, waiting for transfers between devices, local(): lax.all_to_all(sent, LOWS, split_axis=0, concat_axis=0, tiled=True)  36.5 us
    ppermute x4, starting transfers between devices, to_replica(): return lax.ppermute(array, 'replica', [(r, r ^ k) for r in range(parts)])  16.6 us
    all_to_all x1, starting transfers between devices, local(): bags = lax.all_to_all(bags, HIGHS, split_axis=0, concat_axis=0, tiled=True)  16.5 us
    all_to_all x1, starting transfers between devices, local(): lax.all_to_all(sent, LOWS, split_axis=0, concat_axis=0, tiled=True)  15.8 us
    pallas_call x2, Pallas kernels, pool_parts(): pl.pallas_call(kernel, out_shape=jax.ShapeDtypeStruct((many, samples, wid...  9.75 us
    unnamed x28, local copies, waits for them, and re-layouts  7.63 us
    ppermute x4, waiting for transfers between devices, to_replica(): return lax.ppermute(array, 'replica', [(r, r ^ k) for r in range(parts)])  7.55 us
    all_to_all x1, starting transfers between devices, local(): lax.all_to_all(sums, HIGHS, split_axis=0, concat_axis=0, tiled=True)  7.33 us
  transfers between devices with their start and end apart: 10, of which 5 were waited for; matrix products, arithmetic and copies ran while one was open for 1% of the time, Pallas kernels for 12%

profile of v9, /device:TPU:1, one launch (start us, length us, event | category | flops | bytes accessed | tf_op | source)
XLA Modules:
  0.0 164.7 jit_solution(9576376745492880887)
XLA Ops:
  7.2 2.0 %pack_bags.1 = bf16[64,16,128]{2,1,0:T(8,128)(2,1)} custom-call(s32[3,1,64]{2,1,0:T(1,128)} %bitcast.31, s32[4,8192]{1,0:T(4,128)} %bitcast.29, f32[4,8192]{1,0:T(4,128)} %bitcast.30, s32[1,8192]{1,0:T(1,128)} %targets_ref.1), custom_call_target="tpu_custom_call" | custom-call | flops 1000 | bytes 1000 | tf_op jit(solution)/shard_map/bags_over_high/pack_bags/pallas_call | solution.py:105
  9.2 16.5 %all-to-all-start = ((bf16[32,2,16,128]{3,2,1,0:T(8,128)(2,1)}), bf16[32,2,16,128]{3,2,1,0:T(8,128)(2,1)S(1)}, u32[]{:S(2)}, u32[]{:S(2)}) async-start(bf16[32,2,16,128]{3,2,1,0:T(8,128)(2,1)} %bitcast.26), calls=%async_computation | async-start | bytes 524288 | tf_op jit(solution)/shard_map/bags_over_high/all_to_all | solution.py:442
  25.7 1.1 convert_element_type.3
  26.8 2.3 %collective-permute-start = (bf16[4,256,128]{1,2,0:T(8,128)(2,1)S(1)}, bf16[4,256,128]{1,2,0:T(8,128)(2,1)S(1)}, u32[]{:S(2)}, u32[]{:S(2)}) collective-permute-start(bf16[4,256,128]{1,2,0:T(8,128)(2,1)S(1)} %bitcast.28), channel_id=1, source_target_pairs={{0,0},{1,9},{2,18},{3,27},{4,36},{5,45},{6,54},{7,63},{8,64},{9,73... | collective-permute-start | bytes 786440 | tf_op jit(solution)/shard_map/table_gather/ppermute | solution.py:436
  29.1 1.7 %copy-done.1 = bf16[1,40,128,256]{3,2,1,0:T(8,128)(2,1)S(1)} copy-done((bf16[1,40,128,256]{3,2,1,0:T(8,128)(2,1)S(1)}, bf16[1,40,128,256]{3,2,1,0:T(8,128)(2,1)}, u32[]{:S(2)}) %copy-start.1) | copy-done | bytes 2621464
  30.9 3.5 %pack_parts.1.packed_ref = bf16[16,45,16,128]{3,2,1,0:T(8,128)(2,1)} custom-call(bf16[40,128,256]{2,1,0:T(8,128)(2,1)S(1)} %bitcast.22), custom_call_target="tpu_custom_call" | custom-call | flops 1000 | bytes 1000 | tf_op jit(solution)/shard_map/parts_over_low/pack_parts/pallas_call | solution.py:139
  34.5 3.8 %collective-permute-done = bf16[4,256,128]{1,2,0:T(8,128)(2,1)S(1)} collective-permute-done((bf16[4,256,128]{1,2,0:T(8,128)(2,1)S(1)}, bf16[4,256,128]{1,2,0:T(8,128)(2,1)S(1)}, u32[]{:S(2)}, u32[]{:S(2)}) %collective-permute-start) | collective-permute-done | bytes 262176 | tf_op jit(solution)/shard_map/table_gather/ppermute | solution.py:436
  38.6 1.4 add_bags.1
  40.0 15.8 %all-to-all-start.1 = ((bf16[16,45,16,128]{3,2,1,0:T(8,128)(2,1)}), bf16[16,45,16,128]{3,2,1,0:T(8,128)(2,1)S(1)}, u32[]{:S(2)}, u32[]{:S(2)}) async-start(bf16[16,45,16,128]{3,2,1,0:T(8,128)(2,1)} %add_bags.1), calls=%async_computation.1 | async-start | bytes 5898240 | tf_op jit(solution)/shard_map/parts_over_low/all_to_all | solution.py:448
  55.9 0.8 copy.17
  56.8 36.5 %all-to-all-done.1.recv_ref = bf16[16,45,16,128]{3,2,1,0:T(8,128)(2,1)S(1)} async-done(((bf16[16,45,16,128]{3,2,1,0:T(8,128)(2,1)}), bf16[16,45,16,128]{3,2,1,0:T(8,128)(2,1)S(1)}, u32[]{:S(2)}, u32[]{:S(2)}) %all-to-all-start.1) | async-done | bytes 2949152 | tf_op jit(solution)/shard_map/parts_over_low/all_to_all | solution.py:448
  93.2 2.9 %add_parts.1 = (bf16[32,128,128]{2,1,0:T(8,128)(2,1)S(1)}, bf16[8,8,16,128]{3,2,1,0:T(8,128)(2,1)S(1)}) custom-call(bf16[16,45,16,128]{3,2,1,0:T(8,128)(2,1)S(1)} %all-to-all-done.1.recv_ref), custom_call_target="tpu_custom_call" | custom-call | flops 1000 | bytes 1000 | tf_op jit(solution)/shard_map/sums_over_high/add_parts/pallas_call | solution.py:217
  96.2 1.0 copy-done.4
  97.1 7.3 %all-to-all-start.2 = ((bf16[32,128,128]{2,1,0:T(8,128)(2,1)}), bf16[32,128,128]{2,1,0:T(8,128)(2,1)S(1)}, u32[]{:S(2)}, u32[]{:S(2)}) async-start(bf16[32,128,128]{2,1,0:T(8,128)(2,1)} %copy-done.4), calls=%async_computation.2 | async-start | bytes 2097152 | tf_op jit(solution)/shard_map/sums_over_high/all_to_all | solution.py:452
  104.5 1.6 copy-done
  106.1 4.9 %pool_parts.3 = bf16[4,512,256]{2,1,0:T(8,128)(2,1)S(1)} custom-call(s32[2]{0:T(128)S(1)} %pad_add_fusion.place_ref, bf16[8,4,256,128]{3,2,1,0:T(8,128)(2,1)S(1)} %bitcast.20, bf16[8,8,16,128]{3,2,1,0:T(8,128)(2,1)S(1)} %get-tuple-element.14.bags_ref), custom_call_target="tpu_custom_call" | custom-call | flops 1000 | bytes 1000 | tf_op jit(solution)/shard_map/pooling/pool_parts/pallas_call | solution.py:319
  111.0 2.8 %collective-permute-start.1 = (bf16[4,512,256]{2,1,0:T(8,128)(2,1)S(1)}, bf16[4,512,256]{2,1,0:T(8,128)(2,1)S(1)}, u32[]{:S(2)}, u32[]{:S(2)}) collective-permute-start(bf16[4,512,256]{2,1,0:T(8,128)(2,1)S(1)} %pool_parts.3), channel_id=1, source_target_pairs={{0,1},{1,0},{2,3},{3,2},{4,5},{5,4},{6,7},{7,6},{8,9},{9,8},{10,11... | collective-permute-start | bytes 3145736 | tf_op jit(solution)/shard_map/pooling/ppermute | solution.py:426
  113.8 4.9 %pool_parts.2.mine_ref = f32[4,512,256]{2,1,0:T(8,128)S(1)} custom-call(s32[2]{0:T(128)S(1)} %pad_add_fusion.place_ref, bf16[8,4,256,128]{3,2,1,0:T(8,128)(2,1)S(1)} %bitcast.21, bf16[8,8,16,128]{3,2,1,0:T(8,128)(2,1)S(1)} %get-tuple-element.14.bags_ref), custom_call_target="tpu_custom_call" | custom-call | flops 1000 | bytes 1000 | tf_op jit(solution)/shard_map/pooling/pool_parts/pallas_call | solution.py:319
  118.7 0.5 join.1
  119.3 4.9 %collective-permute-start.2 = (bf16[512,256]{1,0:T(8,128)(2,1)S(1)}, bf16[512,256]{1,0:T(8,128)(2,1)S(1)}, u32[]{:S(2)}, u32[]{:S(2)}) collective-permute-start(bf16[512,256]{1,0:T(8,128)(2,1)S(1)} %get-tuple-element.16), channel_id=1, source_target_pairs={{0,4},{1,5},{2,6},{3,7},{4,0},{5,1},{6,2},{7,3},{8,12},{9,13},{10,... | collective-permute-start | bytes 786440 | tf_op jit(solution)/shard_map/pooling/ppermute | solution.py:426
  124.1 6.4 %collective-permute-start.3 = (bf16[512,256]{1,0:T(8,128)(2,1)S(1)}, bf16[512,256]{1,0:T(8,128)(2,1)S(1)}, u32[]{:S(2)}, u32[]{:S(2)}) collective-permute-start(bf16[512,256]{1,0:T(8,128)(2,1)S(1)} %get-tuple-element.17), channel_id=1, source_target_pairs={{0,6},{1,7},{2,4},{3,5},{4,2},{5,3},{6,0},{7,1},{8,14},{9,15},{10,... | collective-permute-start | bytes 786440 | tf_op jit(solution)/shard_map/pooling/ppermute | solution.py:426
  130.6 2.5 %collective-permute-start.4 = (bf16[512,256]{1,0:T(8,128)(2,1)S(1)}, bf16[512,256]{1,0:T(8,128)(2,1)S(1)}, u32[]{:S(2)}, u32[]{:S(2)}) collective-permute-start(bf16[512,256]{1,0:T(8,128)(2,1)S(1)} %get-tuple-element.18), channel_id=1, source_target_pairs={{0,2},{1,3},{2,0},{3,1},{4,6},{5,7},{6,4},{7,5},{8,10},{9,11},{10,... | collective-permute-start | bytes 786440 | tf_op jit(solution)/shard_map/pooling/ppermute | solution.py:426
  133.1 7.5 %collective-permute-done.3.refs_2_ = bf16[512,256]{1,0:T(8,128)(2,1)S(1)} collective-permute-done((bf16[512,256]{1,0:T(8,128)(2,1)S(1)}, bf16[512,256]{1,0:T(8,128)(2,1)S(1)}, u32[]{:S(2)}, u32[]{:S(2)}) %collective-permute-start.3) | collective-permute-done | bytes 262176 | tf_op jit(solution)/shard_map/pooling/ppermute | solution.py:426
  140.6 0.7 copy-done.6
  141.3 0.7 copy-done.8
  142.0 0.8 add_sources.1
  142.9 5.9 %all-to-all-start.3 = ((bf16[16,64,128]{2,1,0:T(8,128)(2,1)}), bf16[16,64,128]{2,1,0:T(8,128)(2,1)S(1)}, u32[]{:S(2)}, u32[]{:S(2)}) async-start(bf16[16,64,128]{2,1,0:T(8,128)(2,1)} %add_sources.1), calls=%async_computation.3 | async-start | bytes 524288 | tf_op jit(solution)/shard_map/sums_to_owners/all_to_all | solution.py:463
  148.8 0.9 copy-done.7
  149.8 0.9 copy-done.9
  150.7 2.6 %cross_layers.1 = bf16[512,512]{1,0:T(8,128)(2,1)} custom-call(bf16[512,256]{1,0:T(8,128)(2,1)S(1)} %get-tuple-element.15.refs_0_, bf16[512,256]{1,0:T(8,128)(2,1)S(1)} %collective-permute-done.2.refs_1_, bf16[512,256]{1,0:T(8,128)(2,1)S(1)} %copy-done.7, bf16[512,256]{1,0:T(8,128)(2,1)S(1)} %copy-done.9, bf16[512,256]{1,0:T(8,128)(2,1)S(1)} %bitcast.23, ...), custom_call_target="tpu_custom_call" | custom-call | flops 1000 | bytes 1000 | tf_op jit(solution)/shard_map/cross/cross_layers/pallas_call | solution.py:382
  153.3 2.7 %all-to-all-done.3.grads_ref = bf16[16,64,128]{2,1,0:T(8,128)(2,1)S(1)} async-done(((bf16[16,64,128]{2,1,0:T(8,128)(2,1)}), bf16[16,64,128]{2,1,0:T(8,128)(2,1)S(1)}, u32[]{:S(2)}, u32[]{:S(2)}) %all-to-all-start.3) | async-done | bytes 262176 | tf_op jit(solution)/shard_map/sums_to_owners/all_to_all | solution.py:463
  156.0 1.9 %adagrad.1 = (f32[512,256]{1,0:T(8,128)}, f32[4,128]{1,0:T(4,128)}) custom-call(bf16[16,64,128]{2,1,0:T(8,128)(2,1)S(1)} %all-to-all-done.3.grads_ref, f32[4,128]{1,0:T(4,128)S(1)} %bitcast.24, f32[512,256]{1,0:T(8,128)S(1)} %copy-done.2), custom_call_target="tpu_custom_call" | custom-call | flops 1000 | bytes 1000 | tf_op jit(solution)/shard_map/table_update/adagrad/pallas_call | solution.py:47
  (30 shorter events, 0.5 us)
Async XLA Ops:
  9.2 29.4 %all-to-all-start = ((bf16[32,2,16,128]{3,2,1,0:T(8,128)(2,1)}), bf16[32,2,16,128]{3,2,1,0:T(8,128)(2,1)S(1)}, u32[]{:S(2)}, u32[]{:S(2)}) async-start(bf16[32,2,16,128]{3,2,1,0:T(8,128)(2,1)} %bitcast.26), calls=%async_computation | async-start | bytes 524288 | tf_op jit(solution)/shard_map/bags_over_high/all_to_all | solution.py:442
  26.8 11.8 %copy-start.12 = (s32[1,40,1]{1,2,0:T(1,128)S(1)}, s32[1,40,1]{1,2,0:T(1,128)}, u32[]{:S(2)}) copy-start(s32[1,40,1]{1,2,0:T(1,128)} %param.22) | copy-start | bytes 484
  26.8 11.7 %copy-start.13 = (s32[1,40]{1,0:T(1,128)S(1)}, s32[1,40]{1,0:T(1,128)}, u32[]{:S(2)}) copy-start(s32[1,40]{1,0:T(1,128)} %numbers_ref.1) | copy-start | bytes 484
  26.8 11.4 %collective-permute-start = (bf16[4,256,128]{1,2,0:T(8,128)(2,1)S(1)}, bf16[4,256,128]{1,2,0:T(8,128)(2,1)S(1)}, u32[]{:S(2)}, u32[]{:S(2)}) collective-permute-start(bf16[4,256,128]{1,2,0:T(8,128)(2,1)S(1)} %bitcast.28), channel_id=1, source_target_pairs={{0,0},{1,9},{2,18},{3,27},{4,36},{5,45},{6,54},{7,63},{8,64},{9,73... | collective-permute-start | bytes 786440 | tf_op jit(solution)/shard_map/table_gather/ppermute | solution.py:436
  29.1 1.7 %copy-start.1 = (bf16[1,40,128,256]{3,2,1,0:T(8,128)(2,1)S(1)}, bf16[1,40,128,256]{3,2,1,0:T(8,128)(2,1)}, u32[]{:S(2)}) copy-start(bf16[1,40,128,256]{3,2,1,0:T(8,128)(2,1)} %param.21) | copy-start | bytes 7864324
  40.0 53.2 %all-to-all-start.1 = ((bf16[16,45,16,128]{3,2,1,0:T(8,128)(2,1)}), bf16[16,45,16,128]{3,2,1,0:T(8,128)(2,1)S(1)}, u32[]{:S(2)}, u32[]{:S(2)}) async-start(bf16[16,45,16,128]{3,2,1,0:T(8,128)(2,1)} %add_bags.1), calls=%async_computation.1 | async-start | bytes 5898240 | tf_op jit(solution)/shard_map/parts_over_low/all_to_all | solution.py:448
  55.9 48.7 %all-gather.3.cloned.1.call-start = ((), (), s32[]{:S(2)}) async-start(), calls=%async_computation.4 | async-start | bytes 2359296 | tf_op jit(solution)/shard_map/table_gather/all_gather | solution.py:437
  96.2 1.0 copy-start.4
  97.1 44.9 %all-to-all-start.2 = ((bf16[32,128,128]{2,1,0:T(8,128)(2,1)}), bf16[32,128,128]{2,1,0:T(8,128)(2,1)S(1)}, u32[]{:S(2)}, u32[]{:S(2)}) async-start(bf16[32,128,128]{2,1,0:T(8,128)(2,1)} %copy-done.4), calls=%async_computation.2 | async-start | bytes 2097152 | tf_op jit(solution)/shard_map/sums_over_high/all_to_all | solution.py:452
  104.5 1.6 copy-start
  111.0 7.7 %collective-permute-start.1 = (bf16[4,512,256]{2,1,0:T(8,128)(2,1)S(1)}, bf16[4,512,256]{2,1,0:T(8,128)(2,1)S(1)}, u32[]{:S(2)}, u32[]{:S(2)}) collective-permute-start(bf16[4,512,256]{2,1,0:T(8,128)(2,1)S(1)} %pool_parts.3), channel_id=1, source_target_pairs={{0,1},{1,0},{2,3},{3,2},{4,5},{5,4},{6,7},{7,6},{8,9},{9,8},{10,11... | collective-permute-start | bytes 3145736 | tf_op jit(solution)/shard_map/pooling/ppermute | solution.py:426
  118.7 30.1 %copy-start.3 = (bf16[2,512,512]{2,1,0:T(8,128)(2,1)S(1)}, bf16[2,512,512]{2,1,0:T(8,128)(2,1)}, u32[]{:S(2)}) copy-start(bf16[2,512,512]{2,1,0:T(8,128)(2,1)} %refs_5_.1) | copy-start | bytes 3145732
  118.7 30.1 %copy-start.5 = (bf16[1,512,256]{2,1,0:T(8,128)(2,1)S(1)}, bf16[1,512,256]{2,1,0:T(8,128)(2,1)}, u32[]{:S(2)}) copy-start(bf16[1,512,256]{2,1,0:T(8,128)(2,1)} %param.18) | copy-start | bytes 786436
  118.7 30.1 %copy-start.10 = (f32[2,512]{1,0:T(2,128)S(1)}, f32[2,512]{1,0:T(2,128)}, u32[]{:S(2)}) copy-start(f32[2,512]{1,0:T(2,128)} %refs_6_.1) | copy-start | bytes 12292
  119.2 36.7 %copy-start.2 = (f32[512,256]{1,0:T(8,128)S(1)}, f32[512,256]{1,0:T(8,128)}, u32[]{:S(2)}) copy-start(f32[512,256]{1,0:T(8,128)} %table_ref.1) | copy-start | bytes 1572868
  119.2 36.7 %copy-start.11 = (f32[512]{0:T(512)S(1)}, f32[512]{0:T(512)}, u32[]{:S(2)}) copy-start(f32[512]{0:T(512)} %param.13) | copy-start | bytes 6148
  119.3 13.8 %collective-permute-start.2 = (bf16[512,256]{1,0:T(8,128)(2,1)S(1)}, bf16[512,256]{1,0:T(8,128)(2,1)S(1)}, u32[]{:S(2)}, u32[]{:S(2)}) collective-permute-start(bf16[512,256]{1,0:T(8,128)(2,1)S(1)} %get-tuple-element.16), channel_id=1, source_target_pairs={{0,4},{1,5},{2,6},{3,7},{4,0},{5,1},{6,2},{7,3},{8,12},{9,13},{10,... | collective-permute-start | bytes 786440 | tf_op jit(solution)/shard_map/pooling/ppermute | solution.py:426
  124.1 16.5 %collective-permute-start.3 = (bf16[512,256]{1,0:T(8,128)(2,1)S(1)}, bf16[512,256]{1,0:T(8,128)(2,1)S(1)}, u32[]{:S(2)}, u32[]{:S(2)}) collective-permute-start(bf16[512,256]{1,0:T(8,128)(2,1)S(1)} %get-tuple-element.17), channel_id=1, source_target_pairs={{0,6},{1,7},{2,4},{3,5},{4,2},{5,3},{6,0},{7,1},{8,14},{9,15},{10,... | collective-permute-start | bytes 786440 | tf_op jit(solution)/shard_map/pooling/ppermute | solution.py:426
  130.6 10.7 %collective-permute-start.4 = (bf16[512,256]{1,0:T(8,128)(2,1)S(1)}, bf16[512,256]{1,0:T(8,128)(2,1)S(1)}, u32[]{:S(2)}, u32[]{:S(2)}) collective-permute-start(bf16[512,256]{1,0:T(8,128)(2,1)S(1)} %get-tuple-element.18), channel_id=1, source_target_pairs={{0,2},{1,3},{2,0},{3,1},{4,6},{5,7},{6,4},{7,5},{8,10},{9,11},{10,... | collective-permute-start | bytes 786440 | tf_op jit(solution)/shard_map/pooling/ppermute | solution.py:426
  140.6 0.7 copy-start.6
  141.3 0.7 copy-start.8
  142.9 13.1 %all-to-all-start.3 = ((bf16[16,64,128]{2,1,0:T(8,128)(2,1)}), bf16[16,64,128]{2,1,0:T(8,128)(2,1)S(1)}, u32[]{:S(2)}, u32[]{:S(2)}) async-start(bf16[16,64,128]{2,1,0:T(8,128)(2,1)} %add_sources.1), calls=%async_computation.3 | async-start | bytes 524288 | tf_op jit(solution)/shard_map/sums_to_owners/all_to_all | solution.py:463
  148.8 1.0 copy-start.7
  149.8 0.9 copy-start.9
Sparse Core Ops, SparseCore 0:
  59.3 36.7 all-gather.2

commit v10 on v9

--- a/solution.py
+++ b/solution.py
@@ -186,8 +186,10 @@
     kept = TAIL - 1
     lows = sources // parts
     each = slot_count // highs
-
-    def kernel(recv_ref, out_ref, bags_ref, acc_ref, numbers_ref, slots_ref, sem):
+    chunks = 4
+    chunk = highs // chunks
+
+    def kernel(recv_ref, out_ref, bags_ref, acc_ref, stage_ref, numbers_ref, slots_ref, sem, out_sems):
         for t in range(sources):
             numbers_ref[pl.ds(t, 1), :] = recv_ref[t, count].astype(jnp.float32)[0:1].astype(jnp.int32)
         copy = pltpu.make_async_copy(numbers_ref, slots_ref, sem)
@@ -208,10 +210,17 @@
 
         def place(e, carry):
             for i in range(each):
-                out_ref[e, pl.ds(i * TILE, TILE), :] = acc_ref[e * each + i].astype(out_ref.dtype)
+                stage_ref[e, pl.ds(i * TILE, TILE), :] = acc_ref[e * each + i].astype(stage_ref.dtype)
             return carry
 
-        lax.fori_loop(0, highs, place, 0)
+        copies = []
+        for n in range(chunks):
+            lax.fori_loop(n * chunk, (n + 1) * chunk, place, 0)
+            at = pl.ds(n * chunk, chunk)
+            copies.append(pltpu.make_async_copy(stage_ref.at[at], out_ref.at[at], out_sems.at[n]))
+            copies[-1].start()
+        for out_copy in copies:
+            out_copy.wait()
 
     whole = pl.BlockSpec(memory_space=pltpu.VMEM)
     return pl.pallas_call(
@@ -221,12 +230,14 @@
             jax.ShapeDtypeStruct((parts, lows * kept, TILE, lanes), jnp.bfloat16),
         ],
         in_specs=[whole],
-        out_specs=[whole] * 2,
+        out_specs=[pl.BlockSpec(memory_space=pltpu.HBM), whole],
         scratch_shapes=[
             pltpu.VMEM((slot_count, TILE, lanes), jnp.float32),
+            pltpu.VMEM((highs, each * TILE, lanes), jnp.bfloat16),
             pltpu.VMEM((sources, lanes), jnp.int32),
             pltpu.SMEM((sources, lanes), jnp.int32),
             pltpu.SemaphoreType.DMA(()),
+            pltpu.SemaphoreType.DMA((chunks,)),
         ],
         compiler_params=pltpu.CompilerParams(vmem_limit_bytes=VMEM_LIMIT),
         cost_estimate=SMALL,

time: 165 us -> 166 us (level)
  no operation moved by 1% of the time
where the time goes in v10:
time: 166 us; the launch traced here: 165 us
  starting transfers between devices  64.6 us (39%)
  waiting for transfers between devices  50.8 us (31%)
  Pallas kernels  25.6 us (15%)
  between operations  14.3 us (9%)
  local copies, waits for them, and re-layouts  8.48 us (5%)
    all_to_all x1, waiting for transfers between devices, local(): lax.all_to_all(sent, LOWS, split_axis=0, concat_axis=0, tiled=True)  36.5 us
    ppermute x4, starting transfers between devices, to_replica(): return lax.ppermute(array, 'replica', [(r, r ^ k) for r in range(parts)])  16.6 us
    all_to_all x1, starting transfers between devices, local(): bags = lax.all_to_all(bags, HIGHS, split_axis=0, concat_axis=0, tiled=True)  16.5 us
    all_to_all x1, starting transfers between devices, local(): lax.all_to_all(sent, LOWS, split_axis=0, concat_axis=0, tiled=True)  15.8 us
    pallas_call x2, Pallas kernels, pool_parts(): pl.pallas_call(kernel, out_shape=jax.ShapeDtypeStruct((many, samples, wid...  9.75 us
    unnamed x28, local copies, waits for them, and re-layouts  7.63 us
    ppermute x4, waiting for transfers between devices, to_replica(): return lax.ppermute(array, 'replica', [(r, r ^ k) for r in range(parts)])  7.55 us
    all_to_all x1, starting transfers between devices, local(): lax.all_to_all(sums, HIGHS, split_axis=0, concat_axis=0, tiled=True)  7.35 us
  transfers between devices with their start and end apart: 10, of which 5 were waited for; matrix products, arithmetic and copies ran while one was open for 1% of the time, Pallas kernels for 12%

profile of v10, /device:TPU:1, one launch (start us, length us, event | category | flops | bytes accessed | tf_op | source)
XLA Modules:
  0.0 164.8 jit_solution(1799440823835365190)
XLA Ops:
  7.2 2.0 %pack_bags.1 = bf16[64,16,128]{2,1,0:T(8,128)(2,1)} custom-call(s32[3,1,64]{2,1,0:T(1,128)} %bitcast.31, s32[4,8192]{1,0:T(4,128)} %bitcast.29, f32[4,8192]{1,0:T(4,128)} %bitcast.30, s32[1,8192]{1,0:T(1,128)} %targets_ref.1), custom_call_target="tpu_custom_call" | custom-call | flops 1000 | bytes 1000 | tf_op jit(solution)/shard_map/bags_over_high/pack_bags/pallas_call | solution.py:105
  9.2 16.5 %all-to-all-start = ((bf16[32,2,16,128]{3,2,1,0:T(8,128)(2,1)}), bf16[32,2,16,128]{3,2,1,0:T(8,128)(2,1)S(1)}, u32[]{:S(2)}, u32[]{:S(2)}) async-start(bf16[32,2,16,128]{3,2,1,0:T(8,128)(2,1)} %bitcast.26), calls=%async_computation | async-start | bytes 524288 | tf_op jit(solution)/shard_map/bags_over_high/all_to_all | solution.py:453
  25.7 1.1 convert_element_type.3
  26.8 2.3 %collective-permute-start = (bf16[4,256,128]{1,2,0:T(8,128)(2,1)S(1)}, bf16[4,256,128]{1,2,0:T(8,128)(2,1)S(1)}, u32[]{:S(2)}, u32[]{:S(2)}) collective-permute-start(bf16[4,256,128]{1,2,0:T(8,128)(2,1)S(1)} %bitcast.28), channel_id=1, source_target_pairs={{0,0},{1,9},{2,18},{3,27},{4,36},{5,45},{6,54},{7,63},{8,64},{9,73... | collective-permute-start | bytes 786440 | tf_op jit(solution)/shard_map/table_gather/ppermute | solution.py:447
  29.1 1.7 %copy-done.1 = bf16[1,40,128,256]{3,2,1,0:T(8,128)(2,1)S(1)} copy-done((bf16[1,40,128,256]{3,2,1,0:T(8,128)(2,1)S(1)}, bf16[1,40,128,256]{3,2,1,0:T(8,128)(2,1)}, u32[]{:S(2)}) %copy-start.1) | copy-done | bytes 2621464
  30.9 3.5 %pack_parts.1.packed_ref = bf16[16,45,16,128]{3,2,1,0:T(8,128)(2,1)} custom-call(bf16[40,128,256]{2,1,0:T(8,128)(2,1)S(1)} %bitcast.22), custom_call_target="tpu_custom_call" | custom-call | flops 1000 | bytes 1000 | tf_op jit(solution)/shard_map/parts_over_low/pack_parts/pallas_call | solution.py:139
  34.5 3.8 %collective-permute-done = bf16[4,256,128]{1,2,0:T(8,128)(2,1)S(1)} collective-permute-done((bf16[4,256,128]{1,2,0:T(8,128)(2,1)S(1)}, bf16[4,256,128]{1,2,0:T(8,128)(2,1)S(1)}, u32[]{:S(2)}, u32[]{:S(2)}) %collective-permute-start) | collective-permute-done | bytes 262176 | tf_op jit(solution)/shard_map/table_gather/ppermute | solution.py:447
  38.6 1.4 add_bags.1
  40.0 15.8 %all-to-all-start.1 = ((bf16[16,45,16,128]{3,2,1,0:T(8,128)(2,1)}), bf16[16,45,16,128]{3,2,1,0:T(8,128)(2,1)S(1)}, u32[]{:S(2)}, u32[]{:S(2)}) async-start(bf16[16,45,16,128]{3,2,1,0:T(8,128)(2,1)} %add_bags.1), calls=%async_computation.1 | async-start | bytes 5898240 | tf_op jit(solution)/shard_map/parts_over_low/all_to_all | solution.py:459
  55.9 0.8 copy.17
  56.8 36.5 %all-to-all-done.1.recv_ref = bf16[16,45,16,128]{3,2,1,0:T(8,128)(2,1)S(1)} async-done(((bf16[16,45,16,128]{3,2,1,0:T(8,128)(2,1)}), bf16[16,45,16,128]{3,2,1,0:T(8,128)(2,1)S(1)}, u32[]{:S(2)}, u32[]{:S(2)}) %all-to-all-start.1) | async-done | bytes 2949152 | tf_op jit(solution)/shard_map/parts_over_low/all_to_all | solution.py:459
  93.2 3.1 %add_parts.1 = (bf16[32,128,128]{2,1,0:T(8,128)(2,1)S(1)}, bf16[8,8,16,128]{3,2,1,0:T(8,128)(2,1)S(1)}) custom-call(bf16[16,45,16,128]{3,2,1,0:T(8,128)(2,1)S(1)} %all-to-all-done.1.recv_ref), custom_call_target="tpu_custom_call" | custom-call | flops 1000 | bytes 1000 | tf_op jit(solution)/shard_map/sums_over_high/add_parts/pallas_call | solution.py:226
  96.3 1.0 copy-done.4
  97.3 7.3 %all-to-all-start.2 = ((bf16[32,128,128]{2,1,0:T(8,128)(2,1)}), bf16[32,128,128]{2,1,0:T(8,128)(2,1)S(1)}, u32[]{:S(2)}, u32[]{:S(2)}) async-start(bf16[32,128,128]{2,1,0:T(8,128)(2,1)} %copy-done.4), calls=%async_computation.2 | async-start | bytes 2097152 | tf_op jit(solution)/shard_map/sums_over_high/all_to_all | solution.py:463
  104.7 1.6 copy-done
  106.3 4.9 %pool_parts.3 = bf16[4,512,256]{2,1,0:T(8,128)(2,1)S(1)} custom-call(s32[2]{0:T(128)S(1)} %pad_add_fusion.place_ref, bf16[8,4,256,128]{3,2,1,0:T(8,128)(2,1)S(1)} %bitcast.20, bf16[8,8,16,128]{3,2,1,0:T(8,128)(2,1)S(1)} %get-tuple-element.14.bags_ref), custom_call_target="tpu_custom_call" | custom-call | flops 1000 | bytes 1000 | tf_op jit(solution)/shard_map/pooling/pool_parts/pallas_call | solution.py:330
  111.1 2.8 %collective-permute-start.1 = (bf16[4,512,256]{2,1,0:T(8,128)(2,1)S(1)}, bf16[4,512,256]{2,1,0:T(8,128)(2,1)S(1)}, u32[]{:S(2)}, u32[]{:S(2)}) collective-permute-start(bf16[4,512,256]{2,1,0:T(8,128)(2,1)S(1)} %pool_parts.3), channel_id=1, source_target_pairs={{0,1},{1,0},{2,3},{3,2},{4,5},{5,4},{6,7},{7,6},{8,9},{9,8},{10,11... | collective-permute-start | bytes 3145736 | tf_op jit(solution)/shard_map/pooling/ppermute | solution.py:437
  114.0 4.9 %pool_parts.2.mine_ref = f32[4,512,256]{2,1,0:T(8,128)S(1)} custom-call(s32[2]{0:T(128)S(1)} %pad_add_fusion.place_ref, bf16[8,4,256,128]{3,2,1,0:T(8,128)(2,1)S(1)} %bitcast.21, bf16[8,8,16,128]{3,2,1,0:T(8,128)(2,1)S(1)} %get-tuple-element.14.bags_ref), custom_call_target="tpu_custom_call" | custom-call | flops 1000 | bytes 1000 | tf_op jit(solution)/shard_map/pooling/pool_parts/pallas_call | solution.py:330
  118.9 0.5 join.1
  119.4 4.9 %collective-permute-start.2 = (bf16[512,256]{1,0:T(8,128)(2,1)S(1)}, bf16[512,256]{1,0:T(8,128)(2,1)S(1)}, u32[]{:S(2)}, u32[]{:S(2)}) collective-permute-start(bf16[512,256]{1,0:T(8,128)(2,1)S(1)} %get-tuple-element.16), channel_id=1, source_target_pairs={{0,4},{1,5},{2,6},{3,7},{4,0},{5,1},{6,2},{7,3},{8,12},{9,13},{10,... | collective-permute-start | bytes 786440 | tf_op jit(solution)/shard_map/pooling/ppermute | solution.py:437
  124.3 6.4 %collective-permute-start.3 = (bf16[512,256]{1,0:T(8,128)(2,1)S(1)}, bf16[512,256]{1,0:T(8,128)(2,1)S(1)}, u32[]{:S(2)}, u32[]{:S(2)}) collective-permute-start(bf16[512,256]{1,0:T(8,128)(2,1)S(1)} %get-tuple-element.17), channel_id=1, source_target_pairs={{0,6},{1,7},{2,4},{3,5},{4,2},{5,3},{6,0},{7,1},{8,14},{9,15},{10,... | collective-permute-start | bytes 786440 | tf_op jit(solution)/shard_map/pooling/ppermute | solution.py:437
  130.7 2.5 %collective-permute-start.4 = (bf16[512,256]{1,0:T(8,128)(2,1)S(1)}, bf16[512,256]{1,0:T(8,128)(2,1)S(1)}, u32[]{:S(2)}, u32[]{:S(2)}) collective-permute-start(bf16[512,256]{1,0:T(8,128)(2,1)S(1)} %get-tuple-element.18), channel_id=1, source_target_pairs={{0,2},{1,3},{2,0},{3,1},{4,6},{5,7},{6,4},{7,5},{8,10},{9,11},{10,... | collective-permute-start | bytes 786440 | tf_op jit(solution)/shard_map/pooling/ppermute | solution.py:437
  133.3 7.5 %collective-permute-done.3.refs_2_ = bf16[512,256]{1,0:T(8,128)(2,1)S(1)} collective-permute-done((bf16[512,256]{1,0:T(8,128)(2,1)S(1)}, bf16[512,256]{1,0:T(8,128)(2,1)S(1)}, u32[]{:S(2)}, u32[]{:S(2)}) %collective-permute-start.3) | collective-permute-done | bytes 262176 | tf_op jit(solution)/shard_map/pooling/ppermute | solution.py:437
  140.8 0.7 copy-done.6
  141.5 0.7 copy-done.8
  142.2 0.8 add_sources.1
  143.1 5.9 %all-to-all-start.3 = ((bf16[16,64,128]{2,1,0:T(8,128)(2,1)}), bf16[16,64,128]{2,1,0:T(8,128)(2,1)S(1)}, u32[]{:S(2)}, u32[]{:S(2)}) async-start(bf16[16,64,128]{2,1,0:T(8,128)(2,1)} %add_sources.1), calls=%async_computation.3 | async-start | bytes 524288 | tf_op jit(solution)/shard_map/sums_to_owners/all_to_all | solution.py:474
  149.0 0.9 copy-done.7
  149.9 0.9 copy-done.9
  150.9 2.6 %cross_layers.1 = bf16[512,512]{1,0:T(8,128)(2,1)} custom-call(bf16[512,256]{1,0:T(8,128)(2,1)S(1)} %get-tuple-element.15.refs_0_, bf16[512,256]{1,0:T(8,128)(2,1)S(1)} %collective-permute-done.2.refs_1_, bf16[512,256]{1,0:T(8,128)(2,1)S(1)} %copy-done.7, bf16[512,256]{1,0:T(8,128)(2,1)S(1)} %copy-done.9, bf16[512,256]{1,0:T(8,128)(2,1)S(1)} %bitcast.23, ...), custom_call_target="tpu_custom_call" | custom-call | flops 1000 | bytes 1000 | tf_op jit(solution)/shard_map/cross/cross_layers/pallas_call | solution.py:393
  153.4 2.7 %all-to-all-done.3.grads_ref = bf16[16,64,128]{2,1,0:T(8,128)(2,1)S(1)} async-done(((bf16[16,64,128]{2,1,0:T(8,128)(2,1)}), bf16[16,64,128]{2,1,0:T(8,128)(2,1)S(1)}, u32[]{:S(2)}, u32[]{:S(2)}) %all-to-all-start.3) | async-done | bytes 262176 | tf_op jit(solution)/shard_map/sums_to_owners/all_to_all | solution.py:474
  156.1 1.9 %adagrad.1 = (f32[512,256]{1,0:T(8,128)}, f32[4,128]{1,0:T(4,128)}) custom-call(bf16[16,64,128]{2,1,0:T(8,128)(2,1)S(1)} %all-to-all-done.3.grads_ref, f32[4,128]{1,0:T(4,128)S(1)} %bitcast.24, f32[512,256]{1,0:T(8,128)S(1)} %copy-done.2), custom_call_target="tpu_custom_call" | custom-call | flops 1000 | bytes 1000 | tf_op jit(solution)/shard_map/table_update/adagrad/pallas_call | solution.py:47
  (30 shorter events, 0.5 us)
Async XLA Ops:
  9.2 29.4 %all-to-all-start = ((bf16[32,2,16,128]{3,2,1,0:T(8,128)(2,1)}), bf16[32,2,16,128]{3,2,1,0:T(8,128)(2,1)S(1)}, u32[]{:S(2)}, u32[]{:S(2)}) async-start(bf16[32,2,16,128]{3,2,1,0:T(8,128)(2,1)} %bitcast.26), calls=%async_computation | async-start | bytes 524288 | tf_op jit(solution)/shard_map/bags_over_high/all_to_all | solution.py:453
  26.8 11.8 %copy-start.12 = (s32[1,40,1]{1,2,0:T(1,128)S(1)}, s32[1,40,1]{1,2,0:T(1,128)}, u32[]{:S(2)}) copy-start(s32[1,40,1]{1,2,0:T(1,128)} %param.22) | copy-start | bytes 484
  26.8 11.7 %copy-start.13 = (s32[1,40]{1,0:T(1,128)S(1)}, s32[1,40]{1,0:T(1,128)}, u32[]{:S(2)}) copy-start(s32[1,40]{1,0:T(1,128)} %numbers_ref.1) | copy-start | bytes 484
  26.8 11.4 %collective-permute-start = (bf16[4,256,128]{1,2,0:T(8,128)(2,1)S(1)}, bf16[4,256,128]{1,2,0:T(8,128)(2,1)S(1)}, u32[]{:S(2)}, u32[]{:S(2)}) collective-permute-start(bf16[4,256,128]{1,2,0:T(8,128)(2,1)S(1)} %bitcast.28), channel_id=1, source_target_pairs={{0,0},{1,9},{2,18},{3,27},{4,36},{5,45},{6,54},{7,63},{8,64},{9,73... | collective-permute-start | bytes 786440 | tf_op jit(solution)/shard_map/table_gather/ppermute | solution.py:447
  29.1 1.7 %copy-start.1 = (bf16[1,40,128,256]{3,2,1,0:T(8,128)(2,1)S(1)}, bf16[1,40,128,256]{3,2,1,0:T(8,128)(2,1)}, u32[]{:S(2)}) copy-start(bf16[1,40,128,256]{3,2,1,0:T(8,128)(2,1)} %param.21) | copy-start | bytes 7864324
  40.0 53.2 %all-to-all-start.1 = ((bf16[16,45,16,128]{3,2,1,0:T(8,128)(2,1)}), bf16[16,45,16,128]{3,2,1,0:T(8,128)(2,1)S(1)}, u32[]{:S(2)}, u32[]{:S(2)}) async-start(bf16[16,45,16,128]{3,2,1,0:T(8,128)(2,1)} %add_bags.1), calls=%async_computation.1 | async-start | bytes 5898240 | tf_op jit(solution)/shard_map/parts_over_low/all_to_all | solution.py:459
  55.9 48.8 %all-gather.3.cloned.1.call-start = ((), (), s32[]{:S(2)}) async-start(), calls=%async_computation.4 | async-start | bytes 2359296 | tf_op jit(solution)/shard_map/table_gather/all_gather | solution.py:448
  96.3 1.0 copy-start.4
  97.3 44.9 %all-to-all-start.2 = ((bf16[32,128,128]{2,1,0:T(8,128)(2,1)}), bf16[32,128,128]{2,1,0:T(8,128)(2,1)S(1)}, u32[]{:S(2)}, u32[]{:S(2)}) async-start(bf16[32,128,128]{2,1,0:T(8,128)(2,1)} %copy-done.4), calls=%async_computation.2 | async-start | bytes 2097152 | tf_op jit(solution)/shard_map/sums_over_high/all_to_all | solution.py:463
  104.7 1.6 copy-start
  111.1 7.8 %collective-permute-start.1 = (bf16[4,512,256]{2,1,0:T(8,128)(2,1)S(1)}, bf16[4,512,256]{2,1,0:T(8,128)(2,1)S(1)}, u32[]{:S(2)}, u32[]{:S(2)}) collective-permute-start(bf16[4,512,256]{2,1,0:T(8,128)(2,1)S(1)} %pool_parts.3), channel_id=1, source_target_pairs={{0,1},{1,0},{2,3},{3,2},{4,5},{5,4},{6,7},{7,6},{8,9},{9,8},{10,11... | collective-permute-start | bytes 3145736 | tf_op jit(solution)/shard_map/pooling/ppermute | solution.py:437
  118.8 30.1 %copy-start.3 = (bf16[2,512,512]{2,1,0:T(8,128)(2,1)S(1)}, bf16[2,512,512]{2,1,0:T(8,128)(2,1)}, u32[]{:S(2)}) copy-start(bf16[2,512,512]{2,1,0:T(8,128)(2,1)} %refs_5_.1) | copy-start | bytes 3145732
  118.9 30.1 %copy-start.5 = (bf16[1,512,256]{2,1,0:T(8,128)(2,1)S(1)}, bf16[1,512,256]{2,1,0:T(8,128)(2,1)}, u32[]{:S(2)}) copy-start(bf16[1,512,256]{2,1,0:T(8,128)(2,1)} %param.18) | copy-start | bytes 786436
  118.9 30.1 %copy-start.10 = (f32[2,512]{1,0:T(2,128)S(1)}, f32[2,512]{1,0:T(2,128)}, u32[]{:S(2)}) copy-start(f32[2,512]{1,0:T(2,128)} %refs_6_.1) | copy-start | bytes 12292
  119.4 36.7 %copy-start.2 = (f32[512,256]{1,0:T(8,128)S(1)}, f32[512,256]{1,0:T(8,128)}, u32[]{:S(2)}) copy-start(f32[512,256]{1,0:T(8,128)} %table_ref.1) | copy-start | bytes 1572868
  119.4 36.7 %copy-start.11 = (f32[512]{0:T(512)S(1)}, f32[512]{0:T(512)}, u32[]{:S(2)}) copy-start(f32[512]{0:T(512)} %param.13) | copy-start | bytes 6148
  119.4 13.8 %collective-permute-start.2 = (bf16[512,256]{1,0:T(8,128)(2,1)S(1)}, bf16[512,256]{1,0:T(8,128)(2,1)S(1)}, u32[]{:S(2)}, u32[]{:S(2)}) collective-permute-start(bf16[512,256]{1,0:T(8,128)(2,1)S(1)} %get-tuple-element.16), channel_id=1, source_target_pairs={{0,4},{1,5},{2,6},{3,7},{4,0},{5,1},{6,2},{7,3},{8,12},{9,13},{10,... | collective-permute-start | bytes 786440 | tf_op jit(solution)/shard_map/pooling/ppermute | solution.py:437
  124.3 16.5 %collective-permute-start.3 = (bf16[512,256]{1,0:T(8,128)(2,1)S(1)}, bf16[512,256]{1,0:T(8,128)(2,1)S(1)}, u32[]{:S(2)}, u32[]{:S(2)}) collective-permute-start(bf16[512,256]{1,0:T(8,128)(2,1)S(1)} %get-tuple-element.17), channel_id=1, source_target_pairs={{0,6},{1,7},{2,4},{3,5},{4,2},{5,3},{6,0},{7,1},{8,14},{9,15},{10,... | collective-permute-start | bytes 786440 | tf_op jit(solution)/shard_map/pooling/ppermute | solution.py:437
  130.7 10.7 %collective-permute-start.4 = (bf16[512,256]{1,0:T(8,128)(2,1)S(1)}, bf16[512,256]{1,0:T(8,128)(2,1)S(1)}, u32[]{:S(2)}, u32[]{:S(2)}) collective-permute-start(bf16[512,256]{1,0:T(8,128)(2,1)S(1)} %get-tuple-element.18), channel_id=1, source_target_pairs={{0,2},{1,3},{2,0},{3,1},{4,6},{5,7},{6,4},{7,5},{8,10},{9,11},{10,... | collective-permute-start | bytes 786440 | tf_op jit(solution)/shard_map/pooling/ppermute | solution.py:437
  140.8 0.7 copy-start.6
  141.5 0.7 copy-start.8
  143.1 13.1 %all-to-all-start.3 = ((bf16[16,64,128]{2,1,0:T(8,128)(2,1)}), bf16[16,64,128]{2,1,0:T(8,128)(2,1)S(1)}, u32[]{:S(2)}, u32[]{:S(2)}) async-start(bf16[16,64,128]{2,1,0:T(8,128)(2,1)} %add_sources.1), calls=%async_computation.3 | async-start | bytes 524288 | tf_op jit(solution)/shard_map/sums_to_owners/all_to_all | solution.py:474
  149.0 1.0 copy-start.7
  149.9 0.9 copy-start.9
Sparse Core Ops, SparseCore 0:
  59.3 36.7 all-gather.2
